TPU v7x, 128 devices: a whole 4x4x4 slice. The times are simulated.
128 devices in a mesh: frames: 128 (over y, x, z, core).
Axes of the slice: x: 4, y: 4, z: 4, core: 2. Of those that a mesh axis runs over, the one named last changes fastest.
Arguments:
- coords: bfloat16 [3, 131072, 256], P(None, 'frames'), may hold values from -20 to 20, as said below
Outputs:
- band: float32 [131072, 5, 1024], P('frames')
Inputs may be any that keep to these rules, and one draw needn't show every extreme that they name: `coords`: frames are not centred.
All inputs are finite; a program needn't handle non-finite values.
Results may differ from a plain program's by a relative error of at most 0.0035.
Values may be sent and summed in bfloat16 or wider, within the bound.
A program may use at most 320 MiB of HBM per device.

v0:
```python
import jax
import jax.numpy as jnp
from jax import lax
from jax.sharding import PartitionSpec as P

NEWTON = 8
BAND = 2


def passed_along(value, axis, steps):
    count = lax.axis_size(axis)
    pairs = [(source, (source + steps) % count) for source in range(count)]
    return lax.ppermute(value, axis, pairs)


def centre(coords):
    values = coords.astype(jnp.float32)
    shifted = values - jnp.mean(values, axis=2, keepdims=True)
    return shifted.astype(jnp.bfloat16)


def frame_norms(centred):
    return jnp.sum(jnp.square(centred.astype(jnp.float32)), axis=(0, 2))


def deviation_tile(left, right, left_norms, right_norms):
    rows = left.shape[1]
    cols = right.shape[1]
    width = left.shape[2]
    cov = lax.dot_general(
        left.reshape(3 * rows, width),
        right.reshape(3 * cols, width),
        (((1,), (1,)), ((), ())),
        preferred_element_type=jnp.float32,
    )
    cov = cov.reshape(3, rows, 3, cols)
    entry = [[cov[k, :, l, :] for l in range(3)] for k in range(3)]
    squares = entry[0][0] * entry[0][0]
    for k in range(3):
        for l in range(3):
            if k + l > 0:
                squares = squares + entry[k][l] * entry[k][l]
    square_term = -2.0 * squares
    det_three = (
        entry[0][0] * (entry[1][1] * entry[2][2] - entry[1][2] * entry[2][1])
        - entry[0][1] * (entry[1][0] * entry[2][2] - entry[1][2] * entry[2][0])
        + entry[0][2] * (entry[1][0] * entry[2][1] - entry[1][1] * entry[2][0])
    )
    linear_term = -8.0 * det_three
    sxx, sxy, sxz = entry[0]
    syx, syy, syz = entry[1]
    szx, szy, szz = entry[2]
    horn = [
        [sxx + syy + szz, syz - szy, szx - sxz, sxy - syx],
        [syz - szy, sxx - syy - szz, sxy + syx, szx + sxz],
        [szx - sxz, sxy + syx, syy - sxx - szz, syz + szy],
        [sxy - syx, szx + sxz, syz + szy, szz - sxx - syy],
    ]
    pairs = [(0, 1), (0, 2), (0, 3), (1, 2), (1, 3), (2, 3)]
    upper = [horn[0][p] * horn[1][q] - horn[1][p] * horn[0][q] for p, q in pairs]
    lower = [horn[2][p] * horn[3][q] - horn[3][p] * horn[2][q] for p, q in pairs]
    constant_term = (
        upper[0] * lower[5]
        - upper[1] * lower[4]
        + upper[2] * lower[3]
        + upper[3] * lower[2]
        - upper[4] * lower[1]
        + upper[5] * lower[0]
    )
    pair_norms = left_norms[:, None] + right_norms[None, :]
    top = 0.5 * pair_norms
    for step in range(NEWTON):
        square = top * top
        value = ((square + square_term) * top + linear_term) * top + constant_term
        slope = (4.0 * square + 2.0 * square_term) * top + linear_term
        top = top - value / slope
    return (pair_norms - 2.0 * top) / width


def on_device(coords):
    centred = centre(coords)
    norms = frame_norms(centred)
    ahead = []
    current = centred
    for step in range(1, BAND + 1):
        current = passed_along(current, "frames", -1)
        ahead.append(current)
    tiles = {0: deviation_tile(centred, centred, norms, norms)}
    for step in range(1, BAND + 1):
        other = ahead[step - 1]
        tiles[step] = deviation_tile(centred, other, norms, frame_norms(other))
    for step in range(1, BAND + 1):
        tiles[-step] = passed_along(jnp.transpose(tiles[step]), "frames", step)
    return jnp.stack([tiles[offset - BAND] for offset in range(2 * BAND + 1)], axis=1)


def solution(mesh):
    return jax.shard_map(
        on_device,
        mesh=mesh,
        in_specs=(P(None, "frames", None),),
        out_specs=P("frames", None, None),
        check_vma=False,
    )
```

profile of v0, /device:TPU:0, one launch (start us, length us, event | category | flops | bytes accessed | tf_op | source)
XLA Modules:
  0.0 350.6 jit_solution(2779903943902311083)
XLA Ops:
  0.0 1.9 convert_reduce_fusion
  1.9 2.3 multiply_reduce_fusion.2
  4.2 8.3 %collective-permute-start = (bf16[3,1024,256]{2,1,0:T(8,128)(2,1)S(1)}, bf16[3,1024,256]{2,1,0:T(8,128)(2,1)S(1)}, u32[]{:S(2)}, u32[]{:S(2)}) collective-permute-start(bf16[3,1024,256]{2,1,0:T(8,128)(2,1)S(1)} %get-tuple-element.6), channel_id=1, source_target_pairs={{0,127},{1,0},{2,1},{3,2},{4,3},{5,4},{6,5},{7,6},{8,7},{9,8},{10,... | collective-permute-start | bytes 4718600 | tf_op jit(solution)/shard_map/ppermute | solution.py:13
  12.5 17.9 %collective-permute-done = bf16[3,1024,256]{2,1,0:T(8,128)(2,1)S(1)} collective-permute-done((bf16[3,1024,256]{2,1,0:T(8,128)(2,1)S(1)}, bf16[3,1024,256]{2,1,0:T(8,128)(2,1)S(1)}, u32[]{:S(2)}, u32[]{:S(2)}) %collective-permute-start) | collective-permute-done | bytes 1572896 | tf_op jit(solution)/shard_map/ppermute | solution.py:13
  30.4 0.4 multiply_reduce_fusion
  30.8 7.4 %collective-permute-start.1 = (bf16[3,1024,256]{2,1,0:T(8,128)(2,1)S(1)}, bf16[3,1024,256]{2,1,0:T(8,128)(2,1)S(1)}, u32[]{:S(2)}, u32[]{:S(2)}) collective-permute-start(bf16[3,1024,256]{2,1,0:T(8,128)(2,1)S(1)} %collective-permute-done), channel_id=1, source_target_pairs={{0,127},{1,0},{2,1},{3,2},{4,3},{5,4},{6,5},{7,6},{8,7},{9,8},{10,... | collective-permute-start | bytes 4718600 | tf_op jit(solution)/shard_map/ppermute | solution.py:13
  38.2 14.8 %fusion.152 = f32[3,1024,3,1024]{3,1,2,0:T(8,128)} fusion(bf16[3,1024,256]{2,1,0:T(8,128)(2,1)S(1)} %collective-permute-done, bf16[3,1024,256]{2,1,0:T(8,128)(2,1)S(1)} %get-tuple-element.6), kind=kOutput, calls=%fused_computation.296 | convolution fusion | flops 4831838208 | bytes 40894464 | tf_op jit(solution)/shard_map/dot_general | solution.py:30
  53.0 33.0 %fusion.51 = f32[1024,1024]{0,1:T(8,128)S(1)} fusion(f32[3,1024,3,1024]{3,1,2,0:T(8,128)} %fusion.152, f32[1024]{0:T(1024)S(1)} %multiply_reduce_fusion, f32[1024]{0:T(1024)S(1)} %get-tuple-element.5), kind=kLoop, calls=%fused_computation.61 | loop fusion | flops 202375168 | bytes 41951232 | tf_op jit(solution)/shard_map/transpose | solution.py:93
  86.0 0.3 collective-permute-start.3
  86.2 0.0 collective-permute-done.1
  86.2 0.4 multiply_reduce_fusion.1
  86.6 14.9 %fusion.157 = f32[3,1024,3,1024]{3,1,2,0:T(8,128)} fusion(bf16[3,1024,256]{2,1,0:T(8,128)(2,1)S(1)} %get-tuple-element.6, bf16[3,1024,256]{2,1,0:T(8,128)(2,1)S(1)} %collective-permute-done.1), kind=kOutput, calls=%fused_computation.301 | convolution fusion | flops 4831838208 | bytes 40894464 | tf_op jit(solution)/shard_map/dot_general | solution.py:30
  101.5 33.7 %fusion.45 = f32[1024,1024]{0,1:T(8,128)} fusion(f32[3,1024,3,1024]{3,1,2,0:T(8,128)} %fusion.157, f32[1024]{0:T(1024)S(1)} %multiply_reduce_fusion.1, f32[1024]{0:T(1024)S(1)} %get-tuple-element.5), kind=kLoop, calls=%fused_computation.55 | loop fusion | flops 202375168 | bytes 41951232 | tf_op jit(solution)/shard_map/transpose | solution.py:93
  135.2 0.3 collective-permute-start.2
  135.5 14.7 %fusion.154 = f32[3,1024,3,1024]{3,1,2,0:T(8,128)} fusion(bf16[3,1024,256]{2,1,0:T(8,128)(2,1)S(1)} %get-tuple-element.6), kind=kOutput, calls=%fused_computation.298 | convolution fusion | flops 4831838208 | bytes 39321600 | tf_op jit(solution)/shard_map/dot_general | solution.py:30
  150.2 0.0 collective-permute-done.3
  150.2 5.4 %copy.3 = f32[1024,1,1024]{2,0,1:T(8,128)} copy(f32[1024,1,1024]{0,2,1:T(8,128)} %bitcast.26) | data formatting | bytes 8388608 | tf_op jit(solution)/shard_map/stack | solution.py:94
  155.6 78.5 %collective-permute-done.2 = f32[1024,1024]{0,1:T(8,128)} collective-permute-done((f32[1024,1024]{0,1:T(8,128)}, f32[1024,1024]{0,1:T(8,128)}, u32[]{:S(2)}, u32[]{:S(2)}) %collective-permute-start.2) | collective-permute-done | bytes 4194336 | tf_op jit(solution)/shard_map/ppermute | solution.py:13
  234.1 5.3 %copy.2 = f32[1024,1,1024]{2,0,1:T(8,128)} copy(f32[1024,1,1024]{0,2,1:T(8,128)} %bitcast.13) | data formatting | bytes 8388608 | tf_op jit(solution)/shard_map/stack | solution.py:94
  239.4 0.0 copy-start
  239.4 2.7 constant_dynamic-update-slice_fusion.1
  242.1 0.8 copy-done
  242.9 0.3 constant_dynamic-update-slice_fusion
  243.2 33.0 %fusion.57 = f32[1024,5,1024]{2,0,1:T(8,128)S(1)} fusion(f32[1024,5,1024]{2,0,1:T(8,128)S(1)} %constant_dynamic-update-slice_fusion, f32[3,1024,3,1024]{3,1,2,0:T(8,128)} %fusion.154, f32[1024]{0:T(1024)S(1)} %get-tuple-element.5), kind=kLoop, calls=%fused_computation.67 | loop fusion | flops 202375168 | bytes 41951232
  276.2 33.0 %fusion.63 = f32[1024,5,1024]{2,0,1:T(8,128)S(1)} fusion(f32[1024,5,1024]{2,0,1:T(8,128)S(1)} %fusion.57, f32[3,1024,3,1024]{3,1,2,0:T(8,128)} %fusion.152, f32[1024]{0:T(1024)S(1)} %multiply_reduce_fusion, f32[1024]{0:T(1024)S(1)} %get-tuple-element.5), kind=kLoop, calls=%fused_computation.73 | loop fusion | flops 202375168 | bytes 41951232
  309.2 0.0 copy-start.1
  309.2 7.5 %copy-done.1 = f32[1024,5,1024]{2,0,1:T(8,128)} copy-done((f32[1024,5,1024]{2,0,1:T(8,128)}, f32[1024,5,1024]{2,0,1:T(8,128)S(1)}, u32[]{:S(2)}) %copy-start.1) | copy-done | bytes 20971544
  316.8 33.7 %fusion.69 = f32[1024,5,1024]{2,0,1:T(8,128)} fusion(f32[1024,5,1024]{2,0,1:T(8,128)} %copy-done.1, f32[3,1024,3,1024]{3,1,2,0:T(8,128)} %fusion.157, f32[1024]{0:T(1024)S(1)} %multiply_reduce_fusion.1, f32[1024]{0:T(1024)S(1)} %get-tuple-element.5), kind=kLoop, calls=%fused_computation.79 | loop fusion | flops 202375168 | bytes 41951232 | tf_op jit(solution)/shard_map/stack | solution.py:94
  (1 shorter events, 0.0 us)
Async XLA Ops:
  4.2 26.2 %collective-permute-start = (bf16[3,1024,256]{2,1,0:T(8,128)(2,1)S(1)}, bf16[3,1024,256]{2,1,0:T(8,128)(2,1)S(1)}, u32[]{:S(2)}, u32[]{:S(2)}) collective-permute-start(bf16[3,1024,256]{2,1,0:T(8,128)(2,1)S(1)} %get-tuple-element.6), channel_id=1, source_target_pairs={{0,127},{1,0},{2,1},{3,2},{4,3},{5,4},{6,5},{7,6},{8,7},{9,8},{10,... | collective-permute-start | bytes 4718600 | tf_op jit(solution)/shard_map/ppermute | solution.py:13
  30.8 55.5 %collective-permute-start.1 = (bf16[3,1024,256]{2,1,0:T(8,128)(2,1)S(1)}, bf16[3,1024,256]{2,1,0:T(8,128)(2,1)S(1)}, u32[]{:S(2)}, u32[]{:S(2)}) collective-permute-start(bf16[3,1024,256]{2,1,0:T(8,128)(2,1)S(1)} %collective-permute-done), channel_id=1, source_target_pairs={{0,127},{1,0},{2,1},{3,2},{4,3},{5,4},{6,5},{7,6},{8,7},{9,8},{10,... | collective-permute-start | bytes 4718600 | tf_op jit(solution)/shard_map/ppermute | solution.py:13
  86.0 64.2 %collective-permute-start.3 = (f32[1024,1024]{0,1:T(8,128)S(1)}, f32[1024,1024]{0,1:T(8,128)}, u32[]{:S(2)}, u32[]{:S(2)}) collective-permute-start(f32[1024,1024]{0,1:T(8,128)S(1)} %fusion.51), channel_id=1, source_target_pairs={{0,1},{1,2},{2,3},{3,4},{4,5},{5,6},{6,7},{7,8},{8,9},{9,10},{10,1... | collective-permute-start | bytes 12582920 | tf_op jit(solution)/shard_map/ppermute | solution.py:13
  135.2 98.9 %collective-permute-start.2 = (f32[1024,1024]{0,1:T(8,128)}, f32[1024,1024]{0,1:T(8,128)}, u32[]{:S(2)}, u32[]{:S(2)}) collective-permute-start(f32[1024,1024]{0,1:T(8,128)} %fusion.45), channel_id=1, source_target_pairs={{0,2},{1,3},{2,4},{3,5},{4,6},{5,7},{6,8},{7,9},{8,10},{9,11},{10,... | collective-permute-start | bytes 12582920 | tf_op jit(solution)/shard_map/ppermute | solution.py:13
  239.4 3.4 copy-start
  309.2 7.5 %copy-start.1 = (f32[1024,5,1024]{2,0,1:T(8,128)}, f32[1024,5,1024]{2,0,1:T(8,128)S(1)}, u32[]{:S(2)}) copy-start(f32[1024,5,1024]{2,0,1:T(8,128)S(1)} %fusion.63) | copy-start | bytes 62914564
where the time goes:
time: 351 us
  other arithmetic  171 us (49%)
  waiting for transfers between devices  96.4 us (27%)
  matrix products  44.4 us (13%)
  local copies, waits for them, and re-layouts  22 us (6%)
  starting transfers between devices  16.2 us (5%)
    ppermute x4, waiting for transfers between devices, passed_along(): return lax.ppermute(value, axis, pairs)  96.4 us
    transpose x2, other arithmetic, on_device(): tiles[-step] = passed_along(jnp.transpose(tiles[step]), 'frames', step)  66.7 us
    unnamed x2, other arithmetic  66 us
    dot_general x3, matrix products, deviation_tile(): lax.dot_general(left.reshape(3 * rows, width), right.reshape(3 * cols, wi...  44.4 us
    another operation x1, other arithmetic, on_device(): jnp.stack([tiles[offset - BAND] for offset in range(2 * BAND + 1)], axis=1)  33.7 us
    ppermute x4, starting transfers between devices, passed_along(): return lax.ppermute(value, axis, pairs)  16.2 us
    unnamed x6, local copies, waits for them, and re-layouts  11.3 us
    another operation x2, local copies, waits for them, and re-layouts, on_device(): jnp.stack([tiles[offset - BAND] for offset in range(2 * BAND + 1)], axis=1)  10.7 us
  transfers between devices with their start and end apart: 4, of which 2 were waited for; matrix products, arithmetic and copies ran while one was open for 33% of the time, Pallas kernels for 0%

commit v1 on v0

v1 whole, which is shorter than its diff:
```python
import functools

import jax
import jax.numpy as jnp
from jax import lax
from jax.experimental import pallas as pl
from jax.experimental.pallas import tpu as pltpu
from jax.sharding import PartitionSpec as P

NEWTON = 8
FR = 1024
ATOMS = 256
ROWS = 128
COLS = 256
HALF = FR // 2
VMEM = pl.BlockSpec(memory_space=pltpu.VMEM)
ANY = pl.BlockSpec(memory_space=pl.ANY)
PARAMS = pltpu.CompilerParams(vmem_limit_bytes=40 << 20)


def aligned(index, size):
    return pl.ds(pl.multiple_of(index, size), size)


def centre_kernel(x_ref, c_ref, n_ref):
    total = None
    for k in range(3):
        values = x_ref[k].astype(jnp.float32)
        mean = jnp.sum(values, axis=1, keepdims=True) * (1.0 / ATOMS)
        centred = (values - mean).astype(jnp.bfloat16)
        c_ref[k] = centred
        back = centred.astype(jnp.float32)
        square = back * back
        total = square if total is None else total + square
    norms = 0.5 * jnp.sum(total, axis=1, keepdims=True)
    n_ref[...] = jnp.broadcast_to(norms, n_ref.shape)


def centre(coords):
    rows = 256
    return pl.pallas_call(
        centre_kernel,
        grid=(FR // rows,),
        in_specs=[pl.BlockSpec((3, rows, ATOMS), lambda i: (0, i, 0))],
        out_specs=[
            pl.BlockSpec((3, rows, ATOMS), lambda i: (0, i, 0)),
            pl.BlockSpec((rows, 128), lambda i: (i, 0)),
        ],
        out_shape=[
            jax.ShapeDtypeStruct((3, FR, ATOMS), jnp.bfloat16),
            jax.ShapeDtypeStruct((FR, 128), jnp.float32),
        ],
        name="centre",
    )(coords)


def row_norms(b_ref, first, count, rn_ref):
    @pl.loop(0, count // 128)
    def _(i):
        frames = aligned(first + i * 128, 128)
        total = None
        for k in range(3):
            values = b_ref[k, frames, :].astype(jnp.float32)
            total = values * values if total is None else total + values * values
        norms = 0.5 * jnp.sum(total, axis=1, keepdims=True)
        square = jnp.broadcast_to(norms, (128, 128)).T
        rn_ref[:, frames] = square[0:8, :]


def invariants(entry):
    (a, b, c), (d, f, g), (h, i, j) = entry
    first = a * a + b * b + c * c
    others = (d * d + f * f + g * g) + (h * h + i * i + j * j)
    p = f * j - g * i
    q = g * h - d * j
    r = d * i - f * h
    det = a * p + b * q + c * r
    one = a * d + b * f + c * g
    two = a * h + b * i + c * j
    minors = (first * others - one * one - two * two) + (p * p + q * q + r * r)
    return first + others, det + det, minors


def deviations(entry, left, right):
    n, f, m = invariants(entry)
    start = left + right
    top = start
    for _ in range(NEWTON):
        h = top * top - n
        top = ((h * 0.75 + n) * h + m) * pltpu.reciprocal(top * h - f, approx=True)
    return (start - top) * (2.0 / ATOMS)


def covariance(a_ref, b_ref, row, col, cov_ref):
    left = a_ref[:, aligned(row, ROWS), :].reshape(3 * ROWS, ATOMS)
    for k in range(3):
        right = b_ref[k, aligned(col, COLS), :]
        block = lax.dot_general(
            left, right, (((1,), (1,)), ((), ())), preferred_element_type=jnp.float32
        )
        cov_ref[:, k] = block.reshape(3, ROWS, COLS)


def step_values(cov_ref, ln_ref, rn_ref, row, col, emit):
    step = 16
    for r in range(0, ROWS, step):
        entry = [[cov_ref[k, l, r : r + step, :] for l in range(3)] for k in range(3)]
        left = ln_ref[pl.ds(pl.multiple_of(row + r, step), step), :]
        left = jnp.concatenate([left] * (COLS // 128), axis=1)
        right = rn_ref[:, aligned(col, COLS)]
        right = jnp.concatenate([right] * (step // 8), axis=0)
        emit(r, step, deviations(entry, left, right))


def run_steps(total, place, a_ref, b_ref, ln_ref, rn_ref, cov0, cov1, emit, after):
    covariance(a_ref, b_ref, *place(0), cov0)

    @pl.loop(0, total // 2)
    def _(i):
        even, odd = 2 * i, 2 * i + 1
        covariance(a_ref, b_ref, *place(odd), cov1)
        step_values(cov0, ln_ref, rn_ref, *place(even), functools.partial(emit, even))
        after(even)
        covariance(a_ref, b_ref, *place(jnp.minimum(odd + 1, total - 1)), cov0)
        step_values(cov1, ln_ref, rn_ref, *place(odd), functools.partial(emit, odd))
        after(odd)


def encode(values):
    square = values * values
    return (square * square).astype(jnp.bfloat16)


def diagonal_kernel(a_ref, ln_ref, out_ref, tile, rn, cov0, cov1, sem):
    row_norms(a_ref, 0, FR, rn)
    per = COLS // ROWS

    def place(s):
        col = 0
        for c in range(1, FR // COLS):
            col = col + jnp.where(s >= per * c * (c + 1) // 2, 1, 0)
        row = s - per * col * (col + 1) // 2
        return row * ROWS, col * COLS

    def emit(s, r, step, values):
        row, col = place(s)
        tile[pl.ds(pl.multiple_of(row + r, step), step), aligned(col, COLS)] = values

    def after(s):
        row, col = place(s)
        rows, cols = aligned(row, ROWS), aligned(col, COLS)

        @pl.when(row < col)
        def _():
            tile[cols, rows] = tile[rows, cols].T

    total = per * (FR // COLS) * (FR // COLS + 1) // 2
    run_steps(total, place, a_ref, a_ref, ln_ref, rn, cov0, cov1, emit, after)
    copy = pltpu.make_async_copy(tile, out_ref.at[2], sem)
    copy.start()
    copy.wait()


def diagonal(centred, norms):
    return pl.pallas_call(
        diagonal_kernel,
        in_specs=[VMEM, VMEM],
        out_specs=ANY,
        out_shape=jax.ShapeDtypeStruct((5, FR, FR), jnp.float32),
        scratch_shapes=[
            pltpu.VMEM((FR, FR), jnp.float32),
            pltpu.VMEM((8, FR), jnp.float32),
            pltpu.VMEM((3, 3, ROWS, COLS), jnp.float32),
            pltpu.VMEM((3, 3, ROWS, COLS), jnp.float32),
            pltpu.SemaphoreType.DMA,
        ],
        compiler_params=PARAMS,
        cost_estimate=pl.CostEstimate(
            flops=9 * FR * FR * ATOMS, bytes_accessed=6 << 20, transcendentals=0
        ),
        name="diagonal",
    )(centred, norms)


def far_kernel(first, count, a_ref, b_ref, ln_ref, _, out_ref, y_ref, tile, rn, cov0, cov1, sem):
    parity = lax.rem(lax.axis_index("frames"), 2)
    slot = 4 * (1 - parity)
    row_norms(b_ref, first, count, rn)
    per = FR // ROWS

    def place(s):
        return (s % per) * ROWS, first + (s // per) * COLS

    def emit(s, r, step, values):
        row, col = place(s)
        tile[pl.ds(pl.multiple_of(row + r, step), step), aligned(col - first, COLS)] = values

    def after(s):
        row, col = place(s)
        rows, cols = aligned(row, ROWS), aligned(col - first, COLS)
        y_ref[cols, rows] = encode(tile[rows, cols]).T
        pltpu.make_async_copy(
            tile.at[rows, cols], out_ref.at[slot, rows, aligned(col, COLS)], sem
        ).start()

    total = per * (count // COLS)
    run_steps(total, place, a_ref, b_ref, ln_ref, rn, cov0, cov1, emit, after)
    pltpu.make_async_copy(tile, out_ref.at[slot, :, pl.ds(first, count)], sem).wait()


def far_part(centred, other, norms, out, first, count):
    return pl.pallas_call(
        functools.partial(far_kernel, first, count),
        in_specs=[VMEM, VMEM, VMEM, ANY],
        out_specs=[ANY, VMEM],
        out_shape=[
            jax.ShapeDtypeStruct((5, FR, FR), jnp.float32),
            jax.ShapeDtypeStruct((count, FR), jnp.bfloat16),
        ],
        input_output_aliases={3: 0},
        scratch_shapes=[
            pltpu.VMEM((FR, count), jnp.float32),
            pltpu.VMEM((8, FR), jnp.float32),
            pltpu.VMEM((3, 3, ROWS, COLS), jnp.float32),
            pltpu.VMEM((3, 3, ROWS, COLS), jnp.float32),
            pltpu.SemaphoreType.DMA,
        ],
        compiler_params=PARAMS,
        cost_estimate=pl.CostEstimate(
            flops=18 * FR * count * ATOMS, bytes_accessed=6 << 20, transcendentals=0
        ),
        name="far",
    )(centred, other, norms, out)


def quarters_kernel(mate, a_ref, b_ref, ln_ref, _, out_ref, y_ref, tile, rn, cov0, cov1, sem):
    parity = lax.rem(lax.axis_index("frames"), 2)
    if mate:
        slot, flip = 3 - 2 * parity, parity
    else:
        slot, flip = 1 + 2 * parity, 1 - parity
    row_norms(b_ref, 0, FR, rn)
    per_row, per_col = HALF // ROWS, HALF // COLS
    per = per_row * per_col

    def place(s):
        half = s // per
        other = half + flip - 2 * half * flip
        inner = s % per
        row = half * HALF + (inner % per_row) * ROWS
        return row, other * HALF + (inner // per_row) * COLS

    def local(s):
        half, inner = s // per, s % per
        return half, (inner % per_row) * ROWS, (inner // per_row) * COLS

    def emit(s, r, step, values):
        half, row, col = local(s)
        tile[half, pl.ds(pl.multiple_of(row + r, step), step), aligned(col, COLS)] = values

    def after(s):
        half, row, col = local(s)
        rows, cols = aligned(row, ROWS), aligned(col, COLS)
        y_ref[half, cols, rows] = encode(tile[half, rows, cols]).T
        row, col = place(s)
        pltpu.make_async_copy(
            tile.at[half, rows, cols],
            out_ref.at[slot, aligned(row, ROWS), aligned(col, COLS)],
            sem,
        ).start()

    run_steps(2 * per, place, a_ref, b_ref, ln_ref, rn, cov0, cov1, emit, after)
    for half in range(2):
        pltpu.make_async_copy(
            tile.at[half], out_ref.at[slot, pl.ds(0, HALF), pl.ds(0, HALF)], sem
        ).wait()


def quarters(centred, other, norms, out, mate):
    return pl.pallas_call(
        functools.partial(quarters_kernel, mate),
        in_specs=[VMEM, VMEM, VMEM, ANY],
        out_specs=[ANY, VMEM],
        out_shape=[
            jax.ShapeDtypeStruct((5, FR, FR), jnp.float32),
            jax.ShapeDtypeStruct((2, HALF, HALF), jnp.bfloat16),
        ],
        input_output_aliases={3: 0},
        scratch_shapes=[
            pltpu.VMEM((2, HALF, HALF), jnp.float32),
            pltpu.VMEM((8, FR), jnp.float32),
            pltpu.VMEM((3, 3, ROWS, COLS), jnp.float32),
            pltpu.VMEM((3, 3, ROWS, COLS), jnp.float32),
            pltpu.SemaphoreType.DMA,
        ],
        compiler_params=PARAMS,
        cost_estimate=pl.CostEstimate(
            flops=9 * FR * FR * ATOMS, bytes_accessed=6 << 20, transcendentals=0
        ),
        name="mate" if mate else "near",
    )(centred, other, norms, out)


def decode(values):
    return lax.rsqrt(lax.rsqrt(values.astype(jnp.float32)))


def received_kernel(far0, far1, near, mate, _, out_ref, far_tile, near_tile, mate_tile, sem):
    parity = lax.rem(lax.axis_index("frames"), 2)
    copies = []
    for i, (ref, rows) in enumerate(((far0, pl.ds(0, HALF)), (far1, pl.ds(HALF, HALF)))):
        far_tile[rows, :] = decode(ref[...])
        copies.append(pltpu.make_async_copy(
            far_tile.at[rows], out_ref.at[4 * parity, rows], sem.at[i]
        ))
        copies[-1].start()
    for i, (ref, tile, slot, flip) in enumerate(
        ((near, near_tile, 1 + 2 * parity, parity), (mate, mate_tile, 3 - 2 * parity, 1 - parity))
    ):
        for half in range(2):
            tile[half] = decode(ref[half])
            own = half + flip - 2 * half * flip
            copies.append(pltpu.make_async_copy(
                tile.at[half],
                out_ref.at[slot, aligned(own * HALF, HALF), pl.ds(half * HALF, HALF)],
                sem.at[2 + 2 * i + half],
            ))
            copies[-1].start()
    for copy in copies:
        copy.wait()


def received(far0, far1, near, mate, out):
    return pl.pallas_call(
        received_kernel,
        in_specs=[VMEM, VMEM, VMEM, VMEM, ANY],
        out_specs=ANY,
        out_shape=jax.ShapeDtypeStruct((5, FR, FR), jnp.float32),
        input_output_aliases={4: 0},
        scratch_shapes=[
            pltpu.VMEM((FR, FR), jnp.float32),
            pltpu.VMEM((2, HALF, HALF), jnp.float32),
            pltpu.VMEM((2, HALF, HALF), jnp.float32),
            pltpu.SemaphoreType.DMA((6,)),
        ],
        compiler_params=PARAMS,
        name="received",
    )(far0, far1, near, mate, out)


def on_device(coords):
    count = lax.axis_size("frames")
    reach = [2 if s % 2 == 0 else -2 for s in range(count)]
    fetch_far = [((s + reach[s]) % count, s) for s in range(count)]
    send_far = [(s, (s + reach[s]) % count) for s in range(count)]
    send_near = [(s, (s - 1 if s % 2 == 0 else s + 1) % count) for s in range(count)]
    swap = [(s, s ^ 1) for s in range(count)]
    move = functools.partial(lax.ppermute, axis_name="frames")

    centred, norms = centre(coords)
    far = move(centred, perm=fetch_far)
    mate = move(centred, perm=swap)
    out = diagonal(centred, norms)
    far, out = lax.optimization_barrier((far, out))
    near = move(far, perm=swap)
    out, far0 = far_part(centred, far, norms, out, 0, HALF)
    far0 = move(far0, perm=send_far)
    out, far1 = far_part(centred, far, norms, out, HALF, HALF)
    far1 = move(far1, perm=send_far)
    out, near_y = quarters(centred, near, norms, out, False)
    near_y = move(near_y, perm=send_near)
    out, mate_y = quarters(centred, mate, norms, out, True)
    mate_y = move(mate_y, perm=swap)
    out = received(far0, far1, near_y, mate_y, out)
    return jnp.transpose(out, (1, 0, 2))


def solution(mesh):
    return jax.shard_map(
        on_device,
        mesh=mesh,
        in_specs=(P(None, "frames", None),),
        out_specs=P("frames", None, None),
        check_vma=False,
    )
```

time: 351 us -> 104 us (0.30)
  other arithmetic: 171 us -> 0 us
  waiting for transfers between devices: 96.4 us -> 2.54 us
  Pallas kernels: 0 us -> 85.3 us
  matrix products: 44.4 us -> 0 us
  local copies, waits for them, and re-layouts: 22 us -> 2.48 us
    ppermute x4 -> x7, waiting for transfers between devices: 96.4 us -> 2.54 us  [the longest x1 1.86 us: on_device(): near_y = move(near_y, perm=send_near)]
    pallas_call x0 -> x7, Pallas kernels: none -> 85.3 us  [the longest x2 29.2 us: quarters(): pl.pallas_call(functools.partial(quarters_kernel, mate), in_specs=[VMEM,...]
    transpose x2 -> x0, other arithmetic: 66.7 us -> none  [on_device(): tiles[-step] = passed_along(jnp.transpose(tiles[step]), 'frames', step)]
    unnamed x2 -> x0, other arithmetic: 66 us -> none
    dot_general x3 -> x0, matrix products: 44.4 us -> none  [deviation_tile(): lax.dot_general(left.reshape(3 * rows, width), right.reshape(3 * cols, wi...]
    another operation x1 -> x0, other arithmetic: 33.7 us -> none  [on_device(): jnp.stack([tiles[offset - BAND] for offset in range(2 * BAND + 1)], axis=1)]
    another operation x2 -> x0, local copies, waits for them, and re-layouts: 10.7 us -> none  [on_device(): jnp.stack([tiles[offset - BAND] for offset in range(2 * BAND + 1)], axis=1)]
    unnamed x6 -> x4, local copies, waits for them, and re-layouts: 11.3 us -> 2.48 us
  transfers between devices with their start and end apart: 4 -> 7, of which waited for: 2 -> 2; matrix products, arithmetic and copies ran while one was open for 33% -> 0% of each run, Pallas kernels for 0% -> 75%
where the time goes in v1:
time: 104 us; the launch traced here: 103 us
  Pallas kernels  85.3 us (82%)
  starting transfers between devices  12.8 us (12%)
  waiting for transfers between devices  2.54 us (2%)
  local copies, waits for them, and re-layouts  2.48 us (2%)
    pallas_call x2, Pallas kernels, quarters(): pl.pallas_call(functools.partial(quarters_kernel, mate), in_specs=[VMEM,...  29.2 us
    pallas_call x2, Pallas kernels, far_part(): pl.pallas_call(functools.partial(far_kernel, first, count), in_specs=[VME...  27.9 us
    pallas_call x1, Pallas kernels, diagonal(): pl.pallas_call(diagonal_kernel, in_specs=[VMEM, VMEM], out_specs=ANY, out...  20.1 us
    ppermute x1, starting transfers between devices, on_device(): far = move(centred, perm=fetch_far)  8.77 us
    pallas_call x1, Pallas kernels, centre(): pl.pallas_call(centre_kernel, grid=(FR // rows,), in_specs=[pl.BlockSpec(...  4.24 us
    pallas_call x1, Pallas kernels, received(): pl.pallas_call(received_kernel, in_specs=[VMEM, VMEM, VMEM, VMEM, ANY], o...  3.9 us
    ppermute x1, starting transfers between devices, on_device(): near_y = move(near_y, perm=send_near)  3.07 us
    unnamed x4, local copies, waits for them, and re-layouts  2.48 us
  transfers between devices with their start and end apart: 7, of which 2 were waited for; matrix products, arithmetic and copies ran while one was open for 0% of the time, Pallas kernels for 75%

profile of v1, /device:TPU:0, one launch (start us, length us, event | category | flops | bytes accessed | tf_op | source)
XLA Modules:
  0.0 103.2 jit_solution(4849444717116179191)
XLA Ops:
  0.0 4.2 %centre.1 = (bf16[3,1024,256]{2,1,0:T(8,128)(2,1)}, f32[1024,128]{1,0:T(8,128)}) custom-call(bf16[3,1024,256]{2,1,0:T(8,128)(2,1)} %x_ref.1), custom_call_target="tpu_custom_call" | custom-call | tf_op jit(solution)/shard_map/centre/pallas_call | solution.py:41
  4.2 8.8 %collective-permute-start = (bf16[3,1024,256]{2,1,0:T(8,128)(2,1)}, bf16[3,1024,256]{2,1,0:T(8,128)(2,1)S(1)}, u32[]{:S(2)}, u32[]{:S(2)}) collective-permute-start(bf16[3,1024,256]{2,1,0:T(8,128)(2,1)} %get-tuple-element.17.a_ref), channel_id=1, source_target_pairs={{2,0},{127,1},{4,2},{1,3},{6,4},{3,5},{8,6},{5,7},{10,8},{7,9},{12... | collective-permute-start | bytes 4718600 | tf_op jit(solution)/shard_map/ppermute | solution.py:361
  13.0 0.0 copy-start
  13.0 1.4 %copy-done = bf16[3,1024,256]{2,1,0:T(8,128)(2,1)S(1)} copy-done((bf16[3,1024,256]{2,1,0:T(8,128)(2,1)S(1)}, bf16[3,1024,256]{2,1,0:T(8,128)(2,1)}, u32[]{:S(2)}) %copy-start) | copy-done | bytes 1572888
  14.4 0.0 copy-start.1
  14.5 1.0 %copy-done.1 = f32[1024,128]{1,0:T(8,128)S(1)} copy-done((f32[1024,128]{1,0:T(8,128)S(1)}, f32[1024,128]{1,0:T(8,128)}, u32[]{:S(2)}) %copy-start.1) | copy-done | bytes 524312
  15.5 20.1 %diagonal.1._ = f32[5,1024,1024]{2,1,0:T(8,128)} custom-call(bf16[3,1024,256]{2,1,0:T(8,128)(2,1)S(1)} %copy-done, f32[1024,128]{1,0:T(8,128)S(1)} %copy-done.1), custom_call_target="tpu_custom_call" | custom-call | flops 2415919104 | bytes 6291456 | tf_op jit(solution)/shard_map/diagonal/pallas_call | solution.py:165
  35.6 0.0 collective-permute-done.b_ref
  35.6 0.1 collective-permute-start.3
  35.7 0.5 collective-permute-start.5
  36.2 13.9 %far.2 = (f32[5,1024,1024]{2,1,0:T(8,128)}, bf16[512,1024]{1,0:T(8,128)(2,1)S(1)}) custom-call(bf16[3,1024,256]{2,1,0:T(8,128)(2,1)S(1)} %copy-done, bf16[3,1024,256]{2,1,0:T(8,128)(2,1)S(1)} %collective-permute-done.b_ref, f32[1024,128]{1,0:T(8,128)S(1)} %copy-done.1, f32[5,1024,1024]{2,1,0:T(8,128)} %diagonal.1._), custom_call_target="tpu_custom_call", output_to_operand_aliasing={{0}: (3, {})} | custom-call | flops 2415919104 | bytes 6291456 | tf_op jit(solution)/shard_map/far/pallas_call | solution.py:212
  50.1 0.1 collective-permute-start.1
  50.2 14.0 %far.3 = (f32[5,1024,1024]{2,1,0:T(8,128)}, bf16[512,1024]{1,0:T(8,128)(2,1)S(1)}) custom-call(bf16[3,1024,256]{2,1,0:T(8,128)(2,1)S(1)} %copy-done, bf16[3,1024,256]{2,1,0:T(8,128)(2,1)S(1)} %collective-permute-done.b_ref, f32[1024,128]{1,0:T(8,128)S(1)} %copy-done.1, f32[5,1024,1024]{2,1,0:T(8,128)} %get-tuple-element.22._), custom_call_target="tpu_custom_call", output_to_operand_aliasing={{0}: (3, {})} | custom-call | flops 2415919104 | bytes 6291456 | tf_op jit(solution)/shard_map/far/pallas_call | solution.py:212
  64.2 0.1 collective-permute-start.2
  64.3 0.0 collective-permute-done.3.b_ref
  64.3 14.6 %near.1 = (f32[5,1024,1024]{2,1,0:T(8,128)}, bf16[2,512,512]{2,1,0:T(8,128)(2,1)S(1)}) custom-call(bf16[3,1024,256]{2,1,0:T(8,128)(2,1)S(1)} %copy-done, bf16[3,1024,256]{2,1,0:T(8,128)(2,1)S(1)} %collective-permute-done.3.b_ref, f32[1024,128]{1,0:T(8,128)S(1)} %copy-done.1, f32[5,1024,1024]{2,1,0:T(8,128)} %get-tuple-element.24._), custom_call_target="tpu_custom_call", output_to_operand_aliasing={{0}: (3, {})} | custom-call | flops 2415919104 | bytes 6291456 | tf_op jit(solution)/shard_map/near/pallas_call | solution.py:280
  78.9 3.1 %collective-permute-start.4 = (bf16[2,512,512]{2,1,0:T(8,128)(2,1)S(1)}, bf16[2,512,512]{2,1,0:T(8,128)(2,1)S(1)}, u32[]{:S(2)}, u32[]{:S(2)}) collective-permute-start(bf16[2,512,512]{2,1,0:T(8,128)(2,1)S(1)} %get-tuple-element.25), channel_id=1, source_target_pairs={{0,127},{1,2},{2,1},{3,4},{4,3},{5,6},{6,5},{7,8},{8,7},{9,10},{10... | collective-permute-start | bytes 3145736 | tf_op jit(solution)/shard_map/ppermute | solution.py:371
  81.9 0.0 collective-permute-done.5.b_ref
  82.0 14.6 %mate.1 = (f32[5,1024,1024]{2,1,0:T(8,128)}, bf16[2,512,512]{2,1,0:T(8,128)(2,1)S(1)}) custom-call(bf16[3,1024,256]{2,1,0:T(8,128)(2,1)S(1)} %copy-done, bf16[3,1024,256]{2,1,0:T(8,128)(2,1)S(1)} %collective-permute-done.5.b_ref, f32[1024,128]{1,0:T(8,128)S(1)} %copy-done.1, f32[5,1024,1024]{2,1,0:T(8,128)} %get-tuple-element.26._), custom_call_target="tpu_custom_call", output_to_operand_aliasing={{0}: (3, {})} | custom-call | flops 2415919104 | bytes 6291456 | tf_op jit(solution)/shard_map/mate/pallas_call | solution.py:280
  96.5 0.2 collective-permute-start.6
  96.7 0.0 collective-permute-done.1.far0
  96.8 0.0 collective-permute-done.2.far1
  96.8 1.9 %collective-permute-done.4.near = bf16[2,512,512]{2,1,0:T(8,128)(2,1)S(1)} collective-permute-done((bf16[2,512,512]{2,1,0:T(8,128)(2,1)S(1)}, bf16[2,512,512]{2,1,0:T(8,128)(2,1)S(1)}, u32[]{:S(2)}, u32[]{:S(2)}) %collective-permute-start.4) | collective-permute-done | bytes 1048608 | tf_op jit(solution)/shard_map/ppermute | solution.py:371
  98.6 0.7 collective-permute-done.6.mate
  99.3 3.9 %received.1 = f32[5,1024,1024]{2,1,0:T(8,128)} custom-call(bf16[512,1024]{1,0:T(8,128)(2,1)S(1)} %collective-permute-done.1.far0, bf16[512,1024]{1,0:T(8,128)(2,1)S(1)} %collective-permute-done.2.far1, bf16[2,512,512]{2,1,0:T(8,128)(2,1)S(1)} %collective-permute-done.4.near, ...), custom_call_target="tpu_custom_call", output_to_operand_aliasing={{}: (4, {})} | custom-call | tf_op jit(solution)/shard_map/received/pallas_call | solution.py:334
Async XLA Ops:
  4.2 31.3 %collective-permute-start = (bf16[3,1024,256]{2,1,0:T(8,128)(2,1)}, bf16[3,1024,256]{2,1,0:T(8,128)(2,1)S(1)}, u32[]{:S(2)}, u32[]{:S(2)}) collective-permute-start(bf16[3,1024,256]{2,1,0:T(8,128)(2,1)} %get-tuple-element.17.a_ref), channel_id=1, source_target_pairs={{2,0},{127,1},{4,2},{1,3},{6,4},{3,5},{8,6},{5,7},{10,8},{7,9},{12... | collective-permute-start | bytes 4718600 | tf_op jit(solution)/shard_map/ppermute | solution.py:361
  13.0 1.4 %copy-start = (bf16[3,1024,256]{2,1,0:T(8,128)(2,1)S(1)}, bf16[3,1024,256]{2,1,0:T(8,128)(2,1)}, u32[]{:S(2)}) copy-start(bf16[3,1024,256]{2,1,0:T(8,128)(2,1)} %get-tuple-element.17.a_ref) | copy-start | bytes 4718596
  14.4 1.0 %copy-start.1 = (f32[1024,128]{1,0:T(8,128)S(1)}, f32[1024,128]{1,0:T(8,128)}, u32[]{:S(2)}) copy-start(f32[1024,128]{1,0:T(8,128)} %get-tuple-element.18.ln_ref) | copy-start | bytes 1572868
  35.6 28.7 %collective-permute-start.3 = (bf16[3,1024,256]{2,1,0:T(8,128)(2,1)S(1)}, bf16[3,1024,256]{2,1,0:T(8,128)(2,1)S(1)}, u32[]{:S(2)}, u32[]{:S(2)}) collective-permute-start(bf16[3,1024,256]{2,1,0:T(8,128)(2,1)S(1)} %collective-permute-done.b_ref), channel_id=1, source_target_pairs={{0,1},{1,0},{2,3},{3,2},{4,5},{5,4},{6,7},{7,6},{8,9},{9,8},{10,11... | collective-permute-start | bytes 4718600 | tf_op jit(solution)/shard_map/ppermute | solution.py:365
  35.7 46.3 %collective-permute-start.5 = (bf16[3,1024,256]{2,1,0:T(8,128)(2,1)S(1)}, bf16[3,1024,256]{2,1,0:T(8,128)(2,1)S(1)}, u32[]{:S(2)}, u32[]{:S(2)}) collective-permute-start(bf16[3,1024,256]{2,1,0:T(8,128)(2,1)S(1)} %copy-done), channel_id=1, source_target_pairs={{0,1},{1,0},{2,3},{3,2},{4,5},{5,4},{6,7},{7,6},{8,9},{9,8},{10,11... | collective-permute-start | bytes 4718600 | tf_op jit(solution)/shard_map/ppermute | solution.py:362
  50.1 46.6 %collective-permute-start.1 = (bf16[512,1024]{1,0:T(8,128)(2,1)S(1)}, bf16[512,1024]{1,0:T(8,128)(2,1)S(1)}, u32[]{:S(2)}, u32[]{:S(2)}) collective-permute-start(bf16[512,1024]{1,0:T(8,128)(2,1)S(1)} %get-tuple-element.21), channel_id=1, source_target_pairs={{0,2},{1,127},{2,4},{3,1},{4,6},{5,3},{6,8},{7,5},{8,10},{9,7},{10... | collective-permute-start | bytes 3145736 | tf_op jit(solution)/shard_map/ppermute | solution.py:367
  64.2 32.6 %collective-permute-start.2 = (bf16[512,1024]{1,0:T(8,128)(2,1)S(1)}, bf16[512,1024]{1,0:T(8,128)(2,1)S(1)}, u32[]{:S(2)}, u32[]{:S(2)}) collective-permute-start(bf16[512,1024]{1,0:T(8,128)(2,1)S(1)} %get-tuple-element.23), channel_id=1, source_target_pairs={{0,2},{1,127},{2,4},{3,1},{4,6},{5,3},{6,8},{7,5},{8,10},{9,7},{10... | collective-permute-start | bytes 3145736 | tf_op jit(solution)/shard_map/ppermute | solution.py:369
  78.9 19.7 %collective-permute-start.4 = (bf16[2,512,512]{2,1,0:T(8,128)(2,1)S(1)}, bf16[2,512,512]{2,1,0:T(8,128)(2,1)S(1)}, u32[]{:S(2)}, u32[]{:S(2)}) collective-permute-start(bf16[2,512,512]{2,1,0:T(8,128)(2,1)S(1)} %get-tuple-element.25), channel_id=1, source_target_pairs={{0,127},{1,2},{2,1},{3,4},{4,3},{5,6},{6,5},{7,8},{8,7},{9,10},{10... | collective-permute-start | bytes 3145736 | tf_op jit(solution)/shard_map/ppermute | solution.py:371
  96.5 2.7 %collective-permute-start.6 = (bf16[2,512,512]{2,1,0:T(8,128)(2,1)S(1)}, bf16[2,512,512]{2,1,0:T(8,128)(2,1)S(1)}, u32[]{:S(2)}, u32[]{:S(2)}) collective-permute-start(bf16[2,512,512]{2,1,0:T(8,128)(2,1)S(1)} %get-tuple-element.27), channel_id=1, source_target_pairs={{0,1},{1,0},{2,3},{3,2},{4,5},{5,4},{6,7},{7,6},{8,9},{9,8},{10,11... | collective-permute-start | bytes 3145736 | tf_op jit(solution)/shard_map/ppermute | solution.py:373

commit v2 on v1

v2 whole, which is shorter than its diff:
```python
import functools

import jax
import jax.numpy as jnp
from jax import lax
from jax.experimental import pallas as pl
from jax.experimental.pallas import tpu as pltpu
from jax.sharding import PartitionSpec as P

NEWTON = 8
FR = 1024
ATOMS = 256
ROWS = 128
COLS = 256
STEP = 16
HALF = FR // 2
VMEM = pl.BlockSpec(memory_space=pltpu.VMEM)
ANY = pl.BlockSpec(memory_space=pl.ANY)
PARAMS = pltpu.CompilerParams(vmem_limit_bytes=32 << 20)


def aligned(index, size):
    return pl.ds(pl.multiple_of(index, size), size)


def centre_kernel(x_ref, c_ref, low_ref, high_ref, n_ref):
    for part, ref in enumerate((low_ref, high_ref)):

        @pl.loop(0, HALF // ROWS)
        def _(i):
            inner = aligned(i * ROWS, ROWS)
            rows = aligned(part * HALF + i * ROWS, ROWS)
            total = None
            for k in range(3):
                values = x_ref[k, rows, :].astype(jnp.float32)
                mean = jnp.sum(values, axis=1, keepdims=True) * (1.0 / ATOMS)
                centred = (values - mean).astype(jnp.bfloat16)
                c_ref[k, rows, :] = centred
                ref[k, inner, :] = centred
                back = centred.astype(jnp.float32)
                square = back * back
                total = square if total is None else total + square
            norms = 0.5 * jnp.sum(total, axis=1, keepdims=True)
            n_ref[rows, :] = jnp.broadcast_to(norms, (ROWS, 128))


def centre(coords):
    return pl.pallas_call(
        centre_kernel,
        in_specs=[VMEM],
        out_specs=[VMEM] * 4,
        out_shape=[
            jax.ShapeDtypeStruct((3, FR, ATOMS), jnp.bfloat16),
            jax.ShapeDtypeStruct((3, HALF, ATOMS), jnp.bfloat16),
            jax.ShapeDtypeStruct((3, HALF, ATOMS), jnp.bfloat16),
            jax.ShapeDtypeStruct((FR, 128), jnp.float32),
        ],
        compiler_params=pltpu.CompilerParams(vmem_limit_bytes=16 << 20),
        name="centre",
    )(coords)


def row_norms(b_ref, rn_ref):
    @pl.loop(0, b_ref.shape[1] // 128)
    def _(i):
        frames = aligned(i * 128, 128)
        total = None
        for k in range(3):
            values = b_ref[k, frames, :].astype(jnp.float32)
            total = values * values if total is None else total + values * values
        norms = 0.5 * jnp.sum(total, axis=1, keepdims=True)
        square = jnp.broadcast_to(norms, (128, 128)).T
        rn_ref[:, frames] = square[0:8, :]


def invariants(entry):
    (a, b, c), (d, f, g), (h, i, j) = entry
    first = a * a + b * b + c * c
    others = (d * d + f * f + g * g) + (h * h + i * i + j * j)
    p = f * j - g * i
    q = g * h - d * j
    r = d * i - f * h
    det = a * p + b * q + c * r
    one = a * d + b * f + c * g
    two = a * h + b * i + c * j
    minors = (first * others - one * one - two * two) + (p * p + q * q + r * r)
    return first + others, det + det, minors


def deviations(entry, left, right):
    n, f, m = invariants(entry)
    start = left + right
    top = start
    for _ in range(NEWTON):
        h = top * top - n
        top = ((h * 0.75 + n) * h + m) * pltpu.reciprocal(top * h - f, approx=True)
    return (start - top) * (2.0 / ATOMS)


def covariance_pieces(a_ref, b_ref, row, col, cov_ref):
    left = a_ref[:, aligned(row, ROWS), :].reshape(3 * ROWS, ATOMS)
    for k in range(3):
        right = b_ref[k, aligned(col, COLS), :]
        block = lax.dot_general(
            left, right, (((1,), (1,)), ((), ())), preferred_element_type=jnp.float32
        )
        cov_ref[:, k] = block.reshape(3, ROWS, COLS)
        yield


def value_pieces(cov_ref, ln_ref, rn_ref, row, col, emit):
    for r in range(0, ROWS, STEP):
        entry = [[cov_ref[k, l, r : r + STEP, :] for l in range(3)] for k in range(3)]
        left = ln_ref[aligned(row + r, STEP), :]
        left = jnp.concatenate([left] * (COLS // 128), axis=1)
        right = rn_ref[:, aligned(col, COLS)]
        right = jnp.concatenate([right] * (STEP // 8), axis=0)
        emit(r, deviations(entry, left, right))
        yield


def run_steps(total, place, a_ref, b_ref, ln_ref, rn_ref, cov0, cov1, old0, old1, keep, turn, before):
    for _ in covariance_pieces(a_ref, b_ref, *place(0), cov0):
        pass

    def step(s, cov, cov_next, old, old_last):
        row, col = place(jnp.minimum(s + 1, total - 1))
        products = covariance_pieces(a_ref, b_ref, row, col, cov_next)
        row, col = place(s)
        values = value_pieces(cov, ln_ref, rn_ref, row, col, functools.partial(keep, s, old))
        for count, _ in enumerate(values):
            if count in (0, 2, 4):
                next(products)
        turn(jnp.maximum(s - 1, 0), old_last)

    @pl.loop(0, total)
    def _(s):
        before(s)

        @pl.when((s & 1) == 0)
        def _():
            step(s, cov0, cov1, old0, old1)

        @pl.when((s & 1) == 1)
        def _():
            step(s, cov1, cov0, old1, old0)

    turn(total - 1, old1 if total % 2 == 0 else old0)
    before(total)
    before(total + 1)


def encode(values):
    square = values * values
    return (square * square).astype(jnp.bfloat16)


def step_scratch(kind):
    return [
        pltpu.VMEM((3, 3, ROWS, COLS), jnp.float32),
        pltpu.VMEM((3, 3, ROWS, COLS), jnp.float32),
        pltpu.VMEM((ROWS, COLS), kind),
        pltpu.VMEM((ROWS, COLS), kind),
    ]


def diagonal_kernel(first, last, a_ref, ln_ref, *refs):
    out_ref, tile, mirror, rn, cov0, cov1, old0, old1, sem = refs[-9:]
    row_norms(a_ref, rn)
    per = COLS // ROWS
    starts = [per * c * (c + 1) // 2 for c in range(FR // COLS + 1)]

    def place(s):
        s = s + starts[first]
        col = sum(jnp.where(s >= start, 1, 0) for start in starts[1:last])
        row = s - per * (col * (col + 1) // 2)
        return row * ROWS, col * COLS

    def keep(s, old, r, values):
        row, col = place(s)
        tile[aligned(row + r, STEP), aligned(col, COLS)] = values
        old[r : r + STEP, :] = values

    def turn(s, old):
        row, col = place(s)
        mirror[aligned(col, COLS), aligned(row, ROWS)] = old[...].T

    def copies(c):
        cols = pl.ds(c * COLS, COLS)
        yield tile, pl.ds(0, (c + 1) * COLS), cols
        if c > 0:
            yield mirror, cols, pl.ds(0, c * COLS)

    def each_copy(c, act):
        for source, rows, cols in copies(c):
            act(pltpu.make_async_copy(source.at[rows, cols], out_ref.at[2, rows, cols], sem.at[c]))

    def before(s):
        for c in range(first, last):
            if isinstance(s, int):
                if s == starts[c + 1] - starts[first] + 1:
                    each_copy(c, lambda copy: copy.start())
            elif c + 1 < last:

                @pl.when(s == starts[c + 1] - starts[first] + 1)
                def _():
                    each_copy(c, lambda copy: copy.start())

    total = starts[last] - starts[first]
    run_steps(
        total, place, a_ref, a_ref, ln_ref, rn, cov0, cov1, old0, old1, keep, turn, before
    )
    for c in range(first, last):
        each_copy(c, lambda copy: copy.wait())


def diagonal(centred, norms, out, first, last):
    given = () if out is None else (out,)
    return pl.pallas_call(
        functools.partial(diagonal_kernel, first, last),
        in_specs=[VMEM, VMEM] + [ANY] * len(given),
        out_specs=ANY,
        out_shape=jax.ShapeDtypeStruct((5, FR, FR), jnp.float32),
        input_output_aliases={2: 0} if given else {},
        scratch_shapes=[
            pltpu.VMEM((FR, FR), jnp.float32),
            pltpu.VMEM((FR, FR), jnp.float32),
            pltpu.VMEM((8, FR), jnp.float32),
            *step_scratch(jnp.float32),
            pltpu.SemaphoreType.DMA((FR // COLS,)),
        ],
        compiler_params=PARAMS,
        cost_estimate=pl.CostEstimate(
            flops=9 * FR * FR * ATOMS, bytes_accessed=6 << 20, transcendentals=0
        ),
        name="diagonal",
    )(centred, norms, *given)


def far_kernel(part, a_ref, b_ref, ln_ref, _, out_ref, y_ref, tile, rn, cov0, cov1, old0, old1, sem):
    parity = lax.rem(lax.axis_index("frames"), 2)
    slot = 4 * (1 - parity)
    row_norms(b_ref, rn)
    per = FR // ROWS
    total = per * (HALF // COLS)

    def place(s):
        return (s & (per - 1)) * ROWS, (s // per) * COLS

    def keep(s, old, r, values):
        row, col = place(s)
        tile[aligned(row + r, STEP), aligned(col, COLS)] = values
        old[r : r + STEP, :] = encode(values)

    def turn(s, old):
        row, col = place(s)
        y_ref[aligned(col, COLS), aligned(row, ROWS)] = old[...].T

    def column_copy(c):
        cols = pl.ds(c * COLS, COLS)
        target = out_ref.at[slot, :, pl.ds(part * HALF + c * COLS, COLS)]
        return pltpu.make_async_copy(tile.at[:, cols], target, sem.at[c])

    def before(s):
        for c in range(HALF // COLS):
            if isinstance(s, int):
                if s == (c + 1) * per:
                    column_copy(c).start()
            elif (c + 1) * per < total:

                @pl.when(s == (c + 1) * per)
                def _():
                    column_copy(c).start()

    run_steps(
        total, place, a_ref, b_ref, ln_ref, rn, cov0, cov1, old0, old1, keep, turn, before
    )
    for c in range(HALF // COLS):
        column_copy(c).wait()


def far_part(centred, other, norms, out, part):
    return pl.pallas_call(
        functools.partial(far_kernel, part),
        in_specs=[VMEM, VMEM, VMEM, ANY],
        out_specs=[ANY, VMEM],
        out_shape=[
            jax.ShapeDtypeStruct((5, FR, FR), jnp.float32),
            jax.ShapeDtypeStruct((HALF, FR), jnp.bfloat16),
        ],
        input_output_aliases={3: 0},
        scratch_shapes=[
            pltpu.VMEM((FR, HALF), jnp.float32),
            pltpu.VMEM((8, HALF), jnp.float32),
            *step_scratch(jnp.bfloat16),
            pltpu.SemaphoreType.DMA((HALF // COLS,)),
        ],
        compiler_params=PARAMS,
        cost_estimate=pl.CostEstimate(
            flops=9 * FR * FR * ATOMS, bytes_accessed=6 << 20, transcendentals=0
        ),
        name="far",
    )(centred, other, norms, out)


def quarters_kernel(mate, a_ref, ln_ref, *refs):
    *others, _, out_ref, y_ref, b_ref, tile, rn, cov0, cov1, old0, old1, b_sem, sem = refs
    parity = lax.rem(lax.axis_index("frames"), 2)
    if mate:
        slot, flip = 3 - 2 * parity, parity
    else:
        slot, flip = 1 + 2 * parity, 1 - parity
    size = FR // len(others)
    loads = [
        pltpu.make_async_copy(ref, b_ref.at[:, pl.ds(i * size, size)], b_sem.at[i])
        for i, ref in enumerate(others)
    ]
    for load in loads:
        load.start()
    for load in loads:
        load.wait()
    row_norms(b_ref, rn)
    per_row, per_col = HALF // ROWS, HALF // COLS
    per = per_row * per_col

    def local(s):
        inner = s & (per - 1)
        return s // per, (inner & (per_row - 1)) * ROWS, (inner // per_row) * COLS

    def place(s):
        half, row, col = local(s)
        other = half + flip - 2 * half * flip
        return half * HALF + row, other * HALF + col

    def keep(s, old, r, values):
        half, row, col = local(s)
        tile[half, aligned(row + r, STEP), aligned(col, COLS)] = values
        old[r : r + STEP, :] = encode(values)

    def turn(s, old):
        half, row, col = local(s)
        y_ref[half, aligned(col, COLS), aligned(row, ROWS)] = old[...].T

    def half_copy(half):
        other = half + flip - 2 * half * flip
        target = out_ref.at[slot, pl.ds(half * HALF, HALF), aligned(other * HALF, HALF)]
        return pltpu.make_async_copy(tile.at[half], target, sem.at[half])

    def before(s):
        if isinstance(s, int):
            if s == 2 * per:
                half_copy(1).start()
        else:

            @pl.when(s == per)
            def _():
                half_copy(0).start()

    run_steps(
        2 * per, place, a_ref, b_ref, ln_ref, rn, cov0, cov1, old0, old1, keep, turn, before
    )
    for half in range(2):
        half_copy(half).wait()


def quarters(centred, others, norms, out, mate):
    return pl.pallas_call(
        functools.partial(quarters_kernel, mate),
        in_specs=[VMEM, VMEM] + [ANY] * len(others) + [ANY],
        out_specs=[ANY, VMEM],
        out_shape=[
            jax.ShapeDtypeStruct((5, FR, FR), jnp.float32),
            jax.ShapeDtypeStruct((2, HALF, HALF), jnp.bfloat16),
        ],
        input_output_aliases={2 + len(others): 0},
        scratch_shapes=[
            pltpu.VMEM((3, FR, ATOMS), jnp.bfloat16),
            pltpu.VMEM((2, HALF, HALF), jnp.float32),
            pltpu.VMEM((8, FR), jnp.float32),
            *step_scratch(jnp.bfloat16),
            pltpu.SemaphoreType.DMA((len(others),)),
            pltpu.SemaphoreType.DMA((2,)),
        ],
        compiler_params=PARAMS,
        cost_estimate=pl.CostEstimate(
            flops=9 * FR * FR * ATOMS, bytes_accessed=6 << 20, transcendentals=0
        ),
        name="mate" if mate else "near",
    )(centred, norms, *others, out)


def decode(values):
    return lax.rsqrt(lax.rsqrt(values.astype(jnp.float32)))


def received_kernel(far0, far1, near, mate, _, out_ref, far_tile, near_tile, mate_tile, sem):
    parity = lax.rem(lax.axis_index("frames"), 2)
    copies = []
    for i, (ref, rows) in enumerate(((far0, pl.ds(0, HALF)), (far1, pl.ds(HALF, HALF)))):
        far_tile[rows, :] = decode(ref[...])
        copies.append(pltpu.make_async_copy(
            far_tile.at[rows], out_ref.at[4 * parity, rows], sem.at[i]
        ))
        copies[-1].start()
    for i, (ref, tile, slot, flip) in enumerate(
        ((near, near_tile, 1 + 2 * parity, parity), (mate, mate_tile, 3 - 2 * parity, 1 - parity))
    ):
        for half in range(2):
            tile[half] = decode(ref[half])
            own = half + flip - 2 * half * flip
            copies.append(pltpu.make_async_copy(
                tile.at[half],
                out_ref.at[slot, aligned(own * HALF, HALF), pl.ds(half * HALF, HALF)],
                sem.at[2 + 2 * i + half],
            ))
            copies[-1].start()
    for copy in copies:
        copy.wait()


def received(far0, far1, near, mate, out):
    return pl.pallas_call(
        received_kernel,
        in_specs=[VMEM, VMEM, VMEM, VMEM, ANY],
        out_specs=ANY,
        out_shape=jax.ShapeDtypeStruct((5, FR, FR), jnp.float32),
        input_output_aliases={4: 0},
        scratch_shapes=[
            pltpu.VMEM((FR, FR), jnp.float32),
            pltpu.VMEM((2, HALF, HALF), jnp.float32),
            pltpu.VMEM((2, HALF, HALF), jnp.float32),
            pltpu.SemaphoreType.DMA((6,)),
        ],
        compiler_params=PARAMS,
        name="received",
    )(far0, far1, near, mate, out)


def on_device(coords):
    count = lax.axis_size("frames")
    reach = [2 if s % 2 == 0 else -2 for s in range(count)]
    fetch_far = [((s + reach[s]) % count, s) for s in range(count)]
    send_far = [(s, (s + reach[s]) % count) for s in range(count)]
    send_near = [(s, (s - 1 if s % 2 == 0 else s + 1) % count) for s in range(count)]
    swap = [(s, s ^ 1) for s in range(count)]
    move = functools.partial(lax.ppermute, axis_name="frames")

    centred, low, high, norms = centre(coords)
    far_low = move(low, perm=fetch_far)
    far_high = move(high, perm=fetch_far)
    mate = move(centred, perm=swap)
    blocks = FR // COLS
    out = diagonal(centred, norms, None, 0, blocks - 1)
    far_low, out = lax.optimization_barrier((far_low, out))
    near_low = move(far_low, perm=swap)
    out, far0 = far_part(centred, far_low, norms, out, 0)
    far_high, out, far0 = lax.optimization_barrier((far_high, out, far0))
    near_high = move(far_high, perm=swap)
    far0 = move(far0, perm=send_far)
    out, far1 = far_part(centred, far_high, norms, out, 1)
    far1 = move(far1, perm=send_far)
    out, near_y = quarters(centred, (near_low, near_high), norms, out, False)
    near_y = move(near_y, perm=send_near)
    out, mate_y = quarters(centred, (mate,), norms, out, True)
    mate_y = move(mate_y, perm=swap)
    out = diagonal(centred, norms, out, blocks - 1, blocks)
    out = received(far0, far1, near_y, mate_y, out)
    return jnp.transpose(out, (1, 0, 2))


def solution(mesh):
    return jax.shard_map(
        on_device,
        mesh=mesh,
        in_specs=(P(None, "frames", None),),
        out_specs=P("frames", None, None),
        check_vma=False,
    )
```

time: 104 us -> 99.7 us (0.959)
  Pallas kernels: 85.3 us -> 80.7 us
  starting transfers between devices: 12.8 us -> 15.8 us
  waiting for transfers between devices: 2.54 us -> 0.02 us
  local copies, waits for them, and re-layouts: 2.48 us -> 1.41 us
    pallas_call x4 -> x5, Pallas kernels: 52.2 us -> 48.3 us  [the longest x2 26.6 us: far_part(): pl.pallas_call(functools.partial(far_kernel, part), in_specs=[VMEM, VMEM,...]
    ppermute x1, waiting for transfers between devices: 1.86 us -> 0.01 us  [on_device(): near_y = move(near_y, perm=send_near)]
    ppermute x1, starting transfers between devices: 0.08 us -> 1.68 us  [on_device(): far0 = move(far0, perm=send_far)]
    ppermute x2 -> x4, starting transfers between devices: 8.85 us -> 9.94 us  [the longest x1 8.83 us: on_device(): far_low = move(low, perm=fetch_far)]
    unnamed x4 -> x2, local copies, waits for them, and re-layouts: 2.48 us -> 1.41 us
  transfers between devices with their start and end apart: 7 -> 9, of which waited for: 2 -> 0; matrix products, arithmetic and copies ran while one was open for 0% -> 0% of each run, Pallas kernels for 75% -> 76%
where the time goes in v2:
time: 99.7 us; the launch traced here: 98.2 us
  Pallas kernels  80.7 us (81%)
  starting transfers between devices  15.8 us (16%)
  local copies, waits for them, and re-layouts  1.41 us (1%)
    pallas_call x2, Pallas kernels, quarters(): pl.pallas_call(functools.partial(quarters_kernel, mate), in_specs=[VMEM,...  28.5 us
    pallas_call x2, Pallas kernels, far_part(): pl.pallas_call(functools.partial(far_kernel, part), in_specs=[VMEM, VMEM,...  26.6 us
    pallas_call x2, Pallas kernels, diagonal(): pl.pallas_call(functools.partial(diagonal_kernel, first, last), in_specs=...  19.7 us
    ppermute x1, starting transfers between devices, on_device(): far_low = move(low, perm=fetch_far)  8.83 us
    pallas_call x1, Pallas kernels, received(): pl.pallas_call(received_kernel, in_specs=[VMEM, VMEM, VMEM, VMEM, ANY], o...  3.9 us
    ppermute x1, starting transfers between devices, on_device(): near_y = move(near_y, perm=send_near)  3.74 us
  transfers between devices with their start and end apart: 9, of which 0 were waited for; matrix products, arithmetic and copies ran while one was open for 0% of the time, Pallas kernels for 76%

profile of v2, /device:TPU:0, one launch (start us, length us, event | category | flops | bytes accessed | tf_op | source)
XLA Modules:
  0.0 98.2 jit_solution(10047748174948195204)
XLA Ops:
  0.0 0.0 copy-start
  0.0 1.4 %copy-done = bf16[3,1024,256]{2,1,0:T(8,128)(2,1)S(1)} copy-done((bf16[3,1024,256]{2,1,0:T(8,128)(2,1)S(1)}, bf16[3,1024,256]{2,1,0:T(8,128)(2,1)}, u32[]{:S(2)}) %copy-start) | copy-done | bytes 1572888
  1.4 1.9 %centre.1 = (bf16[3,1024,256]{2,1,0:T(8,128)(2,1)S(1)}, bf16[3,512,256]{2,1,0:T(8,128)(2,1)S(1)}, bf16[3,512,256]{2,1,0:T(8,128)(2,1)S(1)}, f32[1024,128]{1,0:T(8,128)S(1)}) custom-call(bf16[3,1024,256]{2,1,0:T(8,128)(2,1)S(1)} %copy-done), custom_call_target="tpu_custom_call" | custom-call | tf_op jit(solution)/shard_map/centre/pallas_call | solution.py:48
  3.3 8.8 %collective-permute-start.1 = (bf16[3,512,256]{2,1,0:T(8,128)(2,1)S(1)}, bf16[3,512,256]{2,1,0:T(8,128)(2,1)S(1)}, u32[]{:S(2)}, u32[]{:S(2)}) collective-permute-start(bf16[3,512,256]{2,1,0:T(8,128)(2,1)S(1)} %get-tuple-element.24), channel_id=1, source_target_pairs={{2,0},{127,1},{4,2},{1,3},{6,4},{3,5},{8,6},{5,7},{10,8},{7,9},{12... | collective-permute-start | bytes 2359304 | tf_op jit(solution)/shard_map/ppermute | solution.py:449
  12.2 0.4 collective-permute-start
  12.6 0.0 collective-permute-start.7
  12.6 11.3 %diagonal.2._ = f32[5,1024,1024]{2,1,0:T(8,128)} custom-call(bf16[3,1024,256]{2,1,0:T(8,128)(2,1)S(1)} %get-tuple-element.23.a_ref, f32[1024,128]{1,0:T(8,128)S(1)} %get-tuple-element.25.ln_ref), custom_call_target="tpu_custom_call" | custom-call | flops 2415919104 | bytes 6291456 | tf_op jit(solution)/shard_map/diagonal/pallas_call | solution.py:219
  23.8 0.0 collective-permute-done.1.b_ref
  23.8 0.6 collective-permute-start.4
  24.4 13.3 %far.2 = (f32[5,1024,1024]{2,1,0:T(8,128)}, bf16[512,1024]{1,0:T(8,128)(2,1)S(1)}) custom-call(bf16[3,1024,256]{2,1,0:T(8,128)(2,1)S(1)} %get-tuple-element.23.a_ref, bf16[3,512,256]{2,1,0:T(8,128)(2,1)S(1)} %collective-permute-done.1.b_ref, f32[1024,128]{1,0:T(8,128)S(1)} %get-tuple-element.25.ln_ref, ...), custom_call_target="tpu_custom_call", output_to_operand_aliasing={{0}: (3, {})} | custom-call | flops 2415919104 | bytes 6291456 | tf_op jit(solution)/shard_map/far/pallas_call | solution.py:283
  37.7 0.0 collective-permute-done.b_ref
  37.7 0.1 collective-permute-start.5
  37.9 1.7 %collective-permute-start.2 = (bf16[512,1024]{1,0:T(8,128)(2,1)S(1)}, bf16[512,1024]{1,0:T(8,128)(2,1)S(1)}, u32[]{:S(2)}, u32[]{:S(2)}) collective-permute-start(bf16[512,1024]{1,0:T(8,128)(2,1)S(1)} %get-tuple-element.30), channel_id=1, source_target_pairs={{0,2},{1,127},{2,4},{3,1},{4,6},{5,3},{6,8},{7,5},{8,10},{9,7},{10... | collective-permute-start | bytes 3145736 | tf_op jit(solution)/shard_map/ppermute | solution.py:459
  39.5 13.3 %far.3 = (f32[5,1024,1024]{2,1,0:T(8,128)}, bf16[512,1024]{1,0:T(8,128)(2,1)S(1)}) custom-call(bf16[3,1024,256]{2,1,0:T(8,128)(2,1)S(1)} %get-tuple-element.23.a_ref, bf16[3,512,256]{2,1,0:T(8,128)(2,1)S(1)} %collective-permute-done.b_ref, f32[1024,128]{1,0:T(8,128)S(1)} %get-tuple-element.25.ln_ref, ...), custom_call_target="tpu_custom_call", output_to_operand_aliasing={{0}: (3, {})} | custom-call | flops 2415919104 | bytes 6291456 | tf_op jit(solution)/shard_map/far/pallas_call | solution.py:283
  52.9 0.1 collective-permute-start.3
  53.0 0.0 collective-permute-done.4.refs_0_
  53.0 0.0 collective-permute-done.5.refs_1_
  53.0 14.3 %near.1 = (f32[5,1024,1024]{2,1,0:T(8,128)}, bf16[2,512,512]{2,1,0:T(8,128)(2,1)S(1)}) custom-call(bf16[3,1024,256]{2,1,0:T(8,128)(2,1)S(1)} %get-tuple-element.23.a_ref, f32[1024,128]{1,0:T(8,128)S(1)} %get-tuple-element.25.ln_ref, bf16[3,512,256]{2,1,0:T(8,128)(2,1)S(1)} %collective-permute-done.4.refs_0_, ...), custom_call_target="tpu_custom_call", output_to_operand_aliasing={{0}: (4, {})} | custom-call | flops 2415919104 | bytes 6291456 | tf_op jit(solution)/shard_map/near/pallas_call | solution.py:367
  67.3 3.7 %collective-permute-start.6 = (bf16[2,512,512]{2,1,0:T(8,128)(2,1)S(1)}, bf16[2,512,512]{2,1,0:T(8,128)(2,1)S(1)}, u32[]{:S(2)}, u32[]{:S(2)}) collective-permute-start(bf16[2,512,512]{2,1,0:T(8,128)(2,1)S(1)} %get-tuple-element.35), channel_id=1, source_target_pairs={{0,127},{1,2},{2,1},{3,4},{4,3},{5,6},{6,5},{7,8},{8,7},{9,10},{10... | collective-permute-start | bytes 3145736 | tf_op jit(solution)/shard_map/ppermute | solution.py:463
  71.1 0.0 collective-permute-done.7.refs_0_
  71.1 14.2 %mate.1 = (f32[5,1024,1024]{2,1,0:T(8,128)}, bf16[2,512,512]{2,1,0:T(8,128)(2,1)S(1)}) custom-call(bf16[3,1024,256]{2,1,0:T(8,128)(2,1)S(1)} %get-tuple-element.23.a_ref, f32[1024,128]{1,0:T(8,128)S(1)} %get-tuple-element.25.ln_ref, bf16[3,1024,256]{2,1,0:T(8,128)(2,1)S(1)} %collective-permute-done.7.refs_0_, ...), custom_call_target="tpu_custom_call", output_to_operand_aliasing={{0}: (3, {})} | custom-call | flops 2415919104 | bytes 6291456 | tf_op jit(solution)/shard_map/mate/pallas_call | solution.py:367
  85.2 0.4 collective-permute-start.8
  85.6 8.5 %diagonal.3._ = f32[5,1024,1024]{2,1,0:T(8,128)} custom-call(bf16[3,1024,256]{2,1,0:T(8,128)(2,1)S(1)} %get-tuple-element.23.a_ref, f32[1024,128]{1,0:T(8,128)S(1)} %get-tuple-element.25.ln_ref, f32[5,1024,1024]{2,1,0:T(8,128)} %get-tuple-element.38.refs_0_), custom_call_target="tpu_custom_call", output_to_operand_aliasing={{}: (2, {})} | custom-call | flops 2415919104 | bytes 6291456 | tf_op jit(solution)/shard_map/diagonal/pallas_call | solution.py:219
  94.1 0.0 collective-permute-done.2.far0
  94.1 0.0 collective-permute-done.3.far1
  94.1 0.0 collective-permute-done.6.near
  94.1 0.0 collective-permute-done.8.mate
  94.2 3.9 %received.1 = f32[5,1024,1024]{2,1,0:T(8,128)} custom-call(bf16[512,1024]{1,0:T(8,128)(2,1)S(1)} %collective-permute-done.2.far0, bf16[512,1024]{1,0:T(8,128)(2,1)S(1)} %collective-permute-done.3.far1, bf16[2,512,512]{2,1,0:T(8,128)(2,1)S(1)} %collective-permute-done.6.near, ...), custom_call_target="tpu_custom_call", output_to_operand_aliasing={{}: (4, {})} | custom-call | tf_op jit(solution)/shard_map/received/pallas_call | solution.py:422
Async XLA Ops:
  0.0 1.4 %copy-start = (bf16[3,1024,256]{2,1,0:T(8,128)(2,1)S(1)}, bf16[3,1024,256]{2,1,0:T(8,128)(2,1)}, u32[]{:S(2)}) copy-start(bf16[3,1024,256]{2,1,0:T(8,128)(2,1)} %x_ref.1) | copy-start | bytes 4718596
  3.3 20.5 %collective-permute-start.1 = (bf16[3,512,256]{2,1,0:T(8,128)(2,1)S(1)}, bf16[3,512,256]{2,1,0:T(8,128)(2,1)S(1)}, u32[]{:S(2)}, u32[]{:S(2)}) collective-permute-start(bf16[3,512,256]{2,1,0:T(8,128)(2,1)S(1)} %get-tuple-element.24), channel_id=1, source_target_pairs={{2,0},{127,1},{4,2},{1,3},{6,4},{3,5},{8,6},{5,7},{10,8},{7,9},{12... | collective-permute-start | bytes 2359304 | tf_op jit(solution)/shard_map/ppermute | solution.py:449
  12.2 25.6 %collective-permute-start = (bf16[3,512,256]{2,1,0:T(8,128)(2,1)S(1)}, bf16[3,512,256]{2,1,0:T(8,128)(2,1)S(1)}, u32[]{:S(2)}, u32[]{:S(2)}) collective-permute-start(bf16[3,512,256]{2,1,0:T(8,128)(2,1)S(1)} %get-tuple-element.22), channel_id=1, source_target_pairs={{2,0},{127,1},{4,2},{1,3},{6,4},{3,5},{8,6},{5,7},{10,8},{7,9},{12... | collective-permute-start | bytes 2359304 | tf_op jit(solution)/shard_map/ppermute | solution.py:450
  12.6 58.5 %collective-permute-start.7 = (bf16[3,1024,256]{2,1,0:T(8,128)(2,1)S(1)}, bf16[3,1024,256]{2,1,0:T(8,128)(2,1)S(1)}, u32[]{:S(2)}, u32[]{:S(2)}) collective-permute-start(bf16[3,1024,256]{2,1,0:T(8,128)(2,1)S(1)} %get-tuple-element.23.a_ref), channel_id=1, source_target_pairs={{0,1},{1,0},{2,3},{3,2},{4,5},{5,4},{6,7},{7,6},{8,9},{9,8},{10,11... | collective-permute-start | bytes 4718600 | tf_op jit(solution)/shard_map/ppermute | solution.py:451
  23.8 29.1 %collective-permute-start.4 = (bf16[3,512,256]{2,1,0:T(8,128)(2,1)S(1)}, bf16[3,512,256]{2,1,0:T(8,128)(2,1)S(1)}, u32[]{:S(2)}, u32[]{:S(2)}) collective-permute-start(bf16[3,512,256]{2,1,0:T(8,128)(2,1)S(1)} %collective-permute-done.1.b_ref), channel_id=1, source_target_pairs={{0,1},{1,0},{2,3},{3,2},{4,5},{5,4},{6,7},{7,6},{8,9},{9,8},{10,11... | collective-permute-start | bytes 2359304 | tf_op jit(solution)/shard_map/ppermute | solution.py:455
  37.7 15.2 %collective-permute-start.5 = (bf16[3,512,256]{2,1,0:T(8,128)(2,1)S(1)}, bf16[3,512,256]{2,1,0:T(8,128)(2,1)S(1)}, u32[]{:S(2)}, u32[]{:S(2)}) collective-permute-start(bf16[3,512,256]{2,1,0:T(8,128)(2,1)S(1)} %collective-permute-done.b_ref), channel_id=1, source_target_pairs={{0,1},{1,0},{2,3},{3,2},{4,5},{5,4},{6,7},{7,6},{8,9},{9,8},{10,11... | collective-permute-start | bytes 2359304 | tf_op jit(solution)/shard_map/ppermute | solution.py:458
  37.9 56.3 %collective-permute-start.2 = (bf16[512,1024]{1,0:T(8,128)(2,1)S(1)}, bf16[512,1024]{1,0:T(8,128)(2,1)S(1)}, u32[]{:S(2)}, u32[]{:S(2)}) collective-permute-start(bf16[512,1024]{1,0:T(8,128)(2,1)S(1)} %get-tuple-element.30), channel_id=1, source_target_pairs={{0,2},{1,127},{2,4},{3,1},{4,6},{5,3},{6,8},{7,5},{8,10},{9,7},{10... | collective-permute-start | bytes 3145736 | tf_op jit(solution)/shard_map/ppermute | solution.py:459
  52.9 41.3 %collective-permute-start.3 = (bf16[512,1024]{1,0:T(8,128)(2,1)S(1)}, bf16[512,1024]{1,0:T(8,128)(2,1)S(1)}, u32[]{:S(2)}, u32[]{:S(2)}) collective-permute-start(bf16[512,1024]{1,0:T(8,128)(2,1)S(1)} %get-tuple-element.33), channel_id=1, source_target_pairs={{0,2},{1,127},{2,4},{3,1},{4,6},{5,3},{6,8},{7,5},{8,10},{9,7},{10... | collective-permute-start | bytes 3145736 | tf_op jit(solution)/shard_map/ppermute | solution.py:461
  67.3 26.8 %collective-permute-start.6 = (bf16[2,512,512]{2,1,0:T(8,128)(2,1)S(1)}, bf16[2,512,512]{2,1,0:T(8,128)(2,1)S(1)}, u32[]{:S(2)}, u32[]{:S(2)}) collective-permute-start(bf16[2,512,512]{2,1,0:T(8,128)(2,1)S(1)} %get-tuple-element.35), channel_id=1, source_target_pairs={{0,127},{1,2},{2,1},{3,4},{4,3},{5,6},{6,5},{7,8},{8,7},{9,10},{10... | collective-permute-start | bytes 3145736 | tf_op jit(solution)/shard_map/ppermute | solution.py:463
  85.2 8.9 %collective-permute-start.8 = (bf16[2,512,512]{2,1,0:T(8,128)(2,1)S(1)}, bf16[2,512,512]{2,1,0:T(8,128)(2,1)S(1)}, u32[]{:S(2)}, u32[]{:S(2)}) collective-permute-start(bf16[2,512,512]{2,1,0:T(8,128)(2,1)S(1)} %get-tuple-element.37), channel_id=1, source_target_pairs={{0,1},{1,0},{2,3},{3,2},{4,5},{5,4},{6,7},{7,6},{8,9},{9,8},{10,11... | collective-permute-start | bytes 3145736 | tf_op jit(solution)/shard_map/ppermute | solution.py:465

commit v3 on v2

v3 whole, which is shorter than its diff:
```python
import functools

import jax
import jax.numpy as jnp
from jax import lax
from jax.experimental import pallas as pl
from jax.experimental.pallas import tpu as pltpu
from jax.sharding import PartitionSpec as P

NEWTON = 8
FR = 1024
ATOMS = 256
ROWS = 128
COLS = 256
STEP = 16
HALF = FR // 2
VMEM = pl.BlockSpec(memory_space=pltpu.VMEM)
ANY = pl.BlockSpec(memory_space=pl.ANY)
PARAMS = pltpu.CompilerParams(vmem_limit_bytes=8 << 20)
COST = pl.CostEstimate(flops=9 * FR * FR * ATOMS, bytes_accessed=6 << 20, transcendentals=0)


def aligned(index, size):
    return pl.ds(pl.multiple_of(index, size), size)


def centre_kernel(x_ref, c_ref, low_ref, high_ref, n_ref):
    for part, ref in enumerate((low_ref, high_ref)):

        @pl.loop(0, HALF // ROWS)
        def _(i):
            inner = aligned(i * ROWS, ROWS)
            rows = aligned(part * HALF + i * ROWS, ROWS)
            total = None
            for k in range(3):
                values = x_ref[k, rows, :].astype(jnp.float32)
                mean = jnp.sum(values, axis=1, keepdims=True) * (1.0 / ATOMS)
                centred = (values - mean).astype(jnp.bfloat16)
                c_ref[k, rows, :] = centred
                ref[k, inner, :] = centred
                back = centred.astype(jnp.float32)
                square = back * back
                total = square if total is None else total + square
            norms = 0.5 * jnp.sum(total, axis=1, keepdims=True)
            n_ref[rows, :] = jnp.broadcast_to(norms, (ROWS, 128))


def centre(coords):
    return pl.pallas_call(
        centre_kernel,
        in_specs=[VMEM],
        out_specs=[VMEM] * 4,
        out_shape=[
            jax.ShapeDtypeStruct((3, FR, ATOMS), jnp.bfloat16),
            jax.ShapeDtypeStruct((3, HALF, ATOMS), jnp.bfloat16),
            jax.ShapeDtypeStruct((3, HALF, ATOMS), jnp.bfloat16),
            jax.ShapeDtypeStruct((FR, 128), jnp.float32),
        ],
        compiler_params=pltpu.CompilerParams(vmem_limit_bytes=16 << 20),
        name="centre",
    )(coords)


def row_norms(b_ref, rn_ref):
    @pl.loop(0, b_ref.shape[1] // 128)
    def _(i):
        frames = aligned(i * 128, 128)
        total = None
        for k in range(3):
            values = b_ref[k, frames, :].astype(jnp.float32)
            total = values * values if total is None else total + values * values
        norms = 0.5 * jnp.sum(total, axis=1, keepdims=True)
        square = jnp.broadcast_to(norms, (128, 128)).T
        rn_ref[:, frames] = square[0:8, :]


def invariants(entry):
    (a, b, c), (d, f, g), (h, i, j) = entry
    first = a * a + b * b + c * c
    others = (d * d + f * f + g * g) + (h * h + i * i + j * j)
    p = f * j - g * i
    q = g * h - d * j
    r = d * i - f * h
    det = a * p + b * q + c * r
    one = a * d + b * f + c * g
    two = a * h + b * i + c * j
    minors = (first * others - one * one - two * two) + (p * p + q * q + r * r)
    return first + others, det + det, minors


def deviations(entry, left, right):
    n, f, m = invariants(entry)
    start = left + right
    top = start
    for _ in range(NEWTON):
        h = top * top - n
        top = ((h * 0.75 + n) * h + m) * pltpu.reciprocal(top * h - f, approx=True)
    return (start - top) * (2.0 / ATOMS)


def covariance_pieces(a_ref, b_ref, row, col, cov_ref):
    left = a_ref[:, aligned(row, ROWS), :].reshape(3 * ROWS, ATOMS)
    for k in range(3):
        right = b_ref[k, aligned(col, COLS), :]
        block = lax.dot_general(
            left, right, (((1,), (1,)), ((), ())), preferred_element_type=jnp.float32
        )
        cov_ref[:, k] = block.reshape(3, ROWS, COLS)
        yield


def value_pieces(cov_ref, ln_ref, rn_ref, row, col, emit):
    for r in range(0, ROWS, STEP):
        entry = [[cov_ref[k, l, r : r + STEP, :] for l in range(3)] for k in range(3)]
        left = ln_ref[aligned(row + r, STEP), :]
        left = jnp.concatenate([left] * (COLS // 128), axis=1)
        right = rn_ref[:, aligned(col, COLS)]
        right = jnp.concatenate([right] * (STEP // 8), axis=0)
        emit(r, deviations(entry, left, right))
        yield


def run_steps(total, place, a_ref, b_ref, ln_ref, rn_ref, cov0, cov1, old0, old1, keep, turn):
    for _ in covariance_pieces(a_ref, b_ref, *place(0), cov0):
        pass

    def step(s, cov, cov_next, old, old_last):
        row, col = place(jnp.minimum(s + 1, total - 1))
        products = covariance_pieces(a_ref, b_ref, row, col, cov_next)
        row, col = place(s)
        values = value_pieces(cov, ln_ref, rn_ref, row, col, functools.partial(keep, s, old))
        for count, _ in enumerate(values):
            if count in (0, 2, 4):
                next(products)
        turn(jnp.maximum(s - 1, 0), old_last)

    @pl.loop(0, total)
    def _(s):
        @pl.when((s & 1) == 0)
        def _():
            step(s, cov0, cov1, old0, old1)

        @pl.when((s & 1) == 1)
        def _():
            step(s, cov1, cov0, old1, old0)

    turn(total - 1, old1 if total % 2 == 0 else old0)


def encode(values):
    square = values * values
    return (square * square).astype(jnp.bfloat16)


def step_scratch(kind):
    return [
        pltpu.VMEM((3, 3, ROWS, COLS), jnp.float32),
        pltpu.VMEM((3, 3, ROWS, COLS), jnp.float32),
        pltpu.VMEM((ROWS, COLS), kind),
        pltpu.VMEM((ROWS, COLS), kind),
    ]


def diagonal_steps(first, last, a_ref, ln_ref, tile, mirror, rn, scratch):
    row_norms(a_ref, rn)
    per = COLS // ROWS
    starts = [per * c * (c + 1) // 2 for c in range(FR // COLS + 1)]

    def place(s):
        s = s + starts[first]
        col = sum(jnp.where(s >= start, 1, 0) for start in starts[1:last])
        row = s - per * (col * (col + 1) // 2)
        return row * ROWS, col * COLS

    def keep(s, old, r, values):
        row, col = place(s)
        tile[aligned(row + r, STEP), aligned(col, COLS)] = values
        old[r : r + STEP, :] = values

    def turn(s, old):
        row, col = place(s)
        mirror[aligned(col, COLS), aligned(row, ROWS)] = old[...].T

    run_steps(starts[last] - starts[first], place, a_ref, a_ref, ln_ref, rn, *scratch, keep, turn)


def diagonal_kernel(last, a_ref, ln_ref, tile, mirror, rn, *scratch):
    diagonal_steps(0, last, a_ref, ln_ref, tile, mirror, rn, scratch)


def diagonal(centred, norms, last):
    return pl.pallas_call(
        functools.partial(diagonal_kernel, last),
        in_specs=[VMEM, VMEM],
        out_specs=[VMEM, VMEM],
        out_shape=[jax.ShapeDtypeStruct((last * COLS, last * COLS), jnp.float32)] * 2,
        scratch_shapes=[pltpu.VMEM((8, FR), jnp.float32), *step_scratch(jnp.float32)],
        compiler_params=PARAMS,
        cost_estimate=COST,
        name="diagonal",
    )(centred, norms)


def far_kernel(a_ref, b_ref, ln_ref, tile, y_ref, rn, *scratch):
    row_norms(b_ref, rn)
    per = FR // ROWS

    def place(s):
        return (s & (per - 1)) * ROWS, (s // per) * COLS

    def keep(s, old, r, values):
        row, col = place(s)
        tile[aligned(row + r, STEP), aligned(col, COLS)] = values
        old[r : r + STEP, :] = encode(values)

    def turn(s, old):
        row, col = place(s)
        y_ref[aligned(col, COLS), aligned(row, ROWS)] = old[...].T

    run_steps(
        per * (HALF // COLS), place, a_ref, b_ref, ln_ref, rn, *scratch, keep, turn
    )


def far_part(centred, other, norms):
    return pl.pallas_call(
        far_kernel,
        in_specs=[VMEM, VMEM, VMEM],
        out_specs=[VMEM, VMEM],
        out_shape=[
            jax.ShapeDtypeStruct((FR, HALF), jnp.float32),
            jax.ShapeDtypeStruct((HALF, FR), jnp.bfloat16),
        ],
        scratch_shapes=[pltpu.VMEM((8, HALF), jnp.float32), *step_scratch(jnp.bfloat16)],
        compiler_params=PARAMS,
        cost_estimate=COST,
        name="far",
    )(centred, other, norms)


def other_half(half, flip):
    return half + flip - 2 * half * flip


def mate_place():
    parity = lax.rem(lax.axis_index("frames"), 2)
    return 3 - 2 * parity, parity


def near_place():
    parity = lax.rem(lax.axis_index("frames"), 2)
    return 1 + 2 * parity, 1 - parity


def quarters_kernel(where, a_ref, ln_ref, *refs):
    *others, tile, y_ref, b_ref, rn, cov0, cov1, old0, old1, sem = refs
    _, flip = where()
    size = FR // len(others)
    loads = [
        pltpu.make_async_copy(ref, b_ref.at[:, pl.ds(i * size, size)], sem.at[i])
        for i, ref in enumerate(others)
    ]
    for load in loads:
        load.start()
    for load in loads:
        load.wait()
    row_norms(b_ref, rn)
    per_row, per_col = HALF // ROWS, HALF // COLS
    per = per_row * per_col

    def local(s):
        inner = s & (per - 1)
        return s // per, (inner & (per_row - 1)) * ROWS, (inner // per_row) * COLS

    def place(s):
        half, row, col = local(s)
        return half * HALF + row, other_half(half, flip) * HALF + col

    def keep(s, old, r, values):
        half, row, col = local(s)
        tile[half, aligned(row + r, STEP), aligned(col, COLS)] = values
        old[r : r + STEP, :] = encode(values)

    def turn(s, old):
        half, row, col = local(s)
        y_ref[half, aligned(col, COLS), aligned(row, ROWS)] = old[...].T

    run_steps(
        2 * per, place, a_ref, b_ref, ln_ref, rn, cov0, cov1, old0, old1, keep, turn
    )


def quarters(centred, others, norms, where, name):
    return pl.pallas_call(
        functools.partial(quarters_kernel, where),
        in_specs=[VMEM, VMEM] + [ANY] * len(others),
        out_specs=[VMEM, VMEM],
        out_shape=[
            jax.ShapeDtypeStruct((2, HALF, HALF), jnp.float32),
            jax.ShapeDtypeStruct((2, HALF, HALF), jnp.bfloat16),
        ],
        scratch_shapes=[
            pltpu.VMEM((3, FR, ATOMS), jnp.bfloat16),
            pltpu.VMEM((8, FR), jnp.float32),
            *step_scratch(jnp.bfloat16),
            pltpu.SemaphoreType.DMA((len(others),)),
        ],
        compiler_params=PARAMS,
        cost_estimate=COST,
        name=name,
    )(centred, norms, *others)


def decode(values):
    return lax.rsqrt(lax.rsqrt(values.astype(jnp.float32)))


def finish_kernel(
    done, a_ref, ln_ref, diag, turned, far0, far1, near, mate, far0_y, far1_y, near_y, mate_y,
    out_ref, tile, mirror, far_tile, near_tile, mate_tile, rn, *scratch,
):
    *scratch, sem = scratch
    parity = lax.rem(lax.axis_index("frames"), 2)
    copies = []

    def copy(source, slot, rows, cols):
        copies.append(
            pltpu.make_async_copy(source, out_ref.at[slot, rows, cols], sem.at[len(copies)])
        )
        copies[-1].start()

    def half(i):
        return aligned(i * HALF, HALF)

    both = pl.ds(0, FR)
    for i, tiles in enumerate((far0, far1)):
        copy(tiles, 4 * (1 - parity), both, half(i))
    for tiles, where in ((near, near_place), (mate, mate_place)):
        slot, flip = where()
        for i in range(2):
            copy(tiles.at[i], slot, half(i), half(other_half(i, flip)))
    for c in range(done):
        rows, cols = pl.ds(0, (c + 1) * COLS), pl.ds(c * COLS, COLS)
        copy(diag.at[rows, cols], 2, rows, cols)
        if c > 0:
            rows = pl.ds(0, c * COLS)
            copy(turned.at[cols, rows], 2, cols, rows)

    for i, ref in enumerate((far0_y, far1_y)):
        far_tile[i] = decode(ref[...])
        copy(far_tile.at[i], 4 * parity, half(i), both)
    for ref, tiles, where in ((near_y, near_tile, near_place), (mate_y, mate_tile, mate_place)):
        slot, flip = where()
        for i in range(2):
            tiles[i] = decode(ref[i])
            copy(tiles.at[i], slot, half(other_half(i, 1 - flip)), half(i))

    last = FR // COLS
    diagonal_steps(done, last, a_ref, ln_ref, tile, mirror, rn, scratch)
    start = done * COLS
    left, below, right = pl.ds(0, start), pl.ds(start, FR - start), both
    copy(tile.at[right, below], 2, right, below)
    copy(mirror.at[below, left], 2, below, left)
    for each in copies:
        each.wait()


def finish(centred, norms, tiles, coded, done):
    return pl.pallas_call(
        functools.partial(finish_kernel, done),
        in_specs=[VMEM, VMEM] + [ANY] * 6 + [VMEM] * 4,
        out_specs=ANY,
        out_shape=jax.ShapeDtypeStruct((5, FR, FR), jnp.float32),
        scratch_shapes=[
            pltpu.VMEM((FR, FR), jnp.float32),
            pltpu.VMEM((FR, FR), jnp.float32),
            pltpu.VMEM((2, HALF, FR), jnp.float32),
            pltpu.VMEM((2, HALF, HALF), jnp.float32),
            pltpu.VMEM((2, HALF, HALF), jnp.float32),
            pltpu.VMEM((8, FR), jnp.float32),
            *step_scratch(jnp.float32),
            pltpu.SemaphoreType.DMA((32,)),
        ],
        compiler_params=pltpu.CompilerParams(vmem_limit_bytes=26 << 20),
        cost_estimate=COST,
        name="finish",
    )(centred, norms, *tiles, *coded)


def on_device(coords):
    count = lax.axis_size("frames")
    reach = [2 if s % 2 == 0 else -2 for s in range(count)]
    fetch_far = [((s + reach[s]) % count, s) for s in range(count)]
    send_far = [(s, (s + reach[s]) % count) for s in range(count)]
    send_near = [(s, (s - 1 if s % 2 == 0 else s + 1) % count) for s in range(count)]
    swap = [(s, s ^ 1) for s in range(count)]
    move = functools.partial(lax.ppermute, axis_name="frames")

    centred, low, high, norms = centre(coords)
    far_low = move(low, perm=fetch_far)
    far_high = move(high, perm=fetch_far)
    mate = move(centred, perm=swap)
    done = FR // COLS - 1
    diag, turned = diagonal(centred, norms, done)
    far_low, diag = lax.optimization_barrier((far_low, diag))
    near_low = move(far_low, perm=swap)
    far0, far0_y = far_part(centred, far_low, norms)
    far_high, far0, far0_y = lax.optimization_barrier((far_high, far0, far0_y))
    near_high = move(far_high, perm=swap)
    far0_y = move(far0_y, perm=send_far)
    far1, far1_y = far_part(centred, far_high, norms)
    centred, far1_y = lax.optimization_barrier((centred, far1_y))
    far1_y = move(far1_y, perm=send_far)
    near, near_y = quarters(centred, (near_low, near_high), norms, near_place, "near")
    centred, near_y = lax.optimization_barrier((centred, near_y))
    near_y = move(near_y, perm=send_near)
    mate, mate_y = quarters(centred, (mate,), norms, mate_place, "mate")
    mate_y = move(mate_y, perm=swap)
    tiles = (diag, turned, far0, far1, near, mate)
    out = finish(centred, norms, tiles, (far0_y, far1_y, near_y, mate_y), done)
    return jnp.transpose(out, (1, 0, 2))


def solution(mesh):
    return jax.shard_map(
        on_device,
        mesh=mesh,
        in_specs=(P(None, "frames", None),),
        out_specs=P("frames", None, None),
        check_vma=False,
    )
```

time: 99.7 us -> 96.3 us (0.966)
  Pallas kernels: 80.7 us -> 74.1 us
  waiting for transfers between devices: 0.02 us -> 2.56 us
  starting transfers between devices: 15.8 us -> 16.9 us
    pallas_call x7 -> x6, Pallas kernels: 78.8 us -> 72.2 us  [the longest x2 26.4 us: quarters(): pl.pallas_call(functools.partial(quarters_kernel, where), in_specs=[VMEM,...]
    ppermute x1, waiting for transfers between devices: 0.01 us -> 1.41 us  [on_device(): near_y = move(near_y, perm=send_near)]
    ppermute x1, waiting for transfers between devices: 0.01 us -> 1.13 us  [on_device(): mate_y = move(mate_y, perm=swap)]
    ppermute x1, starting transfers between devices: 3.74 us -> 4.82 us  [on_device(): near_y = move(near_y, perm=send_near)]
  transfers between devices with their start and end apart: 9 -> 9, of which waited for: 0 -> 2; matrix products, arithmetic and copies ran while one was open for 0% -> 0% of each run, Pallas kernels for 76% -> 64%
where the time goes in v3:
time: 96.3 us; the launch traced here: 95.2 us
  Pallas kernels  74.1 us (77%)
  starting transfers between devices  16.9 us (18%)
  waiting for transfers between devices  2.56 us (3%)
  local copies, waits for them, and re-layouts  1.41 us (1%)
    pallas_call x2, Pallas kernels, quarters(): pl.pallas_call(functools.partial(quarters_kernel, where), in_specs=[VMEM,...  26.4 us
    pallas_call x2, Pallas kernels, far_part(): pl.pallas_call(far_kernel, in_specs=[VMEM, VMEM, VMEM], out_specs=[VMEM,...  24.7 us
    pallas_call x1, Pallas kernels, finish(): pl.pallas_call(functools.partial(finish_kernel, done), in_specs=[VMEM, VM...  10.9 us
    pallas_call x1, Pallas kernels, diagonal(): pl.pallas_call(functools.partial(diagonal_kernel, last), in_specs=[VMEM,...  10.2 us
    ppermute x1, starting transfers between devices, on_device(): far_low = move(low, perm=fetch_far)  8.83 us
    ppermute x1, starting transfers between devices, on_device(): near_y = move(near_y, perm=send_near)  4.82 us
  transfers between devices with their start and end apart: 9, of which 2 were waited for; matrix products, arithmetic and copies ran while one was open for 0% of the time, Pallas kernels for 64%

profile of v3, /device:TPU:0, one launch (start us, length us, event | category | flops | bytes accessed | tf_op | source)
XLA Modules:
  0.0 95.2 jit_solution(1053802489676935753)
XLA Ops:
  0.0 0.0 copy-start
  0.0 1.4 %copy-done = bf16[3,1024,256]{2,1,0:T(8,128)(2,1)S(1)} copy-done((bf16[3,1024,256]{2,1,0:T(8,128)(2,1)S(1)}, bf16[3,1024,256]{2,1,0:T(8,128)(2,1)}, u32[]{:S(2)}) %copy-start) | copy-done | bytes 1572888
  1.4 1.9 %centre.1 = (bf16[3,1024,256]{2,1,0:T(8,128)(2,1)S(1)}, bf16[3,512,256]{2,1,0:T(8,128)(2,1)S(1)}, bf16[3,512,256]{2,1,0:T(8,128)(2,1)S(1)}, f32[1024,128]{1,0:T(8,128)S(1)}) custom-call(bf16[3,1024,256]{2,1,0:T(8,128)(2,1)S(1)} %copy-done), custom_call_target="tpu_custom_call" | custom-call | tf_op jit(solution)/shard_map/centre/pallas_call | solution.py:49
  3.3 8.8 %collective-permute-start.1 = (bf16[3,512,256]{2,1,0:T(8,128)(2,1)S(1)}, bf16[3,512,256]{2,1,0:T(8,128)(2,1)S(1)}, u32[]{:S(2)}, u32[]{:S(2)}) collective-permute-start(bf16[3,512,256]{2,1,0:T(8,128)(2,1)S(1)} %get-tuple-element.30), channel_id=1, source_target_pairs={{2,0},{127,1},{4,2},{1,3},{6,4},{3,5},{8,6},{5,7},{10,8},{7,9},{12... | collective-permute-start | bytes 2359304 | tf_op jit(solution)/shard_map/ppermute | solution.py:400
  12.2 0.4 collective-permute-start
  12.6 0.0 collective-permute-start.4
  12.6 10.2 %diagonal.1 = (f32[768,768]{1,0:T(8,128)S(1)}, f32[768,768]{1,0:T(8,128)S(1)}) custom-call(bf16[3,1024,256]{2,1,0:T(8,128)(2,1)S(1)} %get-tuple-element.40.a_ref, f32[1024,128]{1,0:T(8,128)S(1)} %get-tuple-element.31.ln_ref), custom_call_target="tpu_custom_call" | custom-call | flops 2415919104 | bytes 6291456 | tf_op jit(solution)/shard_map/diagonal/pallas_call | solution.py:192
  22.8 0.0 collective-permute-done.1.b_ref
  22.8 0.6 collective-permute-start.2
  23.4 12.3 %far.2 = (f32[1024,512]{1,0:T(8,128)S(1)}, bf16[512,1024]{1,0:T(8,128)(2,1)S(1)}) custom-call(bf16[3,1024,256]{2,1,0:T(8,128)(2,1)S(1)} %get-tuple-element.40.a_ref, bf16[3,512,256]{2,1,0:T(8,128)(2,1)S(1)} %collective-permute-done.1.b_ref, f32[1024,128]{1,0:T(8,128)S(1)} %get-tuple-element.31.ln_ref), custom_call_target="tpu_custom_call" | custom-call | flops 2415919104 | bytes 6291456 | tf_op jit(solution)/shard_map/far/pallas_call | solution.py:226
  35.7 0.0 collective-permute-done.b_ref
  35.7 0.1 collective-permute-start.3
  35.8 1.7 %collective-permute-start.5 = (bf16[512,1024]{1,0:T(8,128)(2,1)S(1)}, bf16[512,1024]{1,0:T(8,128)(2,1)S(1)}, u32[]{:S(2)}, u32[]{:S(2)}) collective-permute-start(bf16[512,1024]{1,0:T(8,128)(2,1)S(1)} %get-tuple-element.47), channel_id=1, source_target_pairs={{0,2},{1,127},{2,4},{3,1},{4,6},{5,3},{6,8},{7,5},{8,10},{9,7},{10... | collective-permute-start | bytes 3145736 | tf_op jit(solution)/shard_map/ppermute | solution.py:410
  37.5 12.3 %far.3 = (f32[1024,512]{1,0:T(8,128)S(1)}, bf16[512,1024]{1,0:T(8,128)(2,1)S(1)}) custom-call(bf16[3,1024,256]{2,1,0:T(8,128)(2,1)S(1)} %get-tuple-element.40.a_ref, bf16[3,512,256]{2,1,0:T(8,128)(2,1)S(1)} %collective-permute-done.b_ref, f32[1024,128]{1,0:T(8,128)S(1)} %get-tuple-element.31.ln_ref), custom_call_target="tpu_custom_call" | custom-call | flops 2415919104 | bytes 6291456 | tf_op jit(solution)/shard_map/far/pallas_call | solution.py:226
  49.8 0.1 collective-permute-start.6
  49.9 0.0 collective-permute-done.2.refs_0_
  49.9 0.0 collective-permute-done.3.refs_1_
  49.9 13.3 %near.1 = (f32[2,512,512]{2,1,0:T(8,128)S(1)}, bf16[2,512,512]{2,1,0:T(8,128)(2,1)S(1)}) custom-call(bf16[3,1024,256]{2,1,0:T(8,128)(2,1)S(1)} %get-tuple-element.40.a_ref, f32[1024,128]{1,0:T(8,128)S(1)} %get-tuple-element.31.ln_ref, bf16[3,512,256]{2,1,0:T(8,128)(2,1)S(1)} %collective-permute-done.2.refs_0_, ...), custom_call_target="tpu_custom_call" | custom-call | flops 2415919104 | bytes 6291456 | tf_op jit(solution)/shard_map/near/pallas_call | solution.py:294
  63.2 4.8 %collective-permute-start.7 = (bf16[2,512,512]{2,1,0:T(8,128)(2,1)S(1)}, bf16[2,512,512]{2,1,0:T(8,128)(2,1)S(1)}, u32[]{:S(2)}, u32[]{:S(2)}) collective-permute-start(bf16[2,512,512]{2,1,0:T(8,128)(2,1)S(1)} %get-tuple-element.49), channel_id=1, source_target_pairs={{0,127},{1,2},{2,1},{3,4},{4,3},{5,6},{6,5},{7,8},{8,7},{9,10},{10... | collective-permute-start | bytes 3145736 | tf_op jit(solution)/shard_map/ppermute | solution.py:416
  68.0 0.0 collective-permute-done.4.refs_0_
  68.1 13.1 %mate.1 = (f32[2,512,512]{2,1,0:T(8,128)S(1)}, bf16[2,512,512]{2,1,0:T(8,128)(2,1)S(1)}) custom-call(bf16[3,1024,256]{2,1,0:T(8,128)(2,1)S(1)} %get-tuple-element.40.a_ref, f32[1024,128]{1,0:T(8,128)S(1)} %get-tuple-element.31.ln_ref, bf16[3,1024,256]{2,1,0:T(8,128)(2,1)S(1)} %collective-permute-done.4.refs_0_), custom_call_target="tpu_custom_call" | custom-call | flops 2415919104 | bytes 6291456 | tf_op jit(solution)/shard_map/mate/pallas_call | solution.py:294
  81.2 0.4 collective-permute-start.8
  81.5 0.0 collective-permute-done.5.far0_y
  81.5 0.0 collective-permute-done.6.far1_y
  81.6 1.4 %collective-permute-done.7.near_y = bf16[2,512,512]{2,1,0:T(8,128)(2,1)S(1)} collective-permute-done((bf16[2,512,512]{2,1,0:T(8,128)(2,1)S(1)}, bf16[2,512,512]{2,1,0:T(8,128)(2,1)S(1)}, u32[]{:S(2)}, u32[]{:S(2)}) %collective-permute-start.7) | collective-permute-done | bytes 1048608 | tf_op jit(solution)/shard_map/ppermute | solution.py:416
  83.0 1.1 %collective-permute-done.8.mate_y = bf16[2,512,512]{2,1,0:T(8,128)(2,1)S(1)} collective-permute-done((bf16[2,512,512]{2,1,0:T(8,128)(2,1)S(1)}, bf16[2,512,512]{2,1,0:T(8,128)(2,1)S(1)}, u32[]{:S(2)}, u32[]{:S(2)}) %collective-permute-start.8) | collective-permute-done | bytes 1048608 | tf_op jit(solution)/shard_map/ppermute | solution.py:418
  84.1 10.9 %finish.1 = f32[5,1024,1024]{2,1,0:T(8,128)} custom-call(bf16[3,1024,256]{2,1,0:T(8,128)(2,1)S(1)} %get-tuple-element.40.a_ref, f32[1024,128]{1,0:T(8,128)S(1)} %get-tuple-element.31.ln_ref, f32[768,768]{1,0:T(8,128)S(1)} %get-tuple-element.41.diag, f32[768,768]{1,0:T(8,128)S(1)} %get-tuple-element.42.turned, f32[1024,512]{1,0:T(8,128)S(1)} %get-tuple-element.43.far0, ...), custom_call_target="tpu_custom_call" | custom-call | flops 2415919104 | bytes 6291456 | tf_op jit(solution)/shard_map/finish/pallas_call | solution.py:369
Async XLA Ops:
  0.0 1.4 %copy-start = (bf16[3,1024,256]{2,1,0:T(8,128)(2,1)S(1)}, bf16[3,1024,256]{2,1,0:T(8,128)(2,1)}, u32[]{:S(2)}) copy-start(bf16[3,1024,256]{2,1,0:T(8,128)(2,1)} %x_ref.1) | copy-start | bytes 4718596
  3.3 19.4 %collective-permute-start.1 = (bf16[3,512,256]{2,1,0:T(8,128)(2,1)S(1)}, bf16[3,512,256]{2,1,0:T(8,128)(2,1)S(1)}, u32[]{:S(2)}, u32[]{:S(2)}) collective-permute-start(bf16[3,512,256]{2,1,0:T(8,128)(2,1)S(1)} %get-tuple-element.30), channel_id=1, source_target_pairs={{2,0},{127,1},{4,2},{1,3},{6,4},{3,5},{8,6},{5,7},{10,8},{7,9},{12... | collective-permute-start | bytes 2359304 | tf_op jit(solution)/shard_map/ppermute | solution.py:400
  12.2 23.6 %collective-permute-start = (bf16[3,512,256]{2,1,0:T(8,128)(2,1)S(1)}, bf16[3,512,256]{2,1,0:T(8,128)(2,1)S(1)}, u32[]{:S(2)}, u32[]{:S(2)}) collective-permute-start(bf16[3,512,256]{2,1,0:T(8,128)(2,1)S(1)} %get-tuple-element.29), channel_id=1, source_target_pairs={{2,0},{127,1},{4,2},{1,3},{6,4},{3,5},{8,6},{5,7},{10,8},{7,9},{12... | collective-permute-start | bytes 2359304 | tf_op jit(solution)/shard_map/ppermute | solution.py:401
  12.6 55.5 %collective-permute-start.4 = (bf16[3,1024,256]{2,1,0:T(8,128)(2,1)S(1)}, bf16[3,1024,256]{2,1,0:T(8,128)(2,1)S(1)}, u32[]{:S(2)}, u32[]{:S(2)}) collective-permute-start(bf16[3,1024,256]{2,1,0:T(8,128)(2,1)S(1)} %get-tuple-element.40.a_ref), channel_id=1, source_target_pairs={{0,1},{1,0},{2,3},{3,2},{4,5},{5,4},{6,7},{7,6},{8,9},{9,8},{10,11... | collective-permute-start | bytes 4718600 | tf_op jit(solution)/shard_map/ppermute | solution.py:402
  22.8 27.2 %collective-permute-start.2 = (bf16[3,512,256]{2,1,0:T(8,128)(2,1)S(1)}, bf16[3,512,256]{2,1,0:T(8,128)(2,1)S(1)}, u32[]{:S(2)}, u32[]{:S(2)}) collective-permute-start(bf16[3,512,256]{2,1,0:T(8,128)(2,1)S(1)} %collective-permute-done.1.b_ref), channel_id=1, source_target_pairs={{0,1},{1,0},{2,3},{3,2},{4,5},{5,4},{6,7},{7,6},{8,9},{9,8},{10,11... | collective-permute-start | bytes 2359304 | tf_op jit(solution)/shard_map/ppermute | solution.py:406
  35.7 14.2 %collective-permute-start.3 = (bf16[3,512,256]{2,1,0:T(8,128)(2,1)S(1)}, bf16[3,512,256]{2,1,0:T(8,128)(2,1)S(1)}, u32[]{:S(2)}, u32[]{:S(2)}) collective-permute-start(bf16[3,512,256]{2,1,0:T(8,128)(2,1)S(1)} %collective-permute-done.b_ref), channel_id=1, source_target_pairs={{0,1},{1,0},{2,3},{3,2},{4,5},{5,4},{6,7},{7,6},{8,9},{9,8},{10,11... | collective-permute-start | bytes 2359304 | tf_op jit(solution)/shard_map/ppermute | solution.py:409
  35.8 45.7 %collective-permute-start.5 = (bf16[512,1024]{1,0:T(8,128)(2,1)S(1)}, bf16[512,1024]{1,0:T(8,128)(2,1)S(1)}, u32[]{:S(2)}, u32[]{:S(2)}) collective-permute-start(bf16[512,1024]{1,0:T(8,128)(2,1)S(1)} %get-tuple-element.47), channel_id=1, source_target_pairs={{0,2},{1,127},{2,4},{3,1},{4,6},{5,3},{6,8},{7,5},{8,10},{9,7},{10... | collective-permute-start | bytes 3145736 | tf_op jit(solution)/shard_map/ppermute | solution.py:410
  49.8 31.7 %collective-permute-start.6 = (bf16[512,1024]{1,0:T(8,128)(2,1)S(1)}, bf16[512,1024]{1,0:T(8,128)(2,1)S(1)}, u32[]{:S(2)}, u32[]{:S(2)}) collective-permute-start(bf16[512,1024]{1,0:T(8,128)(2,1)S(1)} %get-tuple-element.48), channel_id=1, source_target_pairs={{0,2},{1,127},{2,4},{3,1},{4,6},{5,3},{6,8},{7,5},{8,10},{9,7},{10... | collective-permute-start | bytes 3145736 | tf_op jit(solution)/shard_map/ppermute | solution.py:413
  63.2 19.7 %collective-permute-start.7 = (bf16[2,512,512]{2,1,0:T(8,128)(2,1)S(1)}, bf16[2,512,512]{2,1,0:T(8,128)(2,1)S(1)}, u32[]{:S(2)}, u32[]{:S(2)}) collective-permute-start(bf16[2,512,512]{2,1,0:T(8,128)(2,1)S(1)} %get-tuple-element.49), channel_id=1, source_target_pairs={{0,127},{1,2},{2,1},{3,4},{4,3},{5,6},{6,5},{7,8},{8,7},{9,10},{10... | collective-permute-start | bytes 3145736 | tf_op jit(solution)/shard_map/ppermute | solution.py:416
  81.2 2.9 %collective-permute-start.8 = (bf16[2,512,512]{2,1,0:T(8,128)(2,1)S(1)}, bf16[2,512,512]{2,1,0:T(8,128)(2,1)S(1)}, u32[]{:S(2)}, u32[]{:S(2)}) collective-permute-start(bf16[2,512,512]{2,1,0:T(8,128)(2,1)S(1)} %get-tuple-element.50), channel_id=1, source_target_pairs={{0,1},{1,0},{2,3},{3,2},{4,5},{5,4},{6,7},{7,6},{8,9},{9,8},{10,11... | collective-permute-start | bytes 3145736 | tf_op jit(solution)/shard_map/ppermute | solution.py:418

commit v4 on v0

v4 whole, which is shorter than its diff:
```python
import functools

import jax
import jax.numpy as jnp
from jax import lax
from jax.experimental import pallas as pl
from jax.experimental.pallas import tpu as pltpu
from jax.sharding import PartitionSpec as P

NEWTON = 8
FR = 1024
ATOMS = 256
ROWS = 128
COLS = 256
STEP = 16
HALF = FR // 2
VMEM = pl.BlockSpec(memory_space=pltpu.VMEM)
ANY = pl.BlockSpec(memory_space=pl.ANY)
VMEM_LIMIT = 14 << 20


def aligned(index, size):
    return pl.ds(pl.multiple_of(index, size), size)


def norm_rows(total):
    norms = jnp.broadcast_to(0.5 * jnp.sum(total, axis=1, keepdims=True), (128, 128))
    return norms, norms.T[0:8, :]


def centre(x_ref, all_ref, ln_ref, rn_ref, first, count):
    @pl.loop(first // 128, (first + count) // 128)
    def _(i):
        rows = aligned(i * 128, 128)
        total = None
        for k in range(3):
            values = x_ref[k, rows, :].astype(jnp.float32)
            mean = jnp.sum(values, axis=1, keepdims=True) * (1.0 / ATOMS)
            centred = (values - mean).astype(jnp.bfloat16)
            all_ref[k, rows, :] = centred
            back = centred.astype(jnp.float32)
            total = back * back if total is None else total + back * back
        ln_ref[rows, :], rn_ref[:, rows] = norm_rows(total)


def row_norms(all_ref, rn_ref, first, count):
    @pl.loop(0, count // 128)
    def _(i):
        frames = aligned(first + i * 128, 128)
        total = None
        for k in range(3):
            values = all_ref[k, frames, :].astype(jnp.float32)
            total = values * values if total is None else total + values * values
        rn_ref[:, frames] = norm_rows(total)[1]


def invariants(entry):
    (a, b, c), (d, f, g), (h, i, j) = entry
    first = a * a + b * b + c * c
    others = (d * d + f * f + g * g) + (h * h + i * i + j * j)
    p = f * j - g * i
    q = g * h - d * j
    r = d * i - f * h
    det = a * p + b * q + c * r
    one = a * d + b * f + c * g
    two = a * h + b * i + c * j
    minors = (first * others - one * one - two * two) + (p * p + q * q + r * r)
    return first + others, det + det, minors


def deviations(entry, left, right):
    n, f, m = invariants(entry)
    start = left + right
    top = start
    for _ in range(NEWTON):
        h = top * top - n
        top = ((h * 0.75 + n) * h + m) * pltpu.reciprocal(top * h - f, approx=True)
    return (start - top) * (2.0 / ATOMS)


def covariance_pieces(all_ref, row, col, cov_ref):
    left = all_ref[:, aligned(row, ROWS), :].reshape(3 * ROWS, ATOMS)
    for k in range(3):
        right = all_ref[k, aligned(col, COLS), :]
        block = lax.dot_general(
            left, right, (((1,), (1,)), ((), ())), preferred_element_type=jnp.float32
        )
        cov_ref[:, k] = block.reshape(3, ROWS, COLS)
        yield


def value_pieces(cov_ref, ln_ref, rn_ref, row, col):
    for r in range(0, ROWS, STEP):
        entry = [[cov_ref[k, l, r : r + STEP, :] for l in range(3)] for k in range(3)]
        left = ln_ref[aligned(row + r, STEP), :]
        left = jnp.concatenate([left] * (COLS // 128), axis=1)
        right = rn_ref[:, aligned(col, COLS)]
        right = jnp.concatenate([right] * (STEP // 8), axis=0)
        yield r, deviations(entry, left, right)


def encode(values):
    square = values * values
    return (square * square).astype(jnp.bfloat16)


def other_half(half, flip):
    return half + flip - 2 * half * flip


def mate_place(parity):
    return 3 - 2 * parity, parity


def near_place(parity):
    return 1 + 2 * parity, 1 - parity


OWN, FAR, NEAR, MATE = range(0, 4 * FR, FR)
FAR_AT, NEAR_AT, MATE_AT, LAST_AT, STEPS = 12, 44, 60, 76, 84
CHUNKS = FR // COLS


def step_place(s, parity):
    early = jnp.where(s >= 2, 1, 0) + jnp.where(s >= 6, 1, 0)
    is_last = s >= LAST_AT
    row = jnp.where(is_last, s - LAST_AT, s - early * (early + 1))
    col = jnp.where(is_last, 3 * COLS, early * COLS)

    far = s - FAR_AT
    is_far = s >= FAR_AT
    row = jnp.where(is_far & (s < NEAR_AT), far & 7, row)
    col = jnp.where(is_far & (s < NEAR_AT), FAR + (far >> 3) * COLS, col)

    inner = (s - NEAR_AT) & 15
    is_mate = s >= MATE_AT
    flip = jnp.where(is_mate, parity, 1 - parity)
    half = inner >> 3
    is_quarter = (s >= NEAR_AT) & (s < LAST_AT)
    row = jnp.where(is_quarter, half * (HALF // ROWS) + (inner & 3), row)
    base = jnp.where(is_mate, MATE, NEAR) + ((inner >> 2) & 1) * COLS
    col = jnp.where(is_quarter, base + other_half(half, flip) * HALF, col)
    return row * ROWS, col


def main_kernel(
    count, x_ref, tile, y_ref, got_ref, all_ref, ln_ref, rn_ref, cov0, cov1, old0, old1,
    far_sems, near_sems, mate_sems, far_y_sems, near_y_sems, mate_y_sems,
):
    me = lax.axis_index("frames")
    parity = lax.rem(me, 2)
    way = 1 - 2 * parity
    far = lax.rem(me + 2 * way + count, count)
    far_back = lax.rem(me - 2 * way + count, count)
    near = lax.rem(me - way + count, count)
    mate = me + way

    barrier = pltpu.get_barrier_semaphore()
    for device in (far, far_back, near, mate):
        pl.semaphore_signal(
            barrier, inc=1, device_id=(device,), device_id_type=pl.DeviceIdType.MESH
        )

    def remote(source, target, sems, i, device):
        return pltpu.make_async_remote_copy(
            src_ref=source,
            dst_ref=target,
            send_sem=sems.at[0, i],
            recv_sem=sems.at[1, i],
            device_id=(device,),
            device_id_type=pl.DeviceIdType.MESH,
        )

    def frames(block, i):
        return all_ref.at[:, aligned(block + i * COLS, COLS)]

    def far_copy(i):
        return remote(frames(OWN, i), frames(FAR, i), far_sems, i, far_back)

    def near_copy(i):
        return remote(frames(FAR, i), frames(NEAR, i), near_sems, i, mate)

    def mate_copy(i):
        return remote(frames(OWN, i), frames(MATE, i), mate_sems, i, mate)

    def far_y_copy(i):
        rows = aligned(i * COLS, COLS)
        source = y_ref.at[aligned(FAR + i * COLS, COLS)]
        return remote(source, got_ref.at[rows], far_y_sems, i, far)

    def quarter_y_copy(block, flip, i, sems, device):
        half = i >> 1
        row = block + other_half(half, flip) * HALF + (i & 1) * COLS
        cols = aligned(half * HALF, HALF)
        source = y_ref.at[aligned(row, COLS), cols]
        return remote(source, got_ref.at[aligned(row - FAR, COLS), cols], sems, i, device)

    def near_y_copy(i):
        return quarter_y_copy(NEAR, 1 - parity, i, near_y_sems, near)

    def mate_y_copy(i):
        return quarter_y_copy(MATE, parity, i, mate_y_sems, mate)

    for i in range(CHUNKS):
        centre(x_ref, all_ref, ln_ref, rn_ref, i * COLS, COLS)
        if i == 0:
            pl.semaphore_wait(barrier, 4)
        far_copy(i).start()
        mate_copy(i).start()

    def take(group):
        @pl.when((group >= 2) & (group <= 8) & ((group & 1) == 0))
        def _():
            i = (group - 2) >> 1
            far_copy(i).wait_recv()
            near_copy(i).start()
            row_norms(all_ref, rn_ref, FAR + i * COLS, COLS)

        @pl.when(group == NEAR_AT // 4 - 1)
        def _():
            for i in range(CHUNKS):
                near_copy(i).wait_recv()
            row_norms(all_ref, rn_ref, NEAR, FR)

        @pl.when(group == MATE_AT // 4 - 1)
        def _():
            for i in range(CHUNKS):
                mate_copy(i).wait_recv()
            row_norms(all_ref, rn_ref, MATE, FR)

    def give(group):
        @pl.when((group >= 5) & (group <= 11) & ((group & 1) == 1))
        def _():
            far_y_copy((group - 5) >> 1).start()

        @pl.when((group > NEAR_AT // 4) & (group <= MATE_AT // 4))
        def _():
            near_y_copy(group - NEAR_AT // 4 - 1).start()

        @pl.when((group > MATE_AT // 4) & (group <= LAST_AT // 4))
        def _():
            mate_y_copy(group - MATE_AT // 4 - 1).start()

    def turn(row, col, old):
        y_ref[aligned(col, COLS), aligned(row, ROWS)] = old[...].T

    def step(places, cov, cov_next, old, old_last):
        (row_last, col_last), (row, col), (row_next, col_next) = places
        products = covariance_pieces(all_ref, row_next, col_next, cov_next)
        for piece, (r, values) in enumerate(value_pieces(cov, ln_ref, rn_ref, row, col)):
            tile[aligned(row + r, STEP), aligned(col, COLS)] = values
            old[r : r + STEP, :] = encode(values)
            if piece in (0, 2, 4):
                next(products)
        turn(row_last, col_last, old_last)

    first = step_place(jnp.int32(0), parity)
    for _ in covariance_pieces(all_ref, *first, cov0):
        pass
    old1[...] = jnp.zeros_like(old1)

    def body(s, places):
        @pl.when((s & 3) == 0)
        def _():
            take(s >> 2)

        @pl.when((s & 3) == 1)
        def _():
            give(s >> 2)

        @pl.when((s & 1) == 0)
        def _():
            step(places, cov0, cov1, old0, old1)

        @pl.when((s & 1) == 1)
        def _():
            step(places, cov1, cov0, old1, old0)

        return places[1], places[2], step_place(jnp.minimum(s + 2, STEPS - 1), parity)

    start = (first, first, step_place(jnp.int32(1), parity))
    places = lax.fori_loop(0, STEPS, body, start)
    turn(*places[0], old1)

    for i in range(CHUNKS):
        far_copy(i).wait_send()
        mate_copy(i).wait_send()
        near_copy(i).wait_send()
        far_y_copy(i).wait()
        near_y_copy(i).wait()
        mate_y_copy(i).wait()


def main(coords, count):
    pair = pltpu.SemaphoreType.DMA((2, CHUNKS))
    return pl.pallas_call(
        functools.partial(main_kernel, count),
        in_specs=[VMEM],
        out_specs=[VMEM] * 3,
        out_shape=[
            jax.ShapeDtypeStruct((FR, 4 * FR), jnp.float32),
            jax.ShapeDtypeStruct((4 * FR, FR), jnp.bfloat16),
            jax.ShapeDtypeStruct((3 * FR, FR), jnp.bfloat16),
        ],
        scratch_shapes=[
            pltpu.VMEM((3, 4 * FR, ATOMS), jnp.bfloat16),
            pltpu.VMEM((FR, 128), jnp.float32),
            pltpu.VMEM((8, 4 * FR), jnp.float32),
            pltpu.VMEM((3, 3, ROWS, COLS), jnp.float32),
            pltpu.VMEM((3, 3, ROWS, COLS), jnp.float32),
            pltpu.VMEM((ROWS, COLS), jnp.bfloat16),
            pltpu.VMEM((ROWS, COLS), jnp.bfloat16),
            *[pair] * 6,
        ],
        compiler_params=pltpu.CompilerParams(
            collective_id=0, has_side_effects=True, vmem_limit_bytes=VMEM_LIMIT
        ),
        cost_estimate=pl.CostEstimate(
            flops=45 * FR * FR * ATOMS, bytes_accessed=32 << 20, transcendentals=0
        ),
        name="deviations",
    )(coords)


def decode(values):
    return lax.rsqrt(lax.rsqrt(values.astype(jnp.float32)))


def finish_kernel(tile, y_ref, got_ref, out_ref, far_tile, near_tile, mate_tile, low_tile, sem):
    parity = lax.rem(lax.axis_index("frames"), 2)
    copies = []

    def copy(source, slot, rows, cols):
        copies.append(
            pltpu.make_async_copy(source, out_ref.at[slot, rows, cols], sem.at[len(copies)])
        )
        copies[-1].start()

    def half(i, base=0):
        return pl.ds(pl.multiple_of(base + i * HALF, HALF), HALF)

    both = pl.ds(0, FR)
    quarters = ((NEAR, near_place(parity), near_tile), (MATE, mate_place(parity), mate_tile))
    copy(tile.at[:, pl.ds(FAR, FR)], 4 * (1 - parity), both, both)
    for block, (slot, flip), _ in quarters:
        for i in range(2):
            other = other_half(i, flip)
            copy(tile.at[half(i), half(other, block)], slot, half(i), half(other))
    for c in range(CHUNKS):
        rows, cols = pl.ds(0, (c + 1) * COLS), pl.ds(c * COLS, COLS)
        copy(tile.at[rows, cols], 2, rows, cols)

    for i in range(CHUNKS):
        rows = pl.ds(i * COLS, COLS)
        far_tile[rows, :] = decode(got_ref[rows, :])
        copy(far_tile.at[rows], 4 * parity, rows, both)
    for block, (slot, flip), tiles in quarters:
        for i in range(2):
            own = other_half(i, 1 - flip)
            tiles[i] = decode(got_ref[half(own, block - FAR), half(i)])
            copy(tiles.at[i], slot, half(own), half(i))
    for c in range(1, CHUNKS):
        rows, cols = pl.ds(c * COLS, COLS), pl.ds(0, c * COLS)
        low_tile[rows, cols] = decode(y_ref[rows, cols])
        copy(low_tile.at[rows, cols], 2, rows, cols)
    for each in copies:
        each.wait()


def finish(tile, y, got):
    return pl.pallas_call(
        finish_kernel,
        in_specs=[ANY, VMEM, VMEM],
        out_specs=ANY,
        out_shape=jax.ShapeDtypeStruct((5, FR, FR), jnp.float32),
        scratch_shapes=[
            pltpu.VMEM((FR, FR), jnp.float32),
            pltpu.VMEM((2, HALF, HALF), jnp.float32),
            pltpu.VMEM((2, HALF, HALF), jnp.float32),
            pltpu.VMEM((FR, FR), jnp.float32),
            pltpu.SemaphoreType.DMA((32,)),
        ],
        compiler_params=pltpu.CompilerParams(vmem_limit_bytes=VMEM_LIMIT),
        name="finish",
    )(tile, y, got)


def on_device(coords):
    out = finish(*main(coords, lax.axis_size("frames")))
    return jnp.transpose(out, (1, 0, 2))


def solution(mesh):
    return jax.shard_map(
        on_device,
        mesh=mesh,
        in_specs=(P(None, "frames", None),),
        out_specs=P("frames", None, None),
        check_vma=False,
    )
```

time: 351 us -> 87.8 us (0.25)
  other arithmetic: 171 us -> 0 us
  waiting for transfers between devices: 96.4 us -> 0 us
  Pallas kernels: 0 us -> 85.8 us
  matrix products: 44.4 us -> 0 us
  local copies, waits for them, and re-layouts: 22 us -> 1.41 us
  starting transfers between devices: 16.2 us -> 0 us
    ppermute x4 -> x0, waiting for transfers between devices: 96.4 us -> none  [passed_along(): return lax.ppermute(value, axis, pairs)]
    pallas_call x0 -> x2, Pallas kernels: none -> 85.8 us  [the longest x1 78.4 us: main(): pl.pallas_call(functools.partial(main_kernel, count), in_specs=[VMEM], ou...]
    transpose x2 -> x0, other arithmetic: 66.7 us -> none  [on_device(): tiles[-step] = passed_along(jnp.transpose(tiles[step]), 'frames', step)]
    unnamed x2 -> x0, other arithmetic: 66 us -> none
    dot_general x3 -> x0, matrix products: 44.4 us -> none  [deviation_tile(): lax.dot_general(left.reshape(3 * rows, width), right.reshape(3 * cols, wi...]
    another operation x1 -> x0, other arithmetic: 33.7 us -> none  [on_device(): jnp.stack([tiles[offset - BAND] for offset in range(2 * BAND + 1)], axis=1)]
    ppermute x4 -> x0, starting transfers between devices: 16.2 us -> none  [passed_along(): return lax.ppermute(value, axis, pairs)]
    another operation x2 -> x0, local copies, waits for them, and re-layouts: 10.7 us -> none  [on_device(): jnp.stack([tiles[offset - BAND] for offset in range(2 * BAND + 1)], axis=1)]
  transfers between devices with their start and end apart: 4 -> 0, of which waited for: 2 -> 0; matrix products, arithmetic and copies ran while one was open for 33% -> 0% of each run, Pallas kernels for 0% -> 0%
where the time goes in v4:
time: 87.8 us; the launch traced here: 87.2 us
  Pallas kernels  85.8 us (98%)
  local copies, waits for them, and re-layouts  1.41 us (2%)
    pallas_call x1, Pallas kernels, main(): pl.pallas_call(functools.partial(main_kernel, count), in_specs=[VMEM], ou...  78.4 us
    pallas_call x1, Pallas kernels, finish(): pl.pallas_call(finish_kernel, in_specs=[ANY, VMEM, VMEM], out_specs=ANY,...  7.36 us

profile of v4, /device:TPU:0, one launch (start us, length us, event | category | flops | bytes accessed | tf_op | source)
XLA Modules:
  0.0 87.2 jit_solution(3014081286059526467)
XLA Ops:
  0.0 0.0 copy-start
  0.0 1.4 %copy-done = bf16[3,1024,256]{2,1,0:T(8,128)(2,1)S(1)} copy-done((bf16[3,1024,256]{2,1,0:T(8,128)(2,1)S(1)}, bf16[3,1024,256]{2,1,0:T(8,128)(2,1)}, u32[]{:S(2)}) %copy-start) | copy-done | bytes 1572888
  1.4 78.4 %deviations.1 = (f32[1024,4096]{1,0:T(8,128)S(1)}, bf16[4096,1024]{1,0:T(8,128)(2,1)S(1)}, bf16[3072,1024]{1,0:T(8,128)(2,1)S(1)}) custom-call(bf16[3,1024,256]{2,1,0:T(8,128)(2,1)S(1)} %copy-done), custom_call_target="tpu_custom_call" | custom-call | flops 12079595520 | bytes 33554432 | tf_op jit(solution)/shard_map/deviations/pallas_call | solution.py:296
  79.8 7.4 %finish.1 = f32[5,1024,1024]{2,1,0:T(8,128)} custom-call(f32[1024,4096]{1,0:T(8,128)S(1)} %get-tuple-element.8.tile, bf16[4096,1024]{1,0:T(8,128)(2,1)S(1)} %get-tuple-element.9.y_ref, bf16[3072,1024]{1,0:T(8,128)(2,1)S(1)} %get-tuple-element.10.got_ref), custom_call_target="tpu_custom_call" | custom-call | tf_op jit(solution)/shard_map/finish/pallas_call | solution.py:371
Async XLA Ops:
  0.0 1.4 %copy-start = (bf16[3,1024,256]{2,1,0:T(8,128)(2,1)S(1)}, bf16[3,1024,256]{2,1,0:T(8,128)(2,1)}, u32[]{:S(2)}) copy-start(bf16[3,1024,256]{2,1,0:T(8,128)(2,1)} %x_ref.1) | copy-start | bytes 4718596

commit v5 on v4

--- a/solution.py
+++ b/solution.py
@@ -10,48 +10,38 @@
 NEWTON = 8
 FR = 1024
 ATOMS = 256
-ROWS = 128
+ROWS = 256
 COLS = 256
 STEP = 16
 HALF = FR // 2
 VMEM = pl.BlockSpec(memory_space=pltpu.VMEM)
 ANY = pl.BlockSpec(memory_space=pl.ANY)
-VMEM_LIMIT = 14 << 20
+MAIN_LIMIT = 15 << 20
+FINISH_LIMIT = 13 << 20
 
 
 def aligned(index, size):
     return pl.ds(pl.multiple_of(index, size), size)
 
 
-def norm_rows(total):
-    norms = jnp.broadcast_to(0.5 * jnp.sum(total, axis=1, keepdims=True), (128, 128))
-    return norms, norms.T[0:8, :]
-
-
-def centre(x_ref, all_ref, ln_ref, rn_ref, first, count):
-    @pl.loop(first // 128, (first + count) // 128)
+def centre(x_ref, all_ref, ln_ref, rn_ref):
+    weights = jnp.full((ATOMS, 128), 1.0 / ATOMS, jnp.bfloat16)
+
+    @pl.loop(0, FR // 128)
     def _(i):
         rows = aligned(i * 128, 128)
         total = None
         for k in range(3):
-            values = x_ref[k, rows, :].astype(jnp.float32)
-            mean = jnp.sum(values, axis=1, keepdims=True) * (1.0 / ATOMS)
-            centred = (values - mean).astype(jnp.bfloat16)
+            values = x_ref[k, rows, :]
+            mean = jnp.dot(values, weights, preferred_element_type=jnp.float32)
+            mean = jnp.concatenate([mean] * (ATOMS // 128), axis=1)
+            centred = (values.astype(jnp.float32) - mean).astype(jnp.bfloat16)
             all_ref[k, rows, :] = centred
             back = centred.astype(jnp.float32)
             total = back * back if total is None else total + back * back
-        ln_ref[rows, :], rn_ref[:, rows] = norm_rows(total)
-
-
-def row_norms(all_ref, rn_ref, first, count):
-    @pl.loop(0, count // 128)
-    def _(i):
-        frames = aligned(first + i * 128, 128)
-        total = None
-        for k in range(3):
-            values = all_ref[k, frames, :].astype(jnp.float32)
-            total = values * values if total is None else total + values * values
-        rn_ref[:, frames] = norm_rows(total)[1]
+        norms = jnp.broadcast_to(0.5 * jnp.sum(total, axis=1, keepdims=True), (128, 128))
+        ln_ref[rows, :] = norms
+        rn_ref[:, rows] = norms.T[0:8, :]
 
 
 def invariants(entry):
@@ -117,35 +107,39 @@
 
 
 OWN, FAR, NEAR, MATE = range(0, 4 * FR, FR)
-FAR_AT, NEAR_AT, MATE_AT, LAST_AT, STEPS = 12, 44, 60, 76, 84
+FAR_AT, NEAR_AT, MATE_AT, GROUPS = 5, 13, 17, 21
+SPLIT = 2
 CHUNKS = FR // COLS
 
 
-def step_place(s, parity):
-    early = jnp.where(s >= 2, 1, 0) + jnp.where(s >= 6, 1, 0)
-    is_last = s >= LAST_AT
-    row = jnp.where(is_last, s - LAST_AT, s - early * (early + 1))
-    col = jnp.where(is_last, 3 * COLS, early * COLS)
-
-    far = s - FAR_AT
-    is_far = s >= FAR_AT
-    row = jnp.where(is_far & (s < NEAR_AT), far & 7, row)
-    col = jnp.where(is_far & (s < NEAR_AT), FAR + (far >> 3) * COLS, col)
-
-    inner = (s - NEAR_AT) & 15
-    is_mate = s >= MATE_AT
+def group_place(g, parity):
+    row = jnp.where(g == SPLIT, 2, jnp.where(g == FAR_AT - 1, 2, 0))
+    col = jnp.where(g == 0, 1, jnp.where(g <= SPLIT, 2, 3)) * COLS
+
+    far = g - FAR_AT
+    is_far = g >= FAR_AT
+    row = jnp.where(is_far, (far & 1) * 2, row)
+    col = jnp.where(is_far, FAR + (far >> 1) * COLS, col)
+
+    inner = (g - NEAR_AT) & 3
+    is_quarter, is_mate = g >= NEAR_AT, g >= MATE_AT
     flip = jnp.where(is_mate, parity, 1 - parity)
-    half = inner >> 3
-    is_quarter = (s >= NEAR_AT) & (s < LAST_AT)
-    row = jnp.where(is_quarter, half * (HALF // ROWS) + (inner & 3), row)
-    base = jnp.where(is_mate, MATE, NEAR) + ((inner >> 2) & 1) * COLS
+    half = inner >> 1
+    row = jnp.where(is_quarter, half * 2, row)
+    base = jnp.where(is_mate, MATE, NEAR) + (inner & 1) * COLS
     col = jnp.where(is_quarter, base + other_half(half, flip) * HALF, col)
     return row * ROWS, col
+
+
+def second_place(g, first):
+    row, col = first
+    return jnp.where(g == SPLIT, 0, row + ROWS), jnp.where(g == SPLIT, 0, col)
 
 
 def main_kernel(
     count, x_ref, tile, y_ref, got_ref, all_ref, ln_ref, rn_ref, cov0, cov1, old0, old1,
     far_sems, near_sems, mate_sems, far_y_sems, near_y_sems, mate_y_sems,
+    far_n_sems, near_n_sems, mate_n_sems,
 ):
     me = lax.axis_index("frames")
     parity = lax.rem(me, 2)
@@ -174,14 +168,26 @@
     def frames(block, i):
         return all_ref.at[:, aligned(block + i * COLS, COLS)]
 
-    def far_copy(i):
-        return remote(frames(OWN, i), frames(FAR, i), far_sems, i, far_back)
-
-    def near_copy(i):
-        return remote(frames(FAR, i), frames(NEAR, i), near_sems, i, mate)
-
-    def mate_copy(i):
-        return remote(frames(OWN, i), frames(MATE, i), mate_sems, i, mate)
+    def norms(block, i):
+        return rn_ref.at[:, aligned(block + i * COLS, COLS)]
+
+    def far_copies(i):
+        return (
+            remote(frames(OWN, i), frames(FAR, i), far_sems, i, far_back),
+            remote(norms(OWN, i), norms(FAR, i), far_n_sems, i, far_back),
+        )
+
+    def near_copies(i):
+        return (
+            remote(frames(FAR, i), frames(NEAR, i), near_sems, i, mate),
+            remote(norms(FAR, i), norms(NEAR, i), near_n_sems, i, mate),
+        )
+
+    def mate_copies(i):
+        return (
+            remote(frames(OWN, i), frames(MATE, i), mate_sems, i, mate),
+            remote(norms(OWN, i), norms(MATE, i), mate_n_sems, i, mate),
+        )
 
     def far_y_copy(i):
         rows = aligned(i * COLS, COLS)
@@ -201,91 +207,86 @@
     def mate_y_copy(i):
         return quarter_y_copy(MATE, parity, i, mate_y_sems, mate)
 
-    for i in range(CHUNKS):
-        centre(x_ref, all_ref, ln_ref, rn_ref, i * COLS, COLS)
-        if i == 0:
+    centre(x_ref, all_ref, ln_ref, rn_ref)
+
+    def begin(group):
+        @pl.when(group == 1)
+        def _():
             pl.semaphore_wait(barrier, 4)
-        far_copy(i).start()
-        mate_copy(i).start()
+            for i in range(CHUNKS):
+                for copy in (*far_copies(i), *mate_copies(i)):
+                    copy.start()
 
     def take(group):
-        @pl.when((group >= 2) & (group <= 8) & ((group & 1) == 0))
-        def _():
-            i = (group - 2) >> 1
-            far_copy(i).wait_recv()
-            near_copy(i).start()
-            row_norms(all_ref, rn_ref, FAR + i * COLS, COLS)
-
-        @pl.when(group == NEAR_AT // 4 - 1)
+        @pl.when((group >= FAR_AT - 1) & (group < NEAR_AT - 1) & ((group & 1) == 0))
+        def _():
+            i = (group - FAR_AT + 1) >> 1
+            for copy in far_copies(i):
+                copy.wait_recv()
+            for copy in near_copies(i):
+                copy.start()
+
+        @pl.when(group == NEAR_AT - 1)
         def _():
             for i in range(CHUNKS):
-                near_copy(i).wait_recv()
-            row_norms(all_ref, rn_ref, NEAR, FR)
-
-        @pl.when(group == MATE_AT // 4 - 1)
+                for copy in near_copies(i):
+                    copy.wait_recv()
+
+        @pl.when(group == MATE_AT - 1)
         def _():
             for i in range(CHUNKS):
-                mate_copy(i).wait_recv()
-            row_norms(all_ref, rn_ref, MATE, FR)
+                for copy in mate_copies(i):
+                    copy.wait_recv()
 
     def give(group):
-        @pl.when((group >= 5) & (group <= 11) & ((group & 1) == 1))
-        def _():
-            far_y_copy((group - 5) >> 1).start()
-
-        @pl.when((group > NEAR_AT // 4) & (group <= MATE_AT // 4))
-        def _():
-            near_y_copy(group - NEAR_AT // 4 - 1).start()
-
-        @pl.when((group > MATE_AT // 4) & (group <= LAST_AT // 4))
-        def _():
-            mate_y_copy(group - MATE_AT // 4 - 1).start()
+        @pl.when((group > FAR_AT + 1) & (group <= NEAR_AT) & ((group & 1) == 1))
+        def _():
+            far_y_copy((group - FAR_AT - 2) >> 1).start()
+
+        @pl.when((group > NEAR_AT) & (group <= MATE_AT))
+        def _():
+            near_y_copy(group - NEAR_AT - 1).start()
+
+        @pl.when(group > MATE_AT)
+        def _():
+            mate_y_copy(group - MATE_AT - 1).start()
 
     def turn(row, col, old):
         y_ref[aligned(col, COLS), aligned(row, ROWS)] = old[...].T
 
-    def step(places, cov, cov_next, old, old_last):
-        (row_last, col_last), (row, col), (row_next, col_next) = places
-        products = covariance_pieces(all_ref, row_next, col_next, cov_next)
+    def step(last, now, following, cov, cov_next, old, old_last):
+        row, col = now
+        products = covariance_pieces(all_ref, *following, cov_next)
         for piece, (r, values) in enumerate(value_pieces(cov, ln_ref, rn_ref, row, col)):
             tile[aligned(row + r, STEP), aligned(col, COLS)] = values
             old[r : r + STEP, :] = encode(values)
-            if piece in (0, 2, 4):
+            if piece in (2, 8, 13):
                 next(products)
-        turn(row_last, col_last, old_last)
-
-    first = step_place(jnp.int32(0), parity)
+        turn(*last, old_last)
+
+    first = group_place(jnp.int32(0), parity)
     for _ in covariance_pieces(all_ref, *first, cov0):
         pass
     old1[...] = jnp.zeros_like(old1)
 
-    def body(s, places):
-        @pl.when((s & 3) == 0)
-        def _():
-            take(s >> 2)
-
-        @pl.when((s & 3) == 1)
-        def _():
-            give(s >> 2)
-
-        @pl.when((s & 1) == 0)
-        def _():
-            step(places, cov0, cov1, old0, old1)
-
-        @pl.when((s & 1) == 1)
-        def _():
-            step(places, cov1, cov0, old1, old0)
-
-        return places[1], places[2], step_place(jnp.minimum(s + 2, STEPS - 1), parity)
-
-    start = (first, first, step_place(jnp.int32(1), parity))
-    places = lax.fori_loop(0, STEPS, body, start)
-    turn(*places[0], old1)
+    def body(group, places):
+        last, now = places
+        second = second_place(group, now)
+        following = group_place(jnp.minimum(group + 1, GROUPS - 1), parity)
+        begin(group)
+        step(last, now, second, cov0, cov1, old0, old1)
+        take(group)
+        give(group)
+        step(now, second, following, cov1, cov0, old1, old0)
+        return second, following
+
+    last, _ = lax.fori_loop(0, GROUPS, body, (first, first))
+    turn(*last, old1)
+    mate_y_copy(CHUNKS - 1).start()
 
     for i in range(CHUNKS):
-        far_copy(i).wait_send()
-        mate_copy(i).wait_send()
-        near_copy(i).wait_send()
+        for copy in (*far_copies(i), *mate_copies(i), *near_copies(i)):
+            copy.wait_send()
         far_y_copy(i).wait()
         near_y_copy(i).wait()
         mate_y_copy(i).wait()
@@ -310,10 +311,10 @@
             pltpu.VMEM((3, 3, ROWS, COLS), jnp.float32),
             pltpu.VMEM((ROWS, COLS), jnp.bfloat16),
             pltpu.VMEM((ROWS, COLS), jnp.bfloat16),
-            *[pair] * 6,
+            *[pair] * 9,
         ],
         compiler_params=pltpu.CompilerParams(
-            collective_id=0, has_side_effects=True, vmem_limit_bytes=VMEM_LIMIT
+            collective_id=0, has_side_effects=True, vmem_limit_bytes=MAIN_LIMIT
         ),
         cost_estimate=pl.CostEstimate(
             flops=45 * FR * FR * ATOMS, bytes_accessed=32 << 20, transcendentals=0
@@ -380,7 +381,7 @@
             pltpu.VMEM((FR, FR), jnp.float32),
             pltpu.SemaphoreType.DMA((32,)),
         ],
-        compiler_params=pltpu.CompilerParams(vmem_limit_bytes=VMEM_LIMIT),
+        compiler_params=pltpu.CompilerParams(vmem_limit_bytes=FINISH_LIMIT),
         name="finish",
     )(tile, y, got)
 

time: 87.8 us -> 77 us (0.88)
  Pallas kernels: 85.8 us -> 75.5 us
    pallas_call x1, Pallas kernels: 78.4 us -> 68.1 us  [main(): pl.pallas_call(functools.partial(main_kernel, count), in_specs=[VMEM], ou...]
where the time goes in v5:
time: 77 us; the launch traced here: 76.9 us
  Pallas kernels  75.5 us (98%)
  local copies, waits for them, and re-layouts  1.41 us (2%)
    pallas_call x1, Pallas kernels, main(): pl.pallas_call(functools.partial(main_kernel, count), in_specs=[VMEM], ou...  68.1 us
    pallas_call x1, Pallas kernels, finish(): pl.pallas_call(finish_kernel, in_specs=[ANY, VMEM, VMEM], out_specs=ANY,...  7.36 us

profile of v5, /device:TPU:0, one launch (start us, length us, event | category | flops | bytes accessed | tf_op | source)
XLA Modules:
  0.0 76.9 jit_solution(3098462734647638043)
XLA Ops:
  0.0 0.0 copy-start
  0.0 1.4 %copy-done = bf16[3,1024,256]{2,1,0:T(8,128)(2,1)S(1)} copy-done((bf16[3,1024,256]{2,1,0:T(8,128)(2,1)S(1)}, bf16[3,1024,256]{2,1,0:T(8,128)(2,1)}, u32[]{:S(2)}) %copy-start) | copy-done | bytes 1572888
  1.4 68.1 %deviations.1 = (f32[1024,4096]{1,0:T(8,128)S(1)}, bf16[4096,1024]{1,0:T(8,128)(2,1)S(1)}, bf16[3072,1024]{1,0:T(8,128)(2,1)S(1)}) custom-call(bf16[3,1024,256]{2,1,0:T(8,128)(2,1)S(1)} %copy-done), custom_call_target="tpu_custom_call" | custom-call | flops 12079595520 | bytes 33554432 | tf_op jit(solution)/shard_map/deviations/pallas_call | solution.py:297
  69.5 7.4 %finish.1 = f32[5,1024,1024]{2,1,0:T(8,128)} custom-call(f32[1024,4096]{1,0:T(8,128)S(1)} %get-tuple-element.8.tile, bf16[4096,1024]{1,0:T(8,128)(2,1)S(1)} %get-tuple-element.9.y_ref, bf16[3072,1024]{1,0:T(8,128)(2,1)S(1)} %get-tuple-element.10.got_ref), custom_call_target="tpu_custom_call" | custom-call | tf_op jit(solution)/shard_map/finish/pallas_call | solution.py:372
Async XLA Ops:
  0.0 1.4 %copy-start = (bf16[3,1024,256]{2,1,0:T(8,128)(2,1)S(1)}, bf16[3,1024,256]{2,1,0:T(8,128)(2,1)}, u32[]{:S(2)}) copy-start(bf16[3,1024,256]{2,1,0:T(8,128)(2,1)} %x_ref.1) | copy-start | bytes 4718596

commit v6 on v5

--- a/solution.py
+++ b/solution.py
@@ -16,15 +16,17 @@
 HALF = FR // 2
 VMEM = pl.BlockSpec(memory_space=pltpu.VMEM)
 ANY = pl.BlockSpec(memory_space=pl.ANY)
-MAIN_LIMIT = 15 << 20
-FINISH_LIMIT = 13 << 20
+MAIN_LIMIT = 12 << 20
+FINISH_LIMIT = 22 << 20
 
 
 def aligned(index, size):
+    if isinstance(index, int):
+        return pl.ds(index, size)
     return pl.ds(pl.multiple_of(index, size), size)
 
 
-def centre(x_ref, all_ref, ln_ref, rn_ref):
+def centre(x_ref, all_ref, own_ref, ln_ref, rn_ref):
     weights = jnp.full((ATOMS, 128), 1.0 / ATOMS, jnp.bfloat16)
 
     @pl.loop(0, FR // 128)
@@ -37,6 +39,7 @@
             mean = jnp.concatenate([mean] * (ATOMS // 128), axis=1)
             centred = (values.astype(jnp.float32) - mean).astype(jnp.bfloat16)
             all_ref[k, rows, :] = centred
+            own_ref[k, rows, :] = centred
             back = centred.astype(jnp.float32)
             total = back * back if total is None else total + back * back
         norms = jnp.broadcast_to(0.5 * jnp.sum(total, axis=1, keepdims=True), (128, 128))
@@ -79,6 +82,13 @@
         yield
 
 
+def interleave(values, products):
+    for piece, value in enumerate(values):
+        yield piece, value
+        if piece in (2, 8, 13):
+            next(products, None)
+
+
 def value_pieces(cov_ref, ln_ref, rn_ref, row, col):
     for r in range(0, ROWS, STEP):
         entry = [[cov_ref[k, l, r : r + STEP, :] for l in range(3)] for k in range(3)]
@@ -107,14 +117,16 @@
 
 
 OWN, FAR, NEAR, MATE = range(0, 4 * FR, FR)
-FAR_AT, NEAR_AT, MATE_AT, GROUPS = 5, 13, 17, 21
+NEAR_OUT, MATE_OUT, WIDTH = 2 * FR, 2 * FR + HALF, 3 * FR
+FAR_AT, NEAR_AT, MATE_AT, GROUPS = 3, 11, 15, 19
 SPLIT = 2
 CHUNKS = FR // COLS
+LAST = FR - COLS
 
 
 def group_place(g, parity):
-    row = jnp.where(g == SPLIT, 2, jnp.where(g == FAR_AT - 1, 2, 0))
-    col = jnp.where(g == 0, 1, jnp.where(g <= SPLIT, 2, 3)) * COLS
+    row = jnp.where(g == SPLIT, 2, 0)
+    col = jnp.where(g == 0, 1, 2) * COLS
 
     far = g - FAR_AT
     is_far = g >= FAR_AT
@@ -126,18 +138,21 @@
     flip = jnp.where(is_mate, parity, 1 - parity)
     half = inner >> 1
     row = jnp.where(is_quarter, half * 2, row)
-    base = jnp.where(is_mate, MATE, NEAR) + (inner & 1) * COLS
+    inside = (inner & 1) * COLS
+    out = jnp.where(is_quarter, jnp.where(is_mate, MATE_OUT, NEAR_OUT) + inside, col)
+    base = jnp.where(is_mate, MATE, NEAR) + inside
     col = jnp.where(is_quarter, base + other_half(half, flip) * HALF, col)
-    return row * ROWS, col
+    return row * ROWS, col, out
 
 
 def second_place(g, first):
-    row, col = first
-    return jnp.where(g == SPLIT, 0, row + ROWS), jnp.where(g == SPLIT, 0, col)
+    row, col, out = first
+    return tuple(jnp.where(g == SPLIT, 0, each) for each in (row + ROWS, col, out))
 
 
 def main_kernel(
-    count, x_ref, tile, y_ref, got_ref, all_ref, ln_ref, rn_ref, cov0, cov1, old0, old1,
+    count, x_ref, tile, y_ref, got_ref, own_ref, ln_ref, rn_ref,
+    all_ref, cov0, cov1, old0, old1,
     far_sems, near_sems, mate_sems, far_y_sems, near_y_sems, mate_y_sems,
     far_n_sems, near_n_sems, mate_n_sems,
 ):
@@ -189,36 +204,28 @@
             remote(norms(OWN, i), norms(MATE, i), mate_n_sems, i, mate),
         )
 
-    def far_y_copy(i):
-        rows = aligned(i * COLS, COLS)
-        source = y_ref.at[aligned(FAR + i * COLS, COLS)]
-        return remote(source, got_ref.at[rows], far_y_sems, i, far)
-
-    def quarter_y_copy(block, flip, i, sems, device):
-        half = i >> 1
-        row = block + other_half(half, flip) * HALF + (i & 1) * COLS
+    def y_copy(row, half, sems, i, device):
         cols = aligned(half * HALF, HALF)
         source = y_ref.at[aligned(row, COLS), cols]
         return remote(source, got_ref.at[aligned(row - FAR, COLS), cols], sems, i, device)
 
+    def far_y_copy(i):
+        return y_copy(FAR + (i >> 1) * COLS, i & 1, far_y_sems, i, far)
+
     def near_y_copy(i):
-        return quarter_y_copy(NEAR, 1 - parity, i, near_y_sems, near)
+        return y_copy(NEAR_OUT + (i & 1) * COLS, i >> 1, near_y_sems, i, near)
 
     def mate_y_copy(i):
-        return quarter_y_copy(MATE, parity, i, mate_y_sems, mate)
-
-    centre(x_ref, all_ref, ln_ref, rn_ref)
-
-    def begin(group):
-        @pl.when(group == 1)
-        def _():
-            pl.semaphore_wait(barrier, 4)
-            for i in range(CHUNKS):
-                for copy in (*far_copies(i), *mate_copies(i)):
-                    copy.start()
+        return y_copy(MATE_OUT + (i & 1) * COLS, i >> 1, mate_y_sems, i, mate)
+
+    centre(x_ref, all_ref, own_ref, ln_ref, rn_ref)
+    pl.semaphore_wait(barrier, 4)
+    for i in range(CHUNKS):
+        for copy in (*far_copies(i), *mate_copies(i)):
+            copy.start()
 
     def take(group):
-        @pl.when((group >= FAR_AT - 1) & (group < NEAR_AT - 1) & ((group & 1) == 0))
+        @pl.when((group >= FAR_AT - 1) & (group < NEAR_AT - 1) & ((group & 1) == (FAR_AT - 1) % 2))
         def _():
             i = (group - FAR_AT + 1) >> 1
             for copy in far_copies(i):
@@ -239,9 +246,9 @@
                     copy.wait_recv()
 
     def give(group):
-        @pl.when((group > FAR_AT + 1) & (group <= NEAR_AT) & ((group & 1) == 1))
-        def _():
-            far_y_copy((group - FAR_AT - 2) >> 1).start()
+        @pl.when((group > FAR_AT) & (group <= NEAR_AT))
+        def _():
+            far_y_copy(group - FAR_AT - 1).start()
 
         @pl.when((group > NEAR_AT) & (group <= MATE_AT))
         def _():
@@ -251,21 +258,20 @@
         def _():
             mate_y_copy(group - MATE_AT - 1).start()
 
-    def turn(row, col, old):
-        y_ref[aligned(col, COLS), aligned(row, ROWS)] = old[...].T
+    def turn(row, _, out, old):
+        y_ref[aligned(out, COLS), aligned(row, ROWS)] = old[...].T
 
     def step(last, now, following, cov, cov_next, old, old_last):
-        row, col = now
-        products = covariance_pieces(all_ref, *following, cov_next)
-        for piece, (r, values) in enumerate(value_pieces(cov, ln_ref, rn_ref, row, col)):
-            tile[aligned(row + r, STEP), aligned(col, COLS)] = values
+        row, col, out = now
+        products = covariance_pieces(all_ref, *following[:2], cov_next)
+        pieces = value_pieces(cov, ln_ref, rn_ref, row, col)
+        for _, (r, values) in interleave(pieces, products):
+            tile[aligned(row + r, STEP), aligned(out, COLS)] = values
             old[r : r + STEP, :] = encode(values)
-            if piece in (2, 8, 13):
-                next(products)
         turn(*last, old_last)
 
     first = group_place(jnp.int32(0), parity)
-    for _ in covariance_pieces(all_ref, *first, cov0):
+    for _ in covariance_pieces(all_ref, *first[:2], cov0):
         pass
     old1[...] = jnp.zeros_like(old1)
 
@@ -273,7 +279,6 @@
         last, now = places
         second = second_place(group, now)
         following = group_place(jnp.minimum(group + 1, GROUPS - 1), parity)
-        begin(group)
         step(last, now, second, cov0, cov1, old0, old1)
         take(group)
         give(group)
@@ -287,31 +292,35 @@
     for i in range(CHUNKS):
         for copy in (*far_copies(i), *mate_copies(i), *near_copies(i)):
             copy.wait_send()
-        far_y_copy(i).wait()
         near_y_copy(i).wait()
         mate_y_copy(i).wait()
+    for i in range(2 * CHUNKS):
+        far_y_copy(i).wait()
 
 
 def main(coords, count):
     pair = pltpu.SemaphoreType.DMA((2, CHUNKS))
+    pairs = [pair] * 9
+    pairs[3] = pltpu.SemaphoreType.DMA((2, 2 * CHUNKS))
     return pl.pallas_call(
         functools.partial(main_kernel, count),
         in_specs=[VMEM],
-        out_specs=[VMEM] * 3,
+        out_specs=[VMEM] * 6,
         out_shape=[
-            jax.ShapeDtypeStruct((FR, 4 * FR), jnp.float32),
-            jax.ShapeDtypeStruct((4 * FR, FR), jnp.bfloat16),
-            jax.ShapeDtypeStruct((3 * FR, FR), jnp.bfloat16),
+            jax.ShapeDtypeStruct((FR, WIDTH), jnp.float32),
+            jax.ShapeDtypeStruct((WIDTH, FR), jnp.bfloat16),
+            jax.ShapeDtypeStruct((WIDTH - FR, FR), jnp.bfloat16),
+            jax.ShapeDtypeStruct((3, FR, ATOMS), jnp.bfloat16),
+            jax.ShapeDtypeStruct((FR, 128), jnp.float32),
+            jax.ShapeDtypeStruct((8, 4 * FR), jnp.float32),
         ],
         scratch_shapes=[
             pltpu.VMEM((3, 4 * FR, ATOMS), jnp.bfloat16),
-            pltpu.VMEM((FR, 128), jnp.float32),
-            pltpu.VMEM((8, 4 * FR), jnp.float32),
             pltpu.VMEM((3, 3, ROWS, COLS), jnp.float32),
             pltpu.VMEM((3, 3, ROWS, COLS), jnp.float32),
             pltpu.VMEM((ROWS, COLS), jnp.bfloat16),
             pltpu.VMEM((ROWS, COLS), jnp.bfloat16),
-            *[pair] * 9,
+            *pairs,
         ],
         compiler_params=pltpu.CompilerParams(
             collective_id=0, has_side_effects=True, vmem_limit_bytes=MAIN_LIMIT
@@ -327,63 +336,136 @@
     return lax.rsqrt(lax.rsqrt(values.astype(jnp.float32)))
 
 
-def finish_kernel(tile, y_ref, got_ref, out_ref, far_tile, near_tile, mate_tile, low_tile, sem):
+def finish_kernel(
+    tile, y_ref, got_ref, own_ref, ln_ref, rn_ref, out_ref,
+    far_tile, rest_tile, low_tile, column, turned, cov0, cov1, old0, old1, sem,
+):
     parity = lax.rem(lax.axis_index("frames"), 2)
     copies = []
 
-    def copy(source, slot, rows, cols):
+    def copy(source, slot, rows, cols, start=True):
         copies.append(
             pltpu.make_async_copy(source, out_ref.at[slot, rows, cols], sem.at[len(copies)])
         )
-        copies[-1].start()
-
-    def half(i, base=0):
-        return pl.ds(pl.multiple_of(base + i * HALF, HALF), HALF)
-
-    both = pl.ds(0, FR)
-    quarters = ((NEAR, near_place(parity), near_tile), (MATE, mate_place(parity), mate_tile))
+        if start:
+            copies[-1].start()
+        return copies[-1]
+
+    def half(i):
+        return aligned(i * HALF, HALF)
+
+    both, last = pl.ds(0, FR), pl.ds(LAST, COLS)
+    near_slot, near_flip = near_place(parity)
+    mate_slot, mate_flip = mate_place(parity)
+    quarters = (
+        (NEAR_OUT, near_slot, near_flip, rest_tile.at[0]),
+        (MATE_OUT, mate_slot, mate_flip, rest_tile.at[1]),
+    )
     copy(tile.at[:, pl.ds(FAR, FR)], 4 * (1 - parity), both, both)
-    for block, (slot, flip), _ in quarters:
+    for first, slot, flip, _ in quarters:
         for i in range(2):
-            other = other_half(i, flip)
-            copy(tile.at[half(i), half(other, block)], slot, half(i), half(other))
-    for c in range(CHUNKS):
+            other = half(other_half(i, flip))
+            copy(tile.at[half(i), pl.ds(first, HALF)], slot, half(i), other)
+    for c in range(CHUNKS - 1):
         rows, cols = pl.ds(0, (c + 1) * COLS), pl.ds(c * COLS, COLS)
         copy(tile.at[rows, cols], 2, rows, cols)
 
-    for i in range(CHUNKS):
-        rows = pl.ds(i * COLS, COLS)
+    far_copies = [
+        copy(far_tile.at[half(i)], 4 * parity, half(i), both, start=False) for i in range(2)
+    ]
+    quarter_copies = [
+        [
+            copy(tiles.at[:, half(i)], slot, half(other_half(i, 1 - flip)), half(i), start=False)
+            for i in range(2)
+        ]
+        for _, slot, flip, tiles in quarters
+    ]
+    column_copies = [copy(column.at[half(i)], 2, half(i), last, start=False) for i in range(2)]
+    low_copies = []
+    for c in range(1, CHUNKS - 1):
+        low, cols = pl.ds(c * COLS, COLS), pl.ds(0, c * COLS)
+        low_copies.append(copy(low_tile.at[low, cols], 2, low, cols, start=False))
+    turned_copy = copy(turned, 2, last, pl.ds(0, LAST), start=False)
+
+    def turn(row, old):
+        turned[:, aligned(row, ROWS)] = old[...].T
+
+    def step(row, row_last, row_next, cov, cov_next, old, old_last, also):
+        products = covariance_pieces(own_ref, row_next, LAST, cov_next)
+        pieces = value_pieces(cov, ln_ref, rn_ref, row, LAST)
+        for piece, (r, values) in interleave(pieces, products):
+            column[aligned(row + r, STEP), :] = values
+            old[r : r + STEP, :] = values
+            also(piece)
+        turn(row_last, old_last)
+
+    for _ in covariance_pieces(own_ref, 0, LAST, cov0):
+        pass
+    old1[...] = jnp.zeros_like(old1)
+
+    def decode_far(i, piece):
+        rows = aligned(i * HALF + piece * 32, 32)
         far_tile[rows, :] = decode(got_ref[rows, :])
-        copy(far_tile.at[rows], 4 * parity, rows, both)
-    for block, (slot, flip), tiles in quarters:
-        for i in range(2):
-            own = other_half(i, 1 - flip)
-            tiles[i] = decode(got_ref[half(own, block - FAR), half(i)])
-            copy(tiles.at[i], slot, half(own), half(i))
-    for c in range(1, CHUNKS):
-        rows, cols = pl.ds(c * COLS, COLS), pl.ds(0, c * COLS)
-        low_tile[rows, cols] = decode(y_ref[rows, cols])
-        copy(low_tile.at[rows, cols], 2, rows, cols)
+
+    def decode_rest(i, piece):
+        rows, low = pl.ds(piece * 32, 32), aligned(COLS + i * COLS + piece * 16, 16)
+        near_or_mate = aligned(NEAR_OUT - FAR + i * HALF + piece * 32, 32)
+        rest_tile[i, rows, :] = decode(got_ref[near_or_mate, :])
+        low_tile[low, :] = decode(y_ref[low, 0:HALF])
+
+    completed = (
+        (far_copies[0],),
+        (*quarter_copies[0], column_copies[0], low_copies[0]),
+        (far_copies[1],),
+        (*quarter_copies[1], column_copies[1], low_copies[1]),
+    )
+
+    @pl.loop(0, len(completed))
+    def _(s):
+        row = s * ROWS
+        places = row, jnp.maximum(row - ROWS, 0), jnp.minimum(row + ROWS, LAST)
+
+        @pl.when((s & 1) == 0)
+        def _():
+            step(*places, cov0, cov1, old0, old1, functools.partial(decode_far, s >> 1))
+
+        @pl.when((s & 1) == 1)
+        def _():
+            step(*places, cov1, cov0, old1, old0, functools.partial(decode_rest, s >> 1))
+
+        for each, group in enumerate(completed):
+
+            @pl.when(s == each)
+            def _():
+                for piece in group:
+                    piece.start()
+
+    turned_copy.start()
     for each in copies:
         each.wait()
 
 
-def finish(tile, y, got):
+def finish(*held):
     return pl.pallas_call(
         finish_kernel,
-        in_specs=[ANY, VMEM, VMEM],
+        in_specs=[ANY] + [VMEM] * 5,
         out_specs=ANY,
         out_shape=jax.ShapeDtypeStruct((5, FR, FR), jnp.float32),
         scratch_shapes=[
             pltpu.VMEM((FR, FR), jnp.float32),
-            pltpu.VMEM((2, HALF, HALF), jnp.float32),
-            pltpu.VMEM((2, HALF, HALF), jnp.float32),
-            pltpu.VMEM((FR, FR), jnp.float32),
+            pltpu.VMEM((2, HALF, FR), jnp.float32),
+            pltpu.VMEM((LAST, HALF), jnp.float32),
+            pltpu.VMEM((FR, COLS), jnp.float32),
+            pltpu.VMEM((COLS, LAST), jnp.float32),
+            pltpu.VMEM((3, 3, ROWS, COLS), jnp.float32),
+            pltpu.VMEM((3, 3, ROWS, COLS), jnp.float32),
+            pltpu.VMEM((ROWS, COLS), jnp.float32),
+            pltpu.VMEM((ROWS, COLS), jnp.float32),
             pltpu.SemaphoreType.DMA((32,)),
         ],
         compiler_params=pltpu.CompilerParams(vmem_limit_bytes=FINISH_LIMIT),
         name="finish",
-    )(tile, y, got)
+    )(*held)
 
 
 def on_device(coords):

time: 77 us -> 75.1 us (0.975)
  Pallas kernels: 75.5 us -> 73.6 us
    pallas_call x1, Pallas kernels: 68.1 us -> 64.6 us  [main(): pl.pallas_call(functools.partial(main_kernel, count), in_specs=[VMEM], ou...]
    pallas_call x1, Pallas kernels: 7.36 us -> 8.97 us  [finish(): pl.pallas_call(finish_kernel, in_specs=[ANY] + [VMEM] * 5, out_specs=ANY,...]
where the time goes in v6:
time: 75.1 us; the launch traced here: 75 us
  Pallas kernels  73.6 us (98%)
  local copies, waits for them, and re-layouts  1.41 us (2%)
    pallas_call x1, Pallas kernels, main(): pl.pallas_call(functools.partial(main_kernel, count), in_specs=[VMEM], ou...  64.6 us
    pallas_call x1, Pallas kernels, finish(): pl.pallas_call(finish_kernel, in_specs=[ANY] + [VMEM] * 5, out_specs=ANY,...  8.97 us

profile of v6, /device:TPU:0, one launch (start us, length us, event | category | flops | bytes accessed | tf_op | source)
XLA Modules:
  0.0 75.0 jit_solution(16616619492652345466)
XLA Ops:
  0.0 0.0 copy-start
  0.0 1.4 %copy-done = bf16[3,1024,256]{2,1,0:T(8,128)(2,1)S(1)} copy-done((bf16[3,1024,256]{2,1,0:T(8,128)(2,1)S(1)}, bf16[3,1024,256]{2,1,0:T(8,128)(2,1)}, u32[]{:S(2)}) %copy-start) | copy-done | bytes 1572888
  1.4 64.6 %deviations.1 = (f32[1024,3072]{1,0:T(8,128)S(1)}, bf16[3072,1024]{1,0:T(8,128)(2,1)S(1)}, bf16[2048,1024]{1,0:T(8,128)(2,1)S(1)}, bf16[3,1024,256]{2,1,0:T(8,12...) custom-call(bf16[3,1024,256]{2,1,0:T(8,128)(2,1)S(1)} %copy-done), custom_call_target="tpu_custom_call" | custom-call | flops 12079595520 | bytes 33554432 | tf_op jit(solution)/shard_map/deviations/pallas_call | solution.py:305
  66.1 9.0 %finish.1 = f32[5,1024,1024]{2,1,0:T(8,128)} custom-call(f32[1024,3072]{1,0:T(8,128)S(1)} %get-tuple-element.11.tile, bf16[3072,1024]{1,0:T(8,128)(2,1)S(1)} %get-tuple-element.12.y_ref, bf16[2048,1024]{1,0:T(8,128)(2,1)S(1)} %get-tuple-element.13.got_ref, bf16[3,1024,256]{2,1,0:T(8,128)(2,1)S(1)} %get-tuple-element.14.own_ref, ...), custom_call_target="tpu_custom_call" | custom-call | tf_op jit(solution)/shard_map/finish/pallas_call | solution.py:449
Async XLA Ops:
  0.0 1.4 %copy-start = (bf16[3,1024,256]{2,1,0:T(8,128)(2,1)S(1)}, bf16[3,1024,256]{2,1,0:T(8,128)(2,1)}, u32[]{:S(2)}) copy-start(bf16[3,1024,256]{2,1,0:T(8,128)(2,1)} %x_ref.1) | copy-start | bytes 4718596

commit v7 on v6

--- a/solution.py
+++ b/solution.py
@@ -26,12 +26,12 @@
     return pl.ds(pl.multiple_of(index, size), size)
 
 
-def centre(x_ref, all_ref, own_ref, ln_ref, rn_ref):
+def centre(x_ref, all_ref, own_ref, ln_ref, rn_ref, first):
     weights = jnp.full((ATOMS, 128), 1.0 / ATOMS, jnp.bfloat16)
 
-    @pl.loop(0, FR // 128)
+    @pl.loop(0, COLS // 128)
     def _(i):
-        rows = aligned(i * 128, 128)
+        rows = aligned(first + i * 128, 128)
         total = None
         for k in range(3):
             values = x_ref[k, rows, :]
@@ -118,7 +118,7 @@
 
 OWN, FAR, NEAR, MATE = range(0, 4 * FR, FR)
 NEAR_OUT, MATE_OUT, WIDTH = 2 * FR, 2 * FR + HALF, 3 * FR
-FAR_AT, NEAR_AT, MATE_AT, GROUPS = 3, 11, 15, 19
+FAR_AT, NEAR_AT, MATE_AT, GROUPS = 4, 12, 16, 20
 SPLIT = 2
 CHUNKS = FR // COLS
 LAST = FR - COLS
@@ -126,7 +126,7 @@
 
 def group_place(g, parity):
     row = jnp.where(g == SPLIT, 2, 0)
-    col = jnp.where(g == 0, 1, 2) * COLS
+    col = jnp.where(g == 0, 1, jnp.where(g <= SPLIT, 2, 3)) * COLS
 
     far = g - FAR_AT
     is_far = g >= FAR_AT
@@ -153,8 +153,7 @@
 def main_kernel(
     count, x_ref, tile, y_ref, got_ref, own_ref, ln_ref, rn_ref,
     all_ref, cov0, cov1, old0, old1,
-    far_sems, near_sems, mate_sems, far_y_sems, near_y_sems, mate_y_sems,
-    far_n_sems, near_n_sems, mate_n_sems,
+    frame_sems, norm_sems, y_sems,
 ):
     me = lax.axis_index("frames")
     parity = lax.rem(me, 2)
@@ -186,77 +185,58 @@
     def norms(block, i):
         return rn_ref.at[:, aligned(block + i * COLS, COLS)]
 
-    def far_copies(i):
+    def frame_copies(k):
+        i, kind = k & 3, k >> 2
+        source = jnp.where(kind == 1, FAR, OWN)
+        target = jnp.where(kind == 0, FAR, jnp.where(kind == 1, NEAR, MATE))
+        device = jnp.where(kind == 0, far_back, mate)
         return (
-            remote(frames(OWN, i), frames(FAR, i), far_sems, i, far_back),
-            remote(norms(OWN, i), norms(FAR, i), far_n_sems, i, far_back),
+            remote(frames(source, i), frames(target, i), frame_sems, k, device),
+            remote(norms(source, i), norms(target, i), norm_sems, k, device),
         )
 
-    def near_copies(i):
-        return (
-            remote(frames(FAR, i), frames(NEAR, i), near_sems, i, mate),
-            remote(norms(FAR, i), norms(NEAR, i), near_n_sems, i, mate),
-        )
-
-    def mate_copies(i):
-        return (
-            remote(frames(OWN, i), frames(MATE, i), mate_sems, i, mate),
-            remote(norms(OWN, i), norms(MATE, i), mate_n_sems, i, mate),
-        )
-
-    def y_copy(row, half, sems, i, device):
+    def y_copy(k):
+        is_far = k < 8
+        half = jnp.where(is_far, k & 1, (k >> 1) & 1)
+        quarter = NEAR_OUT + ((k - 8) >> 2) * HALF + (k & 1) * COLS
+        row = jnp.where(is_far, FAR + (k >> 1) * COLS, quarter)
+        device = jnp.where(is_far, far, jnp.where(k < 12, near, mate))
         cols = aligned(half * HALF, HALF)
         source = y_ref.at[aligned(row, COLS), cols]
-        return remote(source, got_ref.at[aligned(row - FAR, COLS), cols], sems, i, device)
-
-    def far_y_copy(i):
-        return y_copy(FAR + (i >> 1) * COLS, i & 1, far_y_sems, i, far)
-
-    def near_y_copy(i):
-        return y_copy(NEAR_OUT + (i & 1) * COLS, i >> 1, near_y_sems, i, near)
-
-    def mate_y_copy(i):
-        return y_copy(MATE_OUT + (i & 1) * COLS, i >> 1, mate_y_sems, i, mate)
-
-    centre(x_ref, all_ref, own_ref, ln_ref, rn_ref)
+        return remote(source, got_ref.at[aligned(row - FAR, COLS), cols], y_sems, k, device)
+
+    centre(x_ref, all_ref, own_ref, ln_ref, rn_ref, 0)
     pl.semaphore_wait(barrier, 4)
-    for i in range(CHUNKS):
-        for copy in (*far_copies(i), *mate_copies(i)):
-            copy.start()
-
-    def take(group):
-        @pl.when((group >= FAR_AT - 1) & (group < NEAR_AT - 1) & ((group & 1) == (FAR_AT - 1) % 2))
-        def _():
-            i = (group - FAR_AT + 1) >> 1
-            for copy in far_copies(i):
+    for copy in frame_copies(jnp.int32(0)):
+        copy.start()
+    for i in range(1, CHUNKS):
+        centre(x_ref, all_ref, own_ref, ln_ref, rn_ref, i * COLS)
+
+    def between(group):
+        @pl.when((group >= FAR_AT - 1) & (group < NEAR_AT - 2) & ((group & 1) == 1))
+        def _():
+            for copy in frame_copies((group - FAR_AT + 1) >> 1):
                 copy.wait_recv()
-            for copy in near_copies(i):
+
+        @pl.when((group >= NEAR_AT - 4) & (group < MATE_AT))
+        def _():
+            for copy in frame_copies(group - NEAR_AT + 8):
+                copy.wait_recv()
+
+        is_far = ((group & 1) == 1) & (group < 7)
+        is_near = ((group & 1) == 0) & (group > 2)
+        chunk = jnp.where(group == 2, 8, 8 + ((group - 5) >> 1))
+        chunk = jnp.where(is_near, 4 + ((group - 4) >> 1), chunk)
+        chunk = jnp.where(is_far, (group + 1) >> 1, chunk)
+
+        @pl.when((group >= 1) & (group < NEAR_AT))
+        def _():
+            for copy in frame_copies(chunk):
                 copy.start()
 
-        @pl.when(group == NEAR_AT - 1)
-        def _():
-            for i in range(CHUNKS):
-                for copy in near_copies(i):
-                    copy.wait_recv()
-
-        @pl.when(group == MATE_AT - 1)
-        def _():
-            for i in range(CHUNKS):
-                for copy in mate_copies(i):
-                    copy.wait_recv()
-
-    def give(group):
-        @pl.when((group > FAR_AT) & (group <= NEAR_AT))
-        def _():
-            far_y_copy(group - FAR_AT - 1).start()
-
-        @pl.when((group > NEAR_AT) & (group <= MATE_AT))
-        def _():
-            near_y_copy(group - NEAR_AT - 1).start()
-
-        @pl.when(group > MATE_AT)
-        def _():
-            mate_y_copy(group - MATE_AT - 1).start()
+        @pl.when(group > FAR_AT)
+        def _():
+            y_copy(group - FAR_AT - 1).start()
 
     def turn(row, _, out, old):
         y_ref[aligned(out, COLS), aligned(row, ROWS)] = old[...].T
@@ -280,28 +260,26 @@
         second = second_place(group, now)
         following = group_place(jnp.minimum(group + 1, GROUPS - 1), parity)
         step(last, now, second, cov0, cov1, old0, old1)
-        take(group)
-        give(group)
+        between(group)
         step(now, second, following, cov1, cov0, old1, old0)
         return second, following
 
     last, _ = lax.fori_loop(0, GROUPS, body, (first, first))
     turn(*last, old1)
-    mate_y_copy(CHUNKS - 1).start()
-
-    for i in range(CHUNKS):
-        for copy in (*far_copies(i), *mate_copies(i), *near_copies(i)):
+    last_copy = GROUPS - FAR_AT - 1
+    y_copy(jnp.int32(last_copy)).start()
+
+    @pl.loop(0, 3 * CHUNKS)
+    def _(k):
+        for copy in frame_copies(k):
             copy.wait_send()
-        near_y_copy(i).wait()
-        mate_y_copy(i).wait()
-    for i in range(2 * CHUNKS):
-        far_y_copy(i).wait()
+
+    @pl.loop(0, last_copy + 1)
+    def _(k):
+        y_copy(k).wait()
 
 
 def main(coords, count):
-    pair = pltpu.SemaphoreType.DMA((2, CHUNKS))
-    pairs = [pair] * 9
-    pairs[3] = pltpu.SemaphoreType.DMA((2, 2 * CHUNKS))
     return pl.pallas_call(
         functools.partial(main_kernel, count),
         in_specs=[VMEM],
@@ -320,7 +298,9 @@
             pltpu.VMEM((3, 3, ROWS, COLS), jnp.float32),
             pltpu.VMEM((ROWS, COLS), jnp.bfloat16),
             pltpu.VMEM((ROWS, COLS), jnp.bfloat16),
-            *pairs,
+            pltpu.SemaphoreType.DMA((2, 3 * CHUNKS)),
+            pltpu.SemaphoreType.DMA((2, 3 * CHUNKS)),
+            pltpu.SemaphoreType.DMA((2, GROUPS - FAR_AT)),
         ],
         compiler_params=pltpu.CompilerParams(
             collective_id=0, has_side_effects=True, vmem_limit_bytes=MAIN_LIMIT
@@ -366,72 +346,57 @@
         for i in range(2):
             other = half(other_half(i, flip))
             copy(tile.at[half(i), pl.ds(first, HALF)], slot, half(i), other)
-    for c in range(CHUNKS - 1):
-        rows, cols = pl.ds(0, (c + 1) * COLS), pl.ds(c * COLS, COLS)
+    for c in range(CHUNKS):
+        rows, cols = pl.ds(0, HALF if c == CHUNKS - 1 else (c + 1) * COLS), pl.ds(c * COLS, COLS)
         copy(tile.at[rows, cols], 2, rows, cols)
 
-    far_copies = [
-        copy(far_tile.at[half(i)], 4 * parity, half(i), both, start=False) for i in range(2)
+    def later(source, slot, rows, cols):
+        return copy(source, slot, rows, cols, start=False)
+
+    first_rows, second_rows = pl.ds(HALF, COLS), pl.ds(LAST, COLS)
+    far_copies = [later(far_tile.at[half(i)], 4 * parity, half(i), both) for i in range(2)]
+    (near_copies, mate_copies) = (
+        [later(tiles.at[:, half(i)], slot, half(other_half(i, 1 - flip)), half(i)) for i in range(2)]
+        for _, slot, flip, tiles in quarters
+    )
+    completed = [
+        [far_copies[0], *near_copies, later(column.at[pl.ds(0, COLS)], 2, first_rows, last)],
+        [far_copies[1], *mate_copies, later(column.at[pl.ds(COLS, COLS)], 2, second_rows, last)],
     ]
-    quarter_copies = [
-        [
-            copy(tiles.at[:, half(i)], slot, half(other_half(i, 1 - flip)), half(i), start=False)
-            for i in range(2)
-        ]
-        for _, slot, flip, tiles in quarters
-    ]
-    column_copies = [copy(column.at[half(i)], 2, half(i), last, start=False) for i in range(2)]
-    low_copies = []
-    for c in range(1, CHUNKS - 1):
-        low, cols = pl.ds(c * COLS, COLS), pl.ds(0, c * COLS)
-        low_copies.append(copy(low_tile.at[low, cols], 2, low, cols, start=False))
-    turned_copy = copy(turned, 2, last, pl.ds(0, LAST), start=False)
-
-    def turn(row, old):
-        turned[:, aligned(row, ROWS)] = old[...].T
-
-    def step(row, row_last, row_next, cov, cov_next, old, old_last, also):
-        products = covariance_pieces(own_ref, row_next, LAST, cov_next)
+    for c in range(1, CHUNKS):
+        low, cols = pl.ds(c * COLS, COLS), pl.ds(0, min(c * COLS, HALF))
+        completed[c > 1].append(later(low_tile.at[low, cols], 2, low, cols))
+    completed[1].append(later(turned, 2, last, first_rows))
+
+    def decode_pieces(s, piece):
+        rows = aligned(s * HALF + piece * 32, 32)
+        far_tile[rows, :] = decode(got_ref[rows, :])
+        near_or_mate = aligned(NEAR_OUT - FAR + s * HALF + piece * 32, 32)
+        rest_tile[s, pl.ds(piece * 32, 32), :] = decode(got_ref[near_or_mate, :])
+        low = pl.ds(COLS + piece * 16, 16) if s == 0 else pl.ds(HALF + piece * 32, 32)
+        low_tile[low, :] = decode(y_ref[low, 0:HALF])
+
+    def step(s, cov, old, products):
+        row = HALF + s * ROWS
         pieces = value_pieces(cov, ln_ref, rn_ref, row, LAST)
         for piece, (r, values) in interleave(pieces, products):
-            column[aligned(row + r, STEP), :] = values
+            column[s * ROWS + r : s * ROWS + r + STEP, :] = values
             old[r : r + STEP, :] = values
-            also(piece)
-        turn(row_last, old_last)
-
-    for _ in covariance_pieces(own_ref, 0, LAST, cov0):
+            decode_pieces(s, piece)
+
+    for _ in covariance_pieces(own_ref, HALF, LAST, cov0):
         pass
-    old1[...] = jnp.zeros_like(old1)
-
-    def decode_far(i, piece):
-        rows = aligned(i * HALF + piece * 32, 32)
-        far_tile[rows, :] = decode(got_ref[rows, :])
-
-    def decode_rest(i, piece):
-        rows, low = pl.ds(piece * 32, 32), aligned(COLS + i * COLS + piece * 16, 16)
-        near_or_mate = aligned(NEAR_OUT - FAR + i * HALF + piece * 32, 32)
-        rest_tile[i, rows, :] = decode(got_ref[near_or_mate, :])
-        low_tile[low, :] = decode(y_ref[low, 0:HALF])
-
-    completed = (
-        (far_copies[0],),
-        (*quarter_copies[0], column_copies[0], low_copies[0]),
-        (far_copies[1],),
-        (*quarter_copies[1], column_copies[1], low_copies[1]),
-    )
-
-    @pl.loop(0, len(completed))
+
+    @pl.loop(0, 2)
     def _(s):
-        row = s * ROWS
-        places = row, jnp.maximum(row - ROWS, 0), jnp.minimum(row + ROWS, LAST)
-
-        @pl.when((s & 1) == 0)
-        def _():
-            step(*places, cov0, cov1, old0, old1, functools.partial(decode_far, s >> 1))
-
-        @pl.when((s & 1) == 1)
-        def _():
-            step(*places, cov1, cov0, old1, old0, functools.partial(decode_rest, s >> 1))
+        @pl.when(s == 0)
+        def _():
+            step(0, cov0, old0, covariance_pieces(own_ref, LAST, LAST, cov1))
+
+        @pl.when(s == 1)
+        def _():
+            step(1, cov1, old1, iter(()))
+            turned[...] = old0[...].T
 
         for each, group in enumerate(completed):
 
@@ -440,7 +405,6 @@
                 for piece in group:
                     piece.start()
 
-    turned_copy.start()
     for each in copies:
         each.wait()
 
@@ -454,9 +418,9 @@
         scratch_shapes=[
             pltpu.VMEM((FR, FR), jnp.float32),
             pltpu.VMEM((2, HALF, FR), jnp.float32),
-            pltpu.VMEM((LAST, HALF), jnp.float32),
-            pltpu.VMEM((FR, COLS), jnp.float32),
-            pltpu.VMEM((COLS, LAST), jnp.float32),
+            pltpu.VMEM((FR, HALF), jnp.float32),
+            pltpu.VMEM((HALF, COLS), jnp.float32),
+            pltpu.VMEM((COLS, COLS), jnp.float32),
             pltpu.VMEM((3, 3, ROWS, COLS), jnp.float32),
             pltpu.VMEM((3, 3, ROWS, COLS), jnp.float32),
             pltpu.VMEM((ROWS, COLS), jnp.float32),

time: 75.1 us -> 77.1 us (1.027)
  Pallas kernels: 73.6 us -> 75.6 us
    pallas_call x1, Pallas kernels: 64.6 us -> 68.2 us  [main(): pl.pallas_call(functools.partial(main_kernel, count), in_specs=[VMEM], ou...]
    pallas_call x1, Pallas kernels: 8.97 us -> 7.36 us  [finish(): pl.pallas_call(finish_kernel, in_specs=[ANY] + [VMEM] * 5, out_specs=ANY,...]
where the time goes in v7:
time: 77.1 us; the launch traced here: 77 us
  Pallas kernels  75.6 us (98%)
  local copies, waits for them, and re-layouts  1.41 us (2%)
    pallas_call x1, Pallas kernels, main(): pl.pallas_call(functools.partial(main_kernel, count), in_specs=[VMEM], ou...  68.2 us
    pallas_call x1, Pallas kernels, finish(): pl.pallas_call(finish_kernel, in_specs=[ANY] + [VMEM] * 5, out_specs=ANY,...  7.36 us

profile of v7, /device:TPU:0, one launch (start us, length us, event | category | flops | bytes accessed | tf_op | source)
XLA Modules:
  0.0 77.0 jit_solution(1448157269331252045)
XLA Ops:
  0.0 0.0 copy-start
  0.0 1.4 %copy-done = bf16[3,1024,256]{2,1,0:T(8,128)(2,1)S(1)} copy-done((bf16[3,1024,256]{2,1,0:T(8,128)(2,1)S(1)}, bf16[3,1024,256]{2,1,0:T(8,128)(2,1)}, u32[]{:S(2)}) %copy-start) | copy-done | bytes 1572888
  1.4 68.2 %deviations.1 = (f32[1024,3072]{1,0:T(8,128)S(1)}, bf16[3072,1024]{1,0:T(8,128)(2,1)S(1)}, bf16[2048,1024]{1,0:T(8,128)(2,1)S(1)}, bf16[3,1024,256]{2,1,0:T(8,12...) custom-call(bf16[3,1024,256]{2,1,0:T(8,128)(2,1)S(1)} %copy-done), custom_call_target="tpu_custom_call" | custom-call | flops 12079595520 | bytes 33554432 | tf_op jit(solution)/shard_map/deviations/pallas_call | solution.py:283
  69.6 7.4 %finish.1 = f32[5,1024,1024]{2,1,0:T(8,128)} custom-call(f32[1024,3072]{1,0:T(8,128)S(1)} %get-tuple-element.11.tile, bf16[3072,1024]{1,0:T(8,128)(2,1)S(1)} %get-tuple-element.12.y_ref, bf16[2048,1024]{1,0:T(8,128)(2,1)S(1)} %get-tuple-element.13.got_ref, bf16[3,1024,256]{2,1,0:T(8,128)(2,1)S(1)} %get-tuple-element.14.own_ref, ...), custom_call_target="tpu_custom_call" | custom-call | tf_op jit(solution)/shard_map/finish/pallas_call | solution.py:413
Async XLA Ops:
  0.0 1.4 %copy-start = (bf16[3,1024,256]{2,1,0:T(8,128)(2,1)S(1)}, bf16[3,1024,256]{2,1,0:T(8,128)(2,1)}, u32[]{:S(2)}) copy-start(bf16[3,1024,256]{2,1,0:T(8,128)(2,1)} %x_ref.1) | copy-start | bytes 4718596

commit v8 on v7

--- a/solution.py
+++ b/solution.py
@@ -118,8 +118,10 @@
 
 OWN, FAR, NEAR, MATE = range(0, 4 * FR, FR)
 NEAR_OUT, MATE_OUT, WIDTH = 2 * FR, 2 * FR + HALF, 3 * FR
-FAR_AT, NEAR_AT, MATE_AT, GROUPS = 4, 12, 16, 20
+LAST_ROW = FR - ROWS
+FAR_AT, NEAR_AT, EXTRA_AT, MATE_AT, GROUPS = 4, 12, 16, 17, 21
 SPLIT = 2
+EXTRA_ROW, SENDS = LAST_ROW, 15
 CHUNKS = FR // COLS
 LAST = FR - COLS
 
@@ -133,8 +135,8 @@
     row = jnp.where(is_far, (far & 1) * 2, row)
     col = jnp.where(is_far, FAR + (far >> 1) * COLS, col)
 
-    inner = (g - NEAR_AT) & 3
     is_quarter, is_mate = g >= NEAR_AT, g >= MATE_AT
+    inner = (g - jnp.where(is_mate, MATE_AT, NEAR_AT)) & 3
     flip = jnp.where(is_mate, parity, 1 - parity)
     half = inner >> 1
     row = jnp.where(is_quarter, half * 2, row)
@@ -142,12 +144,23 @@
     out = jnp.where(is_quarter, jnp.where(is_mate, MATE_OUT, NEAR_OUT) + inside, col)
     base = jnp.where(is_mate, MATE, NEAR) + inside
     col = jnp.where(is_quarter, base + other_half(half, flip) * HALF, col)
-    return row * ROWS, col, out
+
+    is_extra = g == EXTRA_AT
+    out_row = jnp.where(is_extra, EXTRA_ROW, row * ROWS)
+    row = jnp.where(is_extra, extra_row(parity), row * ROWS)
+    return row, jnp.where(is_extra, NEAR + HALF, col), out_row, jnp.where(is_extra, 0, out)
+
+
+def extra_row(parity):
+    return other_half(1, parity) * HALF + COLS
 
 
 def second_place(g, first):
-    row, col, out = first
-    return tuple(jnp.where(g == SPLIT, 0, each) for each in (row + ROWS, col, out))
+    row, col, out_row, out = first
+    is_extra = g == EXTRA_AT
+    down, along = jnp.where(is_extra, 0, ROWS), jnp.where(is_extra, COLS, 0)
+    second = row + down, col + along, out_row + down, out + along
+    return tuple(jnp.where(g == SPLIT, 0, each) for each in second)
 
 
 def main_kernel(
@@ -196,11 +209,12 @@
         )
 
     def y_copy(k):
-        is_far = k < 8
-        half = jnp.where(is_far, k & 1, (k >> 1) & 1)
-        quarter = NEAR_OUT + ((k - 8) >> 2) * HALF + (k & 1) * COLS
+        is_far, is_near = k < 8, k < 11
+        i = k - jnp.where(is_near, 8, 11)
+        half = jnp.where(is_far, k & 1, i >> 1)
+        quarter = jnp.where(is_near, NEAR_OUT, MATE_OUT) + (i & 1) * COLS
         row = jnp.where(is_far, FAR + (k >> 1) * COLS, quarter)
-        device = jnp.where(is_far, far, jnp.where(k < 12, near, mate))
+        device = jnp.where(is_far, far, jnp.where(is_near, near, mate))
         cols = aligned(half * HALF, HALF)
         source = y_ref.at[aligned(row, COLS), cols]
         return remote(source, got_ref.at[aligned(row - FAR, COLS), cols], y_sems, k, device)
@@ -218,35 +232,33 @@
             for copy in frame_copies((group - FAR_AT + 1) >> 1):
                 copy.wait_recv()
 
-        @pl.when((group >= NEAR_AT - 4) & (group < MATE_AT))
+        @pl.when((group >= NEAR_AT - 4) & (group < NEAR_AT + 4))
         def _():
             for copy in frame_copies(group - NEAR_AT + 8):
                 copy.wait_recv()
 
-        is_far = ((group & 1) == 1) & (group < 7)
-        is_near = ((group & 1) == 0) & (group > 2)
-        chunk = jnp.where(group == 2, 8, 8 + ((group - 5) >> 1))
-        chunk = jnp.where(is_near, 4 + ((group - 4) >> 1), chunk)
-        chunk = jnp.where(is_far, (group + 1) >> 1, chunk)
-
-        @pl.when((group >= 1) & (group < NEAR_AT))
+        is_odd = (group & 1) == 1
+        chunk = jnp.where(is_odd, 9 + ((group - 5) >> 1), 4 + ((group - 4) >> 1))
+        chunk = jnp.where(group < 4, jnp.where(group == 1, 8, jnp.maximum(group, 1)), chunk)
+
+        @pl.when(group < NEAR_AT - 1)
         def _():
             for copy in frame_copies(chunk):
                 copy.start()
 
-        @pl.when(group > FAR_AT)
-        def _():
-            y_copy(group - FAR_AT - 1).start()
-
-    def turn(row, _, out, old):
+        @pl.when((group > FAR_AT) & ((group < EXTRA_AT) | (group > MATE_AT)))
+        def _():
+            y_copy(group - FAR_AT - jnp.where(group < EXTRA_AT, 1, 3)).start()
+
+    def turn(_, __, row, out, old):
         y_ref[aligned(out, COLS), aligned(row, ROWS)] = old[...].T
 
     def step(last, now, following, cov, cov_next, old, old_last):
-        row, col, out = now
+        row, col, out_row, out = now
         products = covariance_pieces(all_ref, *following[:2], cov_next)
         pieces = value_pieces(cov, ln_ref, rn_ref, row, col)
         for _, (r, values) in interleave(pieces, products):
-            tile[aligned(row + r, STEP), aligned(out, COLS)] = values
+            tile[aligned(out_row + r, STEP), aligned(out, COLS)] = values
             old[r : r + STEP, :] = encode(values)
         turn(*last, old_last)
 
@@ -266,15 +278,14 @@
 
     last, _ = lax.fori_loop(0, GROUPS, body, (first, first))
     turn(*last, old1)
-    last_copy = GROUPS - FAR_AT - 1
-    y_copy(jnp.int32(last_copy)).start()
+    y_copy(jnp.int32(SENDS - 1)).start()
 
     @pl.loop(0, 3 * CHUNKS)
     def _(k):
         for copy in frame_copies(k):
             copy.wait_send()
 
-    @pl.loop(0, last_copy + 1)
+    @pl.loop(0, SENDS)
     def _(k):
         y_copy(k).wait()
 
@@ -300,7 +311,7 @@
             pltpu.VMEM((ROWS, COLS), jnp.bfloat16),
             pltpu.SemaphoreType.DMA((2, 3 * CHUNKS)),
             pltpu.SemaphoreType.DMA((2, 3 * CHUNKS)),
-            pltpu.SemaphoreType.DMA((2, GROUPS - FAR_AT)),
+            pltpu.SemaphoreType.DMA((2, SENDS)),
         ],
         compiler_params=pltpu.CompilerParams(
             collective_id=0, has_side_effects=True, vmem_limit_bytes=MAIN_LIMIT
@@ -350,15 +361,22 @@
         rows, cols = pl.ds(0, HALF if c == CHUNKS - 1 else (c + 1) * COLS), pl.ds(c * COLS, COLS)
         copy(tile.at[rows, cols], 2, rows, cols)
 
+    extra_rows = aligned(extra_row(parity), ROWS)
+    extra = tile.at[pl.ds(EXTRA_ROW, ROWS), pl.ds(0, HALF)]
+    copy(extra, near_slot, extra_rows, pl.ds(HALF, HALF))
+
     def later(source, slot, rows, cols):
         return copy(source, slot, rows, cols, start=False)
 
     first_rows, second_rows = pl.ds(HALF, COLS), pl.ds(LAST, COLS)
     far_copies = [later(far_tile.at[half(i)], 4 * parity, half(i), both) for i in range(2)]
-    (near_copies, mate_copies) = (
-        [later(tiles.at[:, half(i)], slot, half(other_half(i, 1 - flip)), half(i)) for i in range(2)]
-        for _, slot, flip, tiles in quarters
-    )
+    def quarter_copy(block, i, rows):
+        _, slot, flip, tiles = quarters[block]
+        target = aligned(other_half(i, 1 - flip) * HALF, rows)
+        return later(tiles.at[pl.ds(0, rows), half(i)], slot, target, half(i))
+
+    near_copies = [quarter_copy(0, 0, HALF), quarter_copy(0, 1, HALF - COLS)]
+    mate_copies = [quarter_copy(1, 0, HALF), quarter_copy(1, 1, HALF)]
     completed = [
         [far_copies[0], *near_copies, later(column.at[pl.ds(0, COLS)], 2, first_rows, last)],
         [far_copies[1], *mate_copies, later(column.at[pl.ds(COLS, COLS)], 2, second_rows, last)],

time: 77.1 us -> 79.9 us (1.036); the launches traced: 77 us -> 78.5 us
  Pallas kernels: 75.6 us -> 77.1 us
    pallas_call x1, Pallas kernels: 68.2 us -> 69.7 us  [main(): pl.pallas_call(functools.partial(main_kernel, count), in_specs=[VMEM], ou...]
where the time goes in v8:
time: 79.9 us; the launch traced here: 78.5 us
  Pallas kernels  77.1 us (96%)
  local copies, waits for them, and re-layouts  1.41 us (2%)
    pallas_call x1, Pallas kernels, main(): pl.pallas_call(functools.partial(main_kernel, count), in_specs=[VMEM], ou...  69.7 us
    pallas_call x1, Pallas kernels, finish(): pl.pallas_call(finish_kernel, in_specs=[ANY] + [VMEM] * 5, out_specs=ANY,...  7.35 us

profile of v8, /device:TPU:0, one launch (start us, length us, event | category | flops | bytes accessed | tf_op | source)
XLA Modules:
  0.0 78.5 jit_solution(5798465611693855686)
XLA Ops:
  0.0 0.0 copy-start
  0.0 1.4 %copy-done = bf16[3,1024,256]{2,1,0:T(8,128)(2,1)S(1)} copy-done((bf16[3,1024,256]{2,1,0:T(8,128)(2,1)S(1)}, bf16[3,1024,256]{2,1,0:T(8,128)(2,1)}, u32[]{:S(2)}) %copy-start) | copy-done | bytes 1572888
  1.4 69.7 %deviations.1 = (f32[1024,3072]{1,0:T(8,128)S(1)}, bf16[3072,1024]{1,0:T(8,128)(2,1)S(1)}, bf16[2048,1024]{1,0:T(8,128)(2,1)S(1)}, bf16[3,1024,256]{2,1,0:T(8,12...) custom-call(bf16[3,1024,256]{2,1,0:T(8,128)(2,1)S(1)} %copy-done), custom_call_target="tpu_custom_call" | custom-call | flops 12079595520 | bytes 33554432 | tf_op jit(solution)/shard_map/deviations/pallas_call | solution.py:294
  71.2 7.4 %finish.1 = f32[5,1024,1024]{2,1,0:T(8,128)} custom-call(f32[1024,3072]{1,0:T(8,128)S(1)} %get-tuple-element.11.tile, bf16[3072,1024]{1,0:T(8,128)(2,1)S(1)} %get-tuple-element.12.y_ref, bf16[2048,1024]{1,0:T(8,128)(2,1)S(1)} %get-tuple-element.13.got_ref, bf16[3,1024,256]{2,1,0:T(8,128)(2,1)S(1)} %get-tuple-element.14.own_ref, ...), custom_call_target="tpu_custom_call" | custom-call | tf_op jit(solution)/shard_map/finish/pallas_call | solution.py:431
Async XLA Ops:
  0.0 1.4 %copy-start = (bf16[3,1024,256]{2,1,0:T(8,128)(2,1)S(1)}, bf16[3,1024,256]{2,1,0:T(8,128)(2,1)}, u32[]{:S(2)}) copy-start(bf16[3,1024,256]{2,1,0:T(8,128)(2,1)} %x_ref.1) | copy-start | bytes 4718596

commit v9 on v7

--- a/solution.py
+++ b/solution.py
@@ -205,12 +205,11 @@
         source = y_ref.at[aligned(row, COLS), cols]
         return remote(source, got_ref.at[aligned(row - FAR, COLS), cols], y_sems, k, device)
 
-    centre(x_ref, all_ref, own_ref, ln_ref, rn_ref, 0)
+    for i in range(CHUNKS):
+        centre(x_ref, all_ref, own_ref, ln_ref, rn_ref, i * COLS)
     pl.semaphore_wait(barrier, 4)
     for copy in frame_copies(jnp.int32(0)):
         copy.start()
-    for i in range(1, CHUNKS):
-        centre(x_ref, all_ref, own_ref, ln_ref, rn_ref, i * COLS)
 
     def between(group):
         @pl.when((group >= FAR_AT - 1) & (group < NEAR_AT - 2) & ((group & 1) == 1))
@@ -223,13 +222,11 @@
             for copy in frame_copies(group - NEAR_AT + 8):
                 copy.wait_recv()
 
-        is_far = ((group & 1) == 1) & (group < 7)
-        is_near = ((group & 1) == 0) & (group > 2)
-        chunk = jnp.where(group == 2, 8, 8 + ((group - 5) >> 1))
-        chunk = jnp.where(is_near, 4 + ((group - 4) >> 1), chunk)
-        chunk = jnp.where(is_far, (group + 1) >> 1, chunk)
-
-        @pl.when((group >= 1) & (group < NEAR_AT))
+        is_odd = (group & 1) == 1
+        chunk = jnp.where(is_odd, 9 + ((group - 5) >> 1), 4 + ((group - 4) >> 1))
+        chunk = jnp.where(group < 4, jnp.where(group == 1, 8, jnp.maximum(group, 1)), chunk)
+
+        @pl.when(group < NEAR_AT - 1)
         def _():
             for copy in frame_copies(chunk):
                 copy.start()

time: 77.1 us -> 74.5 us (0.966); the launches traced: 77 us -> 73.1 us
  Pallas kernels: 75.6 us -> 71.7 us
    pallas_call x1, Pallas kernels: 68.2 us -> 64.4 us  [main(): pl.pallas_call(functools.partial(main_kernel, count), in_specs=[VMEM], ou...]
where the time goes in v9:
time: 74.5 us; the launch traced here: 73.1 us
  Pallas kernels  71.7 us (96%)
  local copies, waits for them, and re-layouts  1.41 us (2%)
    pallas_call x1, Pallas kernels, main(): pl.pallas_call(functools.partial(main_kernel, count), in_specs=[VMEM], ou...  64.4 us
    pallas_call x1, Pallas kernels, finish(): pl.pallas_call(finish_kernel, in_specs=[ANY] + [VMEM] * 5, out_specs=ANY,...  7.36 us

profile of v9, /device:TPU:0, one launch (start us, length us, event | category | flops | bytes accessed | tf_op | source)
XLA Modules:
  0.0 73.1 jit_solution(3578250852640696285)
XLA Ops:
  0.0 0.0 copy-start
  0.0 1.4 %copy-done = bf16[3,1024,256]{2,1,0:T(8,128)(2,1)S(1)} copy-done((bf16[3,1024,256]{2,1,0:T(8,128)(2,1)S(1)}, bf16[3,1024,256]{2,1,0:T(8,128)(2,1)}, u32[]{:S(2)}) %copy-start) | copy-done | bytes 1572888
  1.4 64.4 %deviations.1 = (f32[1024,3072]{1,0:T(8,128)S(1)}, bf16[3072,1024]{1,0:T(8,128)(2,1)S(1)}, bf16[2048,1024]{1,0:T(8,128)(2,1)S(1)}, bf16[3,1024,256]{2,1,0:T(8,12...) custom-call(bf16[3,1024,256]{2,1,0:T(8,128)(2,1)S(1)} %copy-done), custom_call_target="tpu_custom_call" | custom-call | flops 12079595520 | bytes 33554432 | tf_op jit(solution)/shard_map/deviations/pallas_call | solution.py:280
  65.8 7.4 %finish.1 = f32[5,1024,1024]{2,1,0:T(8,128)} custom-call(f32[1024,3072]{1,0:T(8,128)S(1)} %get-tuple-element.11.tile, bf16[3072,1024]{1,0:T(8,128)(2,1)S(1)} %get-tuple-element.12.y_ref, bf16[2048,1024]{1,0:T(8,128)(2,1)S(1)} %get-tuple-element.13.got_ref, bf16[3,1024,256]{2,1,0:T(8,128)(2,1)S(1)} %get-tuple-element.14.own_ref, ...), custom_call_target="tpu_custom_call" | custom-call | tf_op jit(solution)/shard_map/finish/pallas_call | solution.py:410
Async XLA Ops:
  0.0 1.4 %copy-start = (bf16[3,1024,256]{2,1,0:T(8,128)(2,1)S(1)}, bf16[3,1024,256]{2,1,0:T(8,128)(2,1)}, u32[]{:S(2)}) copy-start(bf16[3,1024,256]{2,1,0:T(8,128)(2,1)} %x_ref.1) | copy-start | bytes 4718596

commit v10 on v9

--- a/solution.py
+++ b/solution.py
@@ -164,7 +164,7 @@
     mate = me + way
 
     barrier = pltpu.get_barrier_semaphore()
-    for device in (far, far_back, near, mate):
+    for device in (far, mate):
         pl.semaphore_signal(
             barrier, inc=1, device_id=(device,), device_id_type=pl.DeviceIdType.MESH
         )
@@ -207,7 +207,7 @@
 
     for i in range(CHUNKS):
         centre(x_ref, all_ref, own_ref, ln_ref, rn_ref, i * COLS)
-    pl.semaphore_wait(barrier, 4)
+    pl.semaphore_wait(barrier, 2)
     for copy in frame_copies(jnp.int32(0)):
         copy.start()
 

time: 74.5 us -> 74.5 us (level)
  no operation moved by 1% of the time
where the time goes in v10:
time: 74.5 us; the launch traced here: 73.4 us
  Pallas kernels  72 us (97%)
  local copies, waits for them, and re-layouts  1.41 us (2%)
    pallas_call x1, Pallas kernels, main(): pl.pallas_call(functools.partial(main_kernel, count), in_specs=[VMEM], ou...  64.6 us
    pallas_call x1, Pallas kernels, finish(): pl.pallas_call(finish_kernel, in_specs=[ANY] + [VMEM] * 5, out_specs=ANY,...  7.36 us

profile of v10, /device:TPU:0, one launch (start us, length us, event | category | flops | bytes accessed | tf_op | source)
XLA Modules:
  0.0 73.4 jit_solution(12958377059946388401)
XLA Ops:
  0.0 0.0 copy-start
  0.0 1.4 %copy-done = bf16[3,1024,256]{2,1,0:T(8,128)(2,1)S(1)} copy-done((bf16[3,1024,256]{2,1,0:T(8,128)(2,1)S(1)}, bf16[3,1024,256]{2,1,0:T(8,128)(2,1)}, u32[]{:S(2)}) %copy-start) | copy-done | bytes 1572888
  1.4 64.6 %deviations.1 = (f32[1024,3072]{1,0:T(8,128)S(1)}, bf16[3072,1024]{1,0:T(8,128)(2,1)S(1)}, bf16[2048,1024]{1,0:T(8,128)(2,1)S(1)}, bf16[3,1024,256]{2,1,0:T(8,12...) custom-call(bf16[3,1024,256]{2,1,0:T(8,128)(2,1)S(1)} %copy-done), custom_call_target="tpu_custom_call" | custom-call | flops 12079595520 | bytes 33554432 | tf_op jit(solution)/shard_map/deviations/pallas_call | solution.py:280
  66.1 7.4 %finish.1 = f32[5,1024,1024]{2,1,0:T(8,128)} custom-call(f32[1024,3072]{1,0:T(8,128)S(1)} %get-tuple-element.11.tile, bf16[3072,1024]{1,0:T(8,128)(2,1)S(1)} %get-tuple-element.12.y_ref, bf16[2048,1024]{1,0:T(8,128)(2,1)S(1)} %get-tuple-element.13.got_ref, bf16[3,1024,256]{2,1,0:T(8,128)(2,1)S(1)} %get-tuple-element.14.own_ref, ...), custom_call_target="tpu_custom_call" | custom-call | tf_op jit(solution)/shard_map/finish/pallas_call | solution.py:410
Async XLA Ops:
  0.0 1.4 %copy-start = (bf16[3,1024,256]{2,1,0:T(8,128)(2,1)S(1)}, bf16[3,1024,256]{2,1,0:T(8,128)(2,1)}, u32[]{:S(2)}) copy-start(bf16[3,1024,256]{2,1,0:T(8,128)(2,1)} %x_ref.1) | copy-start | bytes 4718596

commit v11 on v10

--- a/solution.py
+++ b/solution.py
@@ -224,7 +224,7 @@
 
         is_odd = (group & 1) == 1
         chunk = jnp.where(is_odd, 9 + ((group - 5) >> 1), 4 + ((group - 4) >> 1))
-        chunk = jnp.where(group < 4, jnp.where(group == 1, 8, jnp.maximum(group, 1)), chunk)
+        chunk = jnp.where(group < 4, jnp.where(group == 0, 8, group), chunk)
 
         @pl.when(group < NEAR_AT - 1)
         def _():

time: 74.5 us -> 74.5 us (level)
  no operation moved by 1% of the time
where the time goes in v11:
time: 74.5 us; the launch traced here: 73.8 us
  Pallas kernels  72.4 us (97%)
  local copies, waits for them, and re-layouts  1.41 us (2%)
    pallas_call x1, Pallas kernels, main(): pl.pallas_call(functools.partial(main_kernel, count), in_specs=[VMEM], ou...  65 us
    pallas_call x1, Pallas kernels, finish(): pl.pallas_call(finish_kernel, in_specs=[ANY] + [VMEM] * 5, out_specs=ANY,...  7.36 us

profile of v11, /device:TPU:0, one launch (start us, length us, event | category | flops | bytes accessed | tf_op | source)
XLA Modules:
  0.0 73.8 jit_solution(18333288200930300952)
XLA Ops:
  0.0 0.0 copy-start
  0.0 1.4 %copy-done = bf16[3,1024,256]{2,1,0:T(8,128)(2,1)S(1)} copy-done((bf16[3,1024,256]{2,1,0:T(8,128)(2,1)S(1)}, bf16[3,1024,256]{2,1,0:T(8,128)(2,1)}, u32[]{:S(2)}) %copy-start) | copy-done | bytes 1572888
  1.4 65.0 %deviations.1 = (f32[1024,3072]{1,0:T(8,128)S(1)}, bf16[3072,1024]{1,0:T(8,128)(2,1)S(1)}, bf16[2048,1024]{1,0:T(8,128)(2,1)S(1)}, bf16[3,1024,256]{2,1,0:T(8,12...) custom-call(bf16[3,1024,256]{2,1,0:T(8,128)(2,1)S(1)} %copy-done), custom_call_target="tpu_custom_call" | custom-call | flops 12079595520 | bytes 33554432 | tf_op jit(solution)/shard_map/deviations/pallas_call | solution.py:280
  66.4 7.4 %finish.1 = f32[5,1024,1024]{2,1,0:T(8,128)} custom-call(f32[1024,3072]{1,0:T(8,128)S(1)} %get-tuple-element.11.tile, bf16[3072,1024]{1,0:T(8,128)(2,1)S(1)} %get-tuple-element.12.y_ref, bf16[2048,1024]{1,0:T(8,128)(2,1)S(1)} %get-tuple-element.13.got_ref, bf16[3,1024,256]{2,1,0:T(8,128)(2,1)S(1)} %get-tuple-element.14.own_ref, ...), custom_call_target="tpu_custom_call" | custom-call | tf_op jit(solution)/shard_map/finish/pallas_call | solution.py:410
Async XLA Ops:
  0.0 1.4 %copy-start = (bf16[3,1024,256]{2,1,0:T(8,128)(2,1)S(1)}, bf16[3,1024,256]{2,1,0:T(8,128)(2,1)}, u32[]{:S(2)}) copy-start(bf16[3,1024,256]{2,1,0:T(8,128)(2,1)} %x_ref.1) | copy-start | bytes 4718596
